TPU v7x, 32 devices: a whole 2x2x4 slice. The times are simulated.
32 devices in a mesh: section: 2 (over x), dp: 8 (over z, y), tensor: 2 (over core).
Axes of the slice: x: 2, y: 2, z: 4, core: 2. Of those that a mesh axis runs over, the one named last changes fastest.
Arguments:
- tokens: bfloat16 [2, 8, 128, 768], P(None, 'dp'), may hold values from -6 to 6
- cotangent: bfloat16 [2, 8, 128, 768], P(None, 'dp'), may hold values from -6 to 6
- segments: int32 [2, 8, 128], P(None, 'dp'), may hold values from 0 to 7, never falling along the last dimension, each value on 1 to 96 neighbouring positions
- pad_mask: int32 [2, 8, 128], P(None, 'dp'), may hold values 0 or 1
- routes: int32 [2, 8, 128, 2], P(None, 'dp'), may hold values from 0 to 7, all different within a row; in each aligned block of 128 rows (0 to 127, 128 to 255, ..., all dimensions but the last counted through in order) at most 48 rows name the same one
- dist_bucket: int32 [128], replicated, may hold values from 0 to 31, as said below
- norm_gains: bfloat16 [2, 2, 768], P('section'), may hold values from 0.5 to 1.5
- qkv_weight: bfloat16 [2, 768, 3, 768], P('section', None, None, 'tensor'), may hold values from -0.21875 to 0.21875
- out_weight: bfloat16 [2, 768, 768], P('section', 'tensor'), may hold values from -0.875 to 0.875
- rel_bias: bfloat16 [2, 32, 12], P('section', None, 'tensor'), may hold values from -4 to 4
- router_weight: bfloat16 [2, 768, 8], P('section'), may hold values from -0.15625 to 0.15625
- expert_up: bfloat16 [2, 8, 768, 3072], P('section', 'dp', None, 'tensor'), may hold values from -0.21875 to 0.21875
- expert_down: bfloat16 [2, 8, 3072, 768], P('section', 'dp', 'tensor'), may hold values from -0.21875 to 0.21875
Outputs:
- section_outputs: float32 [2, 2, 8, 128, 768], P('section', None, 'dp', None, 'tensor')
- input_grads: float32 [2, 2, 8, 128, 768], P('section', None, 'dp', None, 'tensor')
- grad_gains: float32 [2, 2, 768], P('section')
- grad_qkv: float32 [2, 768, 3, 768], P('section', None, None, 'tensor')
- grad_out: float32 [2, 768, 768], P('section', 'tensor')
- grad_bias: float32 [2, 32, 12], P('section', None, 'tensor')
- grad_router: float32 [2, 768, 8], P('section')
- grad_up: float32 [2, 8, 768, 3072], P('section', 'dp', None, 'tensor')
- grad_down: float32 [2, 8, 3072, 768], P('section', 'dp', 'tensor')
Inputs may be any that keep to these rules, and one draw needn't show every extreme that they name: `routes`: in each aligned block of 128 rows (one sequence) no expert is named by more than 48 route entries, a bound that some block reaches; a token's two experts differ. `dist_bucket`: never falls as the distance grows; 0 at distance 0.
All inputs are finite; a program needn't handle non-finite values. No bound on the sum of `pad_mask` on one device may be relied on, other than what follows from the above.
Results may differ from a plain program's by a relative error of at most 0.02.
Values may be sent and summed in bfloat16 or wider, within the bound.
A program may use at most 192 MiB of HBM per device.

v0:
```python
from functools import partial

import jax
import jax.numpy as jnp
from jax import lax
from jax.sharding import PartitionSpec as P

norm_eps = 1e-06
masked_score = -1e30
highest = lax.Precision.HIGHEST


def shifted(block, axis, distance):
    devices = range(lax.axis_size(axis))
    route = [(i - distance, i) for i in devices if i - distance in devices]
    return lax.ppermute(block, axis, route)


def normalize(values, gain_row):
    scale_inv = lax.rsqrt(jnp.mean(values * values, axis=-1, keepdims=True) + norm_eps)
    return values * scale_inv * gain_row


def normalize_back(values, gain_row, upstream):
    scale_inv = lax.rsqrt(jnp.mean(values * values, axis=-1, keepdims=True) + norm_eps)
    normed = values * scale_inv
    gain_grad = jnp.sum(upstream * normed, axis=0)
    scaled = upstream * gain_row
    input_grad = scale_inv * (scaled - normed * jnp.mean(scaled * normed, axis=-1, keepdims=True))
    return (input_grad, gain_grad)


def send_rows(rows):
    return lax.all_to_all(rows, "dp", split_axis=0, concat_axis=0, tiled=True)


def sum_slots(partial_rows):
    return lax.psum(partial_rows, "tensor")


def score_context(segment_row, pad_row, dist_bucket, bucket_count):
    length = segment_row.shape[0]
    places = jnp.arange(length, dtype=jnp.int32)
    offsets = jnp.clip(places[:, None] - places[None, :], 0, length - 1)
    bucket_grid = jnp.take(dist_bucket, offsets)
    bucket_onehot = (
        bucket_grid[:, :, None] == jnp.arange(bucket_count, dtype=jnp.int32)[None, None, :]
    ).astype(jnp.float32)
    allowed = (places[None, :] <= places[:, None]) & (segment_row[:, None] == segment_row[None, :])
    allowed = allowed & ((pad_row[None, :] == 1) | (places[None, :] == places[:, None]))
    return (bucket_onehot, allowed)


def attention_front(inputs, context, weights):
    segment_row, pad_row, route_rows, dist_bucket = context
    gain_pair, qkv_weight, out_weight, bias_table, router_weight, upper_weight, lower_weight = (
        weights
    )
    length = inputs.shape[0]
    head_count = bias_table.shape[1]
    bucket_onehot, allowed = score_context(segment_row, pad_row, dist_bucket, bias_table.shape[0])
    normed_one = normalize(inputs, gain_pair[0]).astype(jnp.bfloat16)
    qkv_rows = jnp.einsum(
        "ld,dch->lch", normed_one, qkv_weight, preferred_element_type=jnp.float32
    ).astype(jnp.bfloat16)
    head_dim = qkv_rows.shape[2] // head_count
    queries = qkv_rows[:, 0].reshape(length, head_count, head_dim)
    keys_in = qkv_rows[:, 1].reshape(length, head_count, head_dim)
    values_in = qkv_rows[:, 2].reshape(length, head_count, head_dim)
    raw_scores = jnp.einsum("qhd,khd->hqk", queries, keys_in, preferred_element_type=jnp.float32)
    bias_grid = jnp.einsum(
        "qkb,bh->hqk", bucket_onehot, bias_table.astype(jnp.float32), precision=highest
    )
    logits = jnp.where(allowed[None], 0.125 * raw_scores + bias_grid, masked_score)
    exp_terms = jnp.exp(logits - jnp.max(logits, axis=-1, keepdims=True))
    attn_probs = exp_terms / jnp.sum(exp_terms, axis=-1, keepdims=True)
    mixed_rows = jnp.einsum(
        "hqk,khd->qhd",
        attn_probs.astype(jnp.bfloat16),
        values_in,
        preferred_element_type=jnp.float32,
    )
    mixed_rows = mixed_rows.reshape(length, -1).astype(jnp.bfloat16)
    return (normed_one, queries, keys_in, values_in, attn_probs, mixed_rows, bucket_onehot)


def slot_tables(route_rows, experts, capacity):
    flat_routes = route_rows.reshape(-1)
    route_hits = (flat_routes[:, None] == jnp.arange(experts, dtype=jnp.int32)[None, :]).astype(
        jnp.int32
    )
    earlier = jnp.cumsum(route_hits, axis=0) - route_hits
    position = jnp.sum(earlier * route_hits, axis=1)
    target = flat_routes * capacity + position
    slot_hits = (
        jnp.arange(experts * capacity, dtype=jnp.int32)[:, None] == target[None, :]
    ).astype(jnp.int32)
    source = jnp.sum(slot_hits * jnp.arange(target.shape[0], dtype=jnp.int32)[None, :], axis=1)
    filled = jnp.sum(slot_hits, axis=1) > 0
    return (target, source, filled, route_hits)


def route_gates(normed_two, router_weight, route_hits):
    length = normed_two.shape[0]
    logits = jnp.dot(normed_two, router_weight, preferred_element_type=jnp.float32)
    route_onehot = route_hits.reshape(length, 2, -1).astype(jnp.float32)
    chosen = jnp.einsum("le,lre->lr", logits, route_onehot, precision=highest)
    return (jax.nn.softmax(chosen, axis=-1), route_onehot)


def gather_back(back_slots, target, length):
    flat_slots = back_slots.reshape(-1, back_slots.shape[-1])
    return jnp.take(flat_slots, target, axis=0).reshape(length, 2, -1)


def forward_rest(inputs, front, context, weights):
    segment_row, pad_row, route_rows, dist_bucket = context
    gain_pair, qkv_weight, out_weight, bias_table, router_weight, upper_weight, lower_weight = (
        weights
    )
    mixed_rows = front[5]
    length, model_width = inputs.shape
    experts = router_weight.shape[1]
    capacity = max(2, 3 * length // experts)
    local_experts = upper_weight.shape[0]
    attn_out = lax.psum(
        jnp.dot(mixed_rows, out_weight, preferred_element_type=jnp.float32), "tensor"
    )
    middle = inputs + attn_out
    normed_two = normalize(middle, gain_pair[1]).astype(jnp.bfloat16)
    target, source, filled, route_hits = slot_tables(route_rows, experts, capacity)
    outgoing = jnp.where(
        filled[:, None], jnp.take(normed_two, source // 2, axis=0), jnp.zeros((), jnp.bfloat16)
    )
    outgoing = outgoing.reshape(experts, capacity, model_width)
    arrived = send_rows(outgoing)
    grouped = arrived.reshape(-1, local_experts, capacity, model_width)
    pre_act = jnp.einsum(
        "secd,edf->secf", grouped, upper_weight, preferred_element_type=jnp.float32
    )
    hidden = jax.nn.gelu(pre_act, approximate=False).astype(jnp.bfloat16)
    partial_out = jnp.einsum(
        "secf,efd->secd", hidden, lower_weight, preferred_element_type=jnp.float32
    )
    summed = sum_slots(partial_out)
    returned = summed.astype(jnp.bfloat16).reshape(arrived.shape[0], arrived.shape[1], -1)
    back_slots = send_rows(returned)
    gate_probs, route_onehot = route_gates(normed_two, router_weight, route_hits)
    back_rows = gather_back(back_slots, target, length)
    output = middle + jnp.sum(gate_probs[:, :, None] * back_rows.astype(jnp.float32), axis=1)
    return (output, (attn_out, arrived, back_slots, pre_act))


def backward_layer(inputs, upstream, context, weights, front, saved_state):
    segment_row, pad_row, route_rows, dist_bucket = context
    gain_pair, qkv_weight, out_weight, bias_table, router_weight, upper_weight, lower_weight = (
        weights
    )
    normed_one, queries, keys_in, values_in, attn_probs, mixed_rows, bucket_onehot = front
    attn_out, arrived_rows, back_slots, pre_rows = saved_state
    length, model_width = inputs.shape
    head_count = bias_table.shape[1]
    head_cols = qkv_weight.shape[2]
    experts = router_weight.shape[1]
    capacity = max(2, 3 * length // experts)
    local_experts = upper_weight.shape[0]
    middle = inputs + attn_out
    normed_two = normalize(middle, gain_pair[1]).astype(jnp.bfloat16)
    target, source, filled, route_hits = slot_tables(route_rows, experts, capacity)
    gate_probs, route_onehot = route_gates(normed_two, router_weight, route_hits)
    back_rows = gather_back(back_slots, target, length)
    gate_grad = jnp.sum(upstream[:, None, :] * back_rows.astype(jnp.float32), axis=-1)
    chosen_grad = gate_probs * (gate_grad - jnp.sum(gate_probs * gate_grad, axis=-1, keepdims=True))
    logit_grad = jnp.einsum("lr,lre->le", chosen_grad, route_onehot, precision=highest).astype(
        jnp.bfloat16
    )
    router_grad = jnp.dot(normed_two.T, logit_grad, preferred_element_type=jnp.float32)
    normed_two_grad = jnp.dot(logit_grad, router_weight.T, preferred_element_type=jnp.float32)
    route_grads = (
        (gate_probs[:, :, None] * upstream[:, None, :])
        .reshape(2 * length, model_width)
        .astype(jnp.bfloat16)
    )
    slot_grads = jnp.where(
        filled[:, None], jnp.take(route_grads, source, axis=0), jnp.zeros((), jnp.bfloat16)
    )
    arrived_grads = send_rows(slot_grads.reshape(experts, capacity, model_width))
    grouped = arrived_rows.reshape(-1, local_experts, capacity, model_width)
    grouped_grads = arrived_grads.reshape(-1, local_experts, capacity, model_width)
    hidden, gelu_pull = jax.vjp(partial(jax.nn.gelu, approximate=False), pre_rows)
    hidden_low = hidden.astype(jnp.bfloat16)
    down_grad = jnp.einsum(
        "secf,secd->efd", hidden_low, grouped_grads, preferred_element_type=jnp.float32
    )
    hidden_grad = jnp.einsum(
        "secd,efd->secf", grouped_grads, lower_weight, preferred_element_type=jnp.float32
    )
    pre_grad = gelu_pull(hidden_grad)[0].astype(jnp.bfloat16)
    up_grad = jnp.einsum("secd,secf->edf", grouped, pre_grad, preferred_element_type=jnp.float32)
    rows_grad = sum_slots(
        jnp.einsum("secf,edf->secd", pre_grad, upper_weight, preferred_element_type=jnp.float32)
    )
    sent_back = send_rows(
        rows_grad.astype(jnp.bfloat16).reshape(arrived_rows.shape[0], arrived_rows.shape[1], -1)
    )
    copy_grads = gather_back(sent_back, target, length).astype(jnp.float32)
    normed_two_grad = normed_two_grad + jnp.sum(copy_grads, axis=1)
    middle_part, gain_two = normalize_back(middle, gain_pair[1], normed_two_grad)
    middle_grad = upstream + middle_part
    attn_grad = middle_grad.astype(jnp.bfloat16)
    out_grad = jnp.dot(mixed_rows.T, attn_grad, preferred_element_type=jnp.float32)
    mixed_grad = jnp.dot(attn_grad, out_weight.T, preferred_element_type=jnp.float32).astype(
        jnp.bfloat16
    )
    mixed_grad = mixed_grad.reshape(length, head_count, -1)
    prob_grad = jnp.einsum(
        "qhd,khd->hqk", mixed_grad, values_in, preferred_element_type=jnp.float32
    )
    value_grad = jnp.einsum(
        "hqk,qhd->khd",
        attn_probs.astype(jnp.bfloat16),
        mixed_grad,
        preferred_element_type=jnp.float32,
    )
    score_grad = attn_probs * (prob_grad - jnp.sum(prob_grad * attn_probs, axis=-1, keepdims=True))
    table_grad = jnp.einsum("hqk,qkb->bh", score_grad, bucket_onehot, precision=highest)
    raw_grad = (0.125 * score_grad).astype(jnp.bfloat16)
    query_grad = jnp.einsum("hqk,khd->qhd", raw_grad, keys_in, preferred_element_type=jnp.float32)
    key_grad = jnp.einsum("hqk,qhd->khd", raw_grad, queries, preferred_element_type=jnp.float32)
    qkv_grad = (
        jnp.stack([query_grad, key_grad, value_grad], axis=1)
        .reshape(length, 3, head_cols)
        .astype(jnp.bfloat16)
    )
    qkv_weight_grad = jnp.einsum(
        "ld,lch->dch", normed_one, qkv_grad, preferred_element_type=jnp.float32
    )
    normed_one_grad = lax.psum(
        jnp.einsum("lch,dch->ld", qkv_grad, qkv_weight, preferred_element_type=jnp.float32),
        "tensor",
    )
    input_part, gain_one = normalize_back(inputs, gain_pair[0], normed_one_grad)
    input_grad = middle_grad + input_part
    gain_grads = jnp.stack([gain_one, gain_two])
    return (
        input_grad,
        (gain_grads, qkv_weight_grad, out_grad, table_grad, router_grad, up_grad, down_grad),
    )


def pick_context(segments, pad_mask, routes, dist_bucket, micro_slot):
    segment_row = lax.dynamic_index_in_dim(segments[:, 0], micro_slot, 0, False)
    pad_row = lax.dynamic_index_in_dim(pad_mask[:, 0], micro_slot, 0, False)
    route_rows = lax.dynamic_index_in_dim(routes[:, 0], micro_slot, 0, False)
    return (segment_row, pad_row, route_rows, dist_bucket)


def place_row(store_all, new_value, micro_slot, is_valid):
    current = lax.dynamic_index_in_dim(store_all, micro_slot, 0, False)
    return lax.dynamic_update_index_in_dim(
        store_all, jnp.where(is_valid, new_value, current), micro_slot, 0
    )


def pick_row(store_all, micro_slot):
    return lax.dynamic_index_in_dim(store_all, micro_slot, 0, False)


def mask_grad(grad_value, is_valid):
    return jnp.where(is_valid, grad_value, jnp.zeros((), grad_value.dtype))


def tensor_half(full_rows, tensor_id, half_width):
    return lax.dynamic_slice_in_dim(full_rows, tensor_id * half_width, half_width, 2)[None, :, None]


def local(
    tokens,
    cotangent,
    segments,
    pad_mask,
    routes,
    dist_bucket,
    norm_gains,
    qkv_weight,
    out_weight,
    rel_bias,
    router_weight,
    expert_up,
    expert_down,
):
    section_id = lax.axis_index("section")
    section_count = lax.axis_size("section")
    micro_count = tokens.shape[0]
    length = tokens.shape[2]
    model_width = tokens.shape[3]
    tick_count = micro_count + section_count - 1
    weights = (
        norm_gains[0].astype(jnp.float32),
        qkv_weight[0],
        out_weight[0],
        rel_bias[0],
        router_weight[0],
        expert_up[0],
        expert_down[0],
    )
    empty_rows = jnp.zeros((length, model_width), jnp.bfloat16)
    arriving = empty_rows
    kept_inputs = jnp.zeros((micro_count, length, model_width), jnp.bfloat16)
    section_out = jnp.zeros((micro_count, length, model_width), jnp.float32)
    for tick_index in range(tick_count):
        micro_index = tick_index - section_id
        is_valid = (micro_index >= 0) & (micro_index < micro_count)
        micro_slot = jnp.clip(micro_index, 0, micro_count - 1)
        own_rows = tokens[tick_index, 0] if tick_index < micro_count else empty_rows
        layer_in = jnp.where(section_id == 0, own_rows, arriving)
        context = pick_context(segments, pad_mask, routes, dist_bucket, micro_slot)
        inputs = layer_in.astype(jnp.float32)
        front = attention_front(inputs, context, weights)
        result, saved_state = forward_rest(inputs, front, context, weights)
        section_out = place_row(section_out, result, micro_slot, is_valid)
        kept_inputs = place_row(kept_inputs, layer_in, micro_slot, is_valid)
        arriving = shifted(result.astype(jnp.bfloat16), "section", 1)
    returning = empty_rows
    input_store = jnp.zeros((micro_count, length, model_width), jnp.float32)
    totals = None
    for tick_index in range(tick_count):
        micro_index = tick_index - (section_count - 1 - section_id)
        is_valid = (micro_index >= 0) & (micro_index < micro_count)
        micro_slot = jnp.clip(micro_index, 0, micro_count - 1)
        own_rows = cotangent[tick_index, 0] if tick_index < micro_count else empty_rows
        upstream = jnp.where(section_id == section_count - 1, own_rows, returning).astype(
            jnp.float32
        )
        inputs = pick_row(kept_inputs, micro_slot).astype(jnp.float32)
        context = pick_context(segments, pad_mask, routes, dist_bucket, micro_slot)
        front = attention_front(inputs, context, weights)
        saved_state = forward_rest(inputs, front, context, weights)[1]
        input_grad, grad_set = backward_layer(
            inputs, upstream, context, weights, front, saved_state
        )
        input_store = place_row(input_store, input_grad, micro_slot, is_valid)
        grad_set = jax.tree.map(partial(mask_grad, is_valid=is_valid), grad_set)
        totals = grad_set if totals is None else jax.tree.map(jnp.add, totals, grad_set)
        returning = shifted(input_grad.astype(jnp.bfloat16), "section", -1)
    shared = lax.psum((totals[0], totals[1], totals[2], totals[3], totals[4]), "dp")
    tensor_id = lax.axis_index("tensor")
    half_width = model_width // lax.axis_size("tensor")
    return (
        tensor_half(section_out, tensor_id, half_width),
        tensor_half(input_store, tensor_id, half_width),
        shared[0][None],
        shared[1][None],
        shared[2][None],
        shared[3][None],
        shared[4][None],
        totals[5][None],
        totals[6][None],
    )


def solution(mesh):
    in_specs = (
        P(None, "dp", None, None),
        P(None, "dp", None, None),
        P(None, "dp", None),
        P(None, "dp", None),
        P(None, "dp", None, None),
        P(),
        P("section", None, None),
        P("section", None, None, "tensor"),
        P("section", "tensor", None),
        P("section", None, "tensor"),
        P("section", None, None),
        P("section", "dp", None, "tensor"),
        P("section", "dp", "tensor", None),
    )
    out_specs = (
        P("section", None, "dp", None, "tensor"),
        P("section", None, "dp", None, "tensor"),
        P("section", None, None),
        P("section", None, None, "tensor"),
        P("section", "tensor", None),
        P("section", None, "tensor"),
        P("section", None, None),
        P("section", "dp", None, "tensor"),
        P("section", "dp", "tensor", None),
    )
    return jax.shard_map(local, mesh=mesh, in_specs=in_specs, out_specs=out_specs, check_vma=False)
```

profile of v0, /device:TPU:0, one launch (start us, length us, event | category | flops | bytes accessed | tf_op | source)
XLA Modules:
  0.0 1198.0 jit_solution(9064854762967102376)
XLA Ops:
  12.1 97.2 %gather_fusion = s32[16384]{0:T(1024)S(1)} fusion(s32[128]{0:T(128)S(1)} %copy-done.1, s32[16384]{0:T(1024)S(1)} %bitcast_clamp_fusion), kind=kCustom, calls=%fused_computation.clone | custom fusion | bytes 196608 | tf_op jit(solution)/shard_map/jit(_take)/gather | solution.py:45
  133.4 6.9 all-reduce.21.cloned.1.call-done
  147.6 6.0 all-to-all-start
  158.6 11.4 all-to-all-done
  170.0 9.5 fusion.201
  179.5 7.6 all-reduce.38
  187.1 4.2 all-to-all-start.1
  194.9 13.2 %all-to-all-done.1 = bf16[8,48,768]{2,1,0:T(8,128)(2,1)} async-done(((bf16[8,48,768]{2,1,0:T(8,128)(2,1)}), bf16[8,48,768]{2,1,0:T(8,128)(2,1)}, u32[]{:S(2)}, u32[]{:S(2)}) %all-to-all-start.1) | async-done | bytes 589856 | tf_op jit(solution)/shard_map/all_to_all | solution.py:34
  242.5 16.8 %all-reduce.23.cloned.1.call-done = f32[128,768]{1,0:T(8,128)} async-done(((f32[128,768]{1,0:T(8,128)}), f32[128,768]{1,0:T(8,128)}) %all-reduce.23.cloned.1.call-update) | async-done | bytes 393232 | tf_op jit(solution)/shard_map/psum | solution.py:126
  266.4 5.8 all-to-all-start.2
  276.4 12.2 %all-to-all-done.2 = bf16[8,48,768]{2,1,0:T(8,128)(2,1)} async-done(((bf16[8,48,768]{2,1,0:T(8,128)(2,1)}), bf16[8,48,768]{2,1,0:T(8,128)(2,1)}, u32[]{:S(2)}, u32[]{:S(2)}) %all-to-all-start.2) | async-done | bytes 589856 | tf_op jit(solution)/shard_map/all_to_all | solution.py:34
  288.6 9.5 fusion.204
  298.1 7.6 all-reduce.39
  305.7 4.2 all-to-all-start.3
  317.7 9.0 all-to-all-done.3
  368.7 10.4 all-reduce.25.cloned.1.call-done
  399.8 5.8 all-to-all-start.6
  416.1 5.9 all-to-all-done.6
  422.0 4.4 all-to-all-start.8
  430.5 7.0 fusion.210
  437.5 4.5 all-to-all-done.8
  442.0 8.0 fusion.110
  453.2 10.5 all-reduce.40
  472.5 11.3 all-to-all-done.7
  483.9 4.2 all-to-all-start.9
  542.9 15.2 %all-reduce.27.cloned.1.call-done = f32[128,768]{1,0:T(8,128)} async-done(((f32[128,768]{1,0:T(8,128)}), f32[128,768]{1,0:T(8,128)}) %all-reduce.27.cloned.1.call-update) | async-done | bytes 393232 | tf_op jit(solution)/shard_map/psum | solution.py:238
  577.9 17.1 %all-reduce.29.cloned.1.call-done = f32[128,768]{1,0:T(8,128)} async-done(((f32[128,768]{1,0:T(8,128)}), f32[128,768]{1,0:T(8,128)}) %all-reduce.29.cloned.1.call-update) | async-done | bytes 393232 | tf_op jit(solution)/shard_map/psum | solution.py:126
  604.6 4.0 collective-permute-done.2
  618.6 5.9 all-to-all-start.10
  634.1 6.1 all-to-all-done.10
  640.2 4.2 all-to-all-start.12
  648.7 7.0 fusion.213
  655.7 4.2 all-to-all-done.12
  659.9 8.0 fusion.98
  671.1 10.5 all-reduce.41
  681.7 4.2 all-to-all-start.11
  685.9 9.1 fusion.678
  695.0 7.7 all-to-all-done.11
  702.7 4.2 all-to-all-start.13
  707.1 5.1 fusion.698
  765.9 10.1 all-reduce.31.cloned.1.call-done
  791.0 9.1 fusion.675
  800.1 4.7 fusion.699
  805.5 6.1 all-reduce.37.cloned.1.call-done
  822.8 6.2 all-to-all-start.4
  845.4 4.2 all-to-all-start.14
  849.6 9.5 fusion.207
  859.1 6.2 all-to-all-done.14
  865.3 4.4 all-to-all-start.16
  874.0 7.0 fusion.216
  881.0 4.3 all-to-all-done.16
  885.3 8.0 fusion.86
  896.5 13.5 %all-reduce.42 = (bf16[8,1,48,768]{3,2,0,1:T(8,128)(2,1)}, bf16[8,1,48,768]{3,2,0,1:T(8,128)(2,1)}, bf16[8,1,48,768]{3,2,0,1:T(8,128)(2,1)}) all-reduce(f32[8,1,48,768]{3,2,0,1:T(8,128)} %fusion.207, f32[8,1,48,768]{3,2,0,1:T(8,128)} %fusion.198, ...), channel_id=1, replica_groups=mesh['section'=2,'dp'=8,'tensor'=2] {'tensor'}, use_global_device_ids=true, to_apply=%region_40.44 | all-reduce | flops 884736 | bytes 5308416 | tf_op jit(solution)/shard_map/psum | solution.py:38
  910.0 4.3 all-to-all-start.17
  923.3 7.9 all-to-all-done.17
  931.2 4.2 all-to-all-start.15
  946.3 5.2 all-to-all-done.15
  951.5 4.3 all-to-all-start.5
  991.4 4.6 add_bitcast_fusion
  996.1 11.4 fusion.7
  1007.5 7.8 fusion.10
  1032.8 41.6 %all-reduce = (f32[1,2,768]{2,1,0:T(2,128)}, f32[1,32,6]{1,2,0:T(8,128)S(1)}, f32[1,768,8]{1,2,0:T(8,128)}) all-reduce(f32[1,2,768]{2,1,0:T(2,128)S(1)} %fusion.546, f32[1,32,6]{1,2,0:T(8,128)S(1)} %fusion.282, f32[1,768,8]{1,2,0:T(8,128)S(1)} %fusion.275), channel_id=1, replica_groups=mesh['section'=2,'dp'=8,'tensor'=2] {'dp'}, use_global_device_ids=true, to_apply=%region_111.116 | all-reduce | flops 7872 | bytes 62976 | tf_op jit(solution)/shard_map/psum | solution.py:346
  1078.9 107.3 %all-reduce.35.cloned.1.call-done = (f32[1,768,3,384]{3,1,2,0:T(8,128)}, f32[1,384,768]{2,1,0:T(8,128)}) async-done(((f32[1,768,3,384]{3,1,2,0:T(8,128)}, f32[1,384,768]{2,1,0:T(8,128)}), (f32[1,768,3,384]{3,1,2,0:T(8,128)}, f32[1,384,768]{2,1,0:T(8,128)})) %all-reduce.35.cloned.1.call-update) | async-done | bytes 4718608 | tf_op jit(solution)/shard_map/psum | solution.py:346
  1186.1 4.1 copy.329
  (821 shorter events, 479.8 us)
Async XLA Ops:
  7.2 162.8 %copy-start = (bf16[1,1,1536,768]{3,2,1,0:T(8,128)(2,1)S(1)}, bf16[1,1,1536,768]{3,2,1,0:T(8,128)(2,1)}, u32[]{:S(2)}) copy-start(bf16[1,1,1536,768]{3,2,1,0:T(8,128)(2,1)} %param.33) | copy-start | bytes 7077892
  7.2 133.1 %all-reduce.21.cloned.1.call-start = ((), (), s32[]{:S(2)}) async-start(), calls=%async_computation.18 | async-start | bytes 786432 | tf_op jit(solution)/shard_map/psum | solution.py:126
  12.1 129.4 %copy-start.77 = (f32[768]{0:T(1024)}, f32[768]{0:T(1024)S(1)}, u32[]{:S(2)}) copy-start(f32[768]{0:T(1024)S(1)} %get-tuple-element.55) | copy-start | bytes 9220
  12.1 98.0 %copy-start.34 = (bf16[2,1,128,768]{3,2,1,0:T(8,128)(2,1)S(1)}, bf16[2,1,128,768]{3,2,1,0:T(8,128)(2,1)}, u32[]{:S(2)}) copy-start(bf16[2,1,128,768]{3,2,1,0:T(8,128)(2,1)} %param.21) | copy-start | bytes 1179652
  116.5 23.8 %copy-start.35 = (bf16[2,1,128,768]{3,2,1,0:T(8,128)(2,1)S(1)}, bf16[2,1,128,768]{3,2,1,0:T(8,128)(2,1)}, u32[]{:S(2)}) copy-start(bf16[2,1,128,768]{3,2,1,0:T(8,128)(2,1)} %param.21) | copy-start | bytes 1179652
  119.1 22.4 %copy-start.134 = (s32[1,1,128,2]{2,3,1,0:T(2,128)}, s32[1,1,128,2]{2,3,1,0:T(2,128)S(1)}, u32[]{:S(2)}) copy-start(s32[1,1,128,2]{2,3,1,0:T(2,128)S(1)} %get-tuple-element.142) | copy-start | bytes 3076
  119.1 22.4 %copy-start.135 = (s32[1,1,128,2]{2,3,1,0:T(2,128)}, s32[1,1,128,2]{2,3,1,0:T(2,128)S(1)}, u32[]{:S(2)}) copy-start(s32[1,1,128,2]{2,3,1,0:T(2,128)S(1)} %get-tuple-element.138) | copy-start | bytes 3076
  127.8 13.7 %copy-start.85 = (s32[1,1,128,2]{3,2,1,0:T(8,128)}, s32[1,1,128,2]{3,2,1,0:T(8,128)S(1)}, u32[]{:S(2)}) copy-start(s32[1,1,128,2]{3,2,1,0:T(8,128)S(1)} %copy.176) | copy-start | bytes 3076
  129.4 12.0 %copy-start.82 = (s32[1,1,128,2]{3,2,1,0:T(8,128)}, s32[1,1,128,2]{3,2,1,0:T(8,128)S(1)}, u32[]{:S(2)}) copy-start(s32[1,1,128,2]{3,2,1,0:T(8,128)S(1)} %copy.204) | copy-start | bytes 3076
  147.6 22.4 %all-to-all-start = ((bf16[8,48,768]{2,1,0:T(8,128)(2,1)}), bf16[8,48,768]{2,1,0:T(8,128)(2,1)}, u32[]{:S(2)}, u32[]{:S(2)}) async-start(bf16[8,48,768]{2,1,0:T(8,128)(2,1)} %bitcast.1384), calls=%async_computation | async-start | bytes 1179648 | tf_op jit(solution)/shard_map/all_to_all | solution.py:34
  154.4 25.1 %copy-start.139 = (s32[256]{0:T(256)}, s32[256]{0:T(256)S(1)}, u32[]{:S(2)}) copy-start(s32[256]{0:T(256)S(1)} %reshape.1433) | copy-start | bytes 3076
  157.8 21.7 %copy-start.142 = (s32[256]{0:T(256)}, s32[256]{0:T(256)S(1)}, u32[]{:S(2)}) copy-start(s32[256]{0:T(256)S(1)} %get-tuple-element.107) | copy-start | bytes 3076
  179.5 12.9 %copy-start.61 = (bf16[1,768,8]{1,2,0:T(8,128)(2,1)S(1)}, bf16[1,768,8]{1,2,0:T(8,128)(2,1)}, u32[]{:S(2)}) copy-start(bf16[1,768,8]{1,2,0:T(8,128)(2,1)} %param.31) | copy-start | bytes 36868
  187.1 20.9 %all-to-all-start.1 = ((bf16[8,48,768]{2,1,0:T(8,128)(2,1)}), bf16[8,48,768]{2,1,0:T(8,128)(2,1)}, u32[]{:S(2)}, u32[]{:S(2)}) async-start(bf16[8,48,768]{2,1,0:T(8,128)(2,1)} %bitcast.1383), calls=%async_computation.1 | async-start | bytes 1179648 | tf_op jit(solution)/shard_map/all_to_all | solution.py:34
  191.3 67.9 %all-reduce.23.cloned.1.call-start = ((), (), s32[]{:S(2)}) async-start(), calls=%async_computation.19 | async-start | bytes 786432 | tf_op jit(solution)/shard_map/psum | solution.py:126
  192.6 18.9 %copy-start.177 = (pred[256]{0:T(512)(128)(4,1)S(1)}, pred[256]{0:T(512)(128)(4,1)}, u32[]{:S(2)}) copy-start(pred[256]{0:T(512)(128)(4,1)} %get-tuple-element.110) | copy-start | bytes 772
  219.5 7.2 collective-permute-start
  226.9 32.4 %copy-start.21 = (bf16[128,768]{1,0:T(8,128)(2,1)}, bf16[128,768]{1,0:T(8,128)(2,1)S(1)}, u32[]{:S(2)}) copy-start(bf16[128,768]{1,0:T(8,128)(2,1)S(1)} %get-tuple-element.105) | copy-start | bytes 589828
  266.4 22.2 %all-to-all-start.2 = ((bf16[8,48,768]{2,1,0:T(8,128)(2,1)}), bf16[8,48,768]{2,1,0:T(8,128)(2,1)}, u32[]{:S(2)}, u32[]{:S(2)}) async-start(bf16[8,48,768]{2,1,0:T(8,128)(2,1)} %bitcast.1386), calls=%async_computation.2 | async-start | bytes 1179648 | tf_op jit(solution)/shard_map/all_to_all | solution.py:34
  305.7 20.9 %all-to-all-start.3 = ((bf16[8,48,768]{2,1,0:T(8,128)(2,1)}), bf16[8,48,768]{2,1,0:T(8,128)(2,1)}, u32[]{:S(2)}, u32[]{:S(2)}) async-start(bf16[8,48,768]{2,1,0:T(8,128)(2,1)} %bitcast.1382), calls=%async_computation.3 | async-start | bytes 1179648 | tf_op jit(solution)/shard_map/all_to_all | solution.py:34
  309.9 69.2 %all-reduce.25.cloned.1.call-start = ((), (), s32[]{:S(2)}) async-start(), calls=%async_computation.20 | async-start | bytes 786432 | tf_op jit(solution)/shard_map/psum | solution.py:126
  334.6 11.6 copy-start.3
  338.1 7.2 collective-permute-start.1
  346.1 465.5 %copy-start.8 = (bf16[2,128,768]{2,1,0:T(8,128)(2,1)}, bf16[2,128,768]{2,1,0:T(8,128)(2,1)S(1)}, u32[]{:S(2)}) copy-start(bf16[2,128,768]{2,1,0:T(8,128)(2,1)S(1)} %bitcast_dynamic-update-slice_fusion.5) | copy-start | bytes 1179652
  381.6 11.7 copy-start.4
  399.8 22.1 %all-to-all-start.6 = ((bf16[8,48,768]{2,1,0:T(8,128)(2,1)}), bf16[8,48,768]{2,1,0:T(8,128)(2,1)S(1)}, u32[]{:S(2)}, u32[]{:S(2)}) async-start(bf16[8,48,768]{2,1,0:T(8,128)(2,1)} %bitcast.133), calls=%async_computation.6 | async-start | bytes 1179648 | tf_op jit(solution)/shard_map/all_to_all | solution.py:34
  422.0 20.0 %all-to-all-start.8 = ((bf16[8,48,768]{2,1,0:T(8,128)(2,1)}), bf16[8,48,768]{2,1,0:T(8,128)(2,1)}, u32[]{:S(2)}, u32[]{:S(2)}) async-start(bf16[8,48,768]{2,1,0:T(8,128)(2,1)} %bitcast.154), calls=%async_computation.8 | async-start | bytes 1179648 | tf_op jit(solution)/shard_map/all_to_all | solution.py:34
  463.7 20.2 %all-to-all-start.7 = ((bf16[8,48,768]{2,1,0:T(8,128)(2,1)}), bf16[8,48,768]{2,1,0:T(8,128)(2,1)S(1)}, u32[]{:S(2)}, u32[]{:S(2)}) async-start(bf16[8,48,768]{2,1,0:T(8,128)(2,1)} %bitcast.1420), calls=%async_computation.7 | async-start | bytes 1179648 | tf_op jit(solution)/shard_map/all_to_all | solution.py:34
  483.9 19.9 %all-to-all-start.9 = ((bf16[8,48,768]{2,1,0:T(8,128)(2,1)}), bf16[8,48,768]{2,1,0:T(8,128)(2,1)}, u32[]{:S(2)}, u32[]{:S(2)}) async-start(bf16[8,48,768]{2,1,0:T(8,128)(2,1)} %bitcast.1417), calls=%async_computation.9 | async-start | bytes 1179648 | tf_op jit(solution)/shard_map/all_to_all | solution.py:34
  488.1 70.0 %all-reduce.27.cloned.1.call-start = ((), (), s32[]{:S(2)}) async-start(), calls=%async_computation.21 | async-start | bytes 786432 | tf_op jit(solution)/shard_map/psum | solution.py:238
  540.4 54.6 %all-reduce.29.cloned.1.call-start = ((), (), s32[]{:S(2)}) async-start(), calls=%async_computation.22 | async-start | bytes 786432 | tf_op jit(solution)/shard_map/psum | solution.py:126
  575.1 19.9 %copy-start.19 = (f32[128,768]{1,0:T(8,128)S(1)}, f32[128,768]{1,0:T(8,128)}, u32[]{:S(2)}) copy-start(f32[128,768]{1,0:T(8,128)} %copy-done.18) | copy-start | bytes 1179652
  575.1 19.9 %copy-start.117 = (f32[128]{0:T(128)S(1)}, f32[128]{0:T(128)}, u32[]{:S(2)}) copy-start(f32[128]{0:T(128)} %copy-done.116) | copy-start | bytes 1540
  575.1 22.6 %copy-start.79 = (f32[768]{0:T(1024)S(1)}, f32[768]{0:T(1024)}, u32[]{:S(2)}) copy-start(f32[768]{0:T(1024)} %copy-done.77) | copy-start | bytes 9220
  575.2 22.8 %copy-start.103 = (s32[128,2]{1,0:T(8,128)S(1)}, s32[128,2]{1,0:T(8,128)}, u32[]{:S(2)}) copy-start(s32[128,2]{1,0:T(8,128)} %copy.203) | copy-start | bytes 3076
  577.9 24.0 %copy-start.131 = (s32[1024]{0:T(1024)S(1)}, s32[1024]{0:T(1024)}, u32[]{:S(2)}) copy-start(s32[1024]{0:T(1024)} %pad_clamp_fusion.5) | copy-start | bytes 12292
  577.9 19.0 %copy-start.181 = (f32[128]{0:T(128)}, f32[128]{0:T(128)S(1)}, u32[]{:S(2)}) copy-start(f32[128]{0:T(128)S(1)} %broadcast_multiply_fusion.4) | copy-start | bytes 1540
  599.4 9.2 collective-permute-start.2
  618.6 21.6 %all-to-all-start.10 = ((bf16[8,48,768]{2,1,0:T(8,128)(2,1)}), bf16[8,48,768]{2,1,0:T(8,128)(2,1)}, u32[]{:S(2)}, u32[]{:S(2)}) async-start(bf16[8,48,768]{2,1,0:T(8,128)(2,1)} %bitcast.192), calls=%async_computation.10 | async-start | bytes 1179648 | tf_op jit(solution)/shard_map/all_to_all | solution.py:34
  640.2 19.7 %all-to-all-start.12 = ((bf16[8,48,768]{2,1,0:T(8,128)(2,1)}), bf16[8,48,768]{2,1,0:T(8,128)(2,1)}, u32[]{:S(2)}, u32[]{:S(2)}) async-start(bf16[8,48,768]{2,1,0:T(8,128)(2,1)} %bitcast.1387), calls=%async_computation.12 | async-start | bytes 1179648 | tf_op jit(solution)/shard_map/all_to_all | solution.py:34
  681.7 21.0 %all-to-all-start.11 = ((bf16[8,48,768]{2,1,0:T(8,128)(2,1)}), bf16[8,48,768]{2,1,0:T(8,128)(2,1)}, u32[]{:S(2)}, u32[]{:S(2)}) async-start(bf16[8,48,768]{2,1,0:T(8,128)(2,1)} %bitcast.1422), calls=%async_computation.11 | async-start | bytes 1179648 | tf_op jit(solution)/shard_map/all_to_all | solution.py:34
  702.7 20.1 %all-to-all-start.13 = ((bf16[8,48,768]{2,1,0:T(8,128)(2,1)}), bf16[8,48,768]{2,1,0:T(8,128)(2,1)}, u32[]{:S(2)}, u32[]{:S(2)}) async-start(bf16[8,48,768]{2,1,0:T(8,128)(2,1)} %bitcast.1419), calls=%async_computation.13 | async-start | bytes 1179648 | tf_op jit(solution)/shard_map/all_to_all | solution.py:34
  706.8 69.2 %all-reduce.31.cloned.1.call-start = ((), (), s32[]{:S(2)}) async-start(), calls=%async_computation.23 | async-start | bytes 786432 | tf_op jit(solution)/shard_map/psum | solution.py:238
  758.5 53.1 %all-reduce.37.cloned.1.call-start = ((), (), s32[]{:S(2)}) async-start(), calls=%async_computation.26 | async-start | bytes 1572864 | tf_op jit(solution)/shard_map/psum | solution.py:126
  760.4 15.7 %copy-start.120 = (f32[128]{0:T(128)S(1)}, f32[128]{0:T(128)}, u32[]{:S(2)}) copy-start(f32[128]{0:T(128)} %copy-done.119) | copy-start | bytes 1540
  800.1 11.5 copy-start.16
  800.1 11.5 copy-start.121
  800.1 13.5 %copy-start.26 = (bf16[128,768]{1,0:T(8,128)(2,1)S(1)}, bf16[128,768]{1,0:T(8,128)(2,1)}, u32[]{:S(2)}) copy-start(bf16[128,768]{1,0:T(8,128)(2,1)} %copy-done.24) | copy-start | bytes 589828
  813.8 18.4 %collective-permute-start.3 = (bf16[128,768]{1,0:T(8,128)(2,1)}, bf16[128,768]{1,0:T(8,128)(2,1)S(1)}, u32[]{:S(2)}, u32[]{:S(2)}) collective-permute-start(bf16[128,768]{1,0:T(8,128)(2,1)} %get-tuple-element.114), channel_id=1, source_target_pairs={{16,0},{17,1},{18,2},{19,3},{20,4},{21,5},{22,6},{23,7},{24,8},{25... | collective-permute-start | bytes 589832 | tf_op jit(solution)/shard_map/ppermute | solution.py:16
  822.8 22.6 %all-to-all-start.4 = ((bf16[8,48,768]{2,1,0:T(8,128)(2,1)}), bf16[8,48,768]{2,1,0:T(8,128)(2,1)}, u32[]{:S(2)}, u32[]{:S(2)}) async-start(bf16[8,48,768]{2,1,0:T(8,128)(2,1)} %bitcast.1385), calls=%async_computation.4 | async-start | bytes 1179648 | tf_op jit(solution)/shard_map/all_to_all | solution.py:34
  845.4 19.9 %all-to-all-start.14 = ((bf16[8,48,768]{2,1,0:T(8,128)(2,1)}), bf16[8,48,768]{2,1,0:T(8,128)(2,1)}, u32[]{:S(2)}, u32[]{:S(2)}) async-start(bf16[8,48,768]{2,1,0:T(8,128)(2,1)} %bitcast.1389), calls=%async_computation.14 | async-start | bytes 1179648 | tf_op jit(solution)/shard_map/all_to_all | solution.py:34
  865.3 20.0 %all-to-all-start.16 = ((bf16[8,48,768]{2,1,0:T(8,128)(2,1)}), bf16[8,48,768]{2,1,0:T(8,128)(2,1)}, u32[]{:S(2)}, u32[]{:S(2)}) async-start(bf16[8,48,768]{2,1,0:T(8,128)(2,1)} %bitcast.1388), calls=%async_computation.16 | async-start | bytes 1179648 | tf_op jit(solution)/shard_map/all_to_all | solution.py:34
  896.5 17.9 %copy-start.7 = (bf16[128,768]{1,0:T(8,128)(2,1)S(1)}, bf16[128,768]{1,0:T(8,128)(2,1)}, u32[]{:S(2)}) copy-start(bf16[128,768]{1,0:T(8,128)(2,1)} %copy-done.6) | copy-start | bytes 589828
  896.5 17.9 %copy-start.90 = (f32[128,1,8]{2,1,0:T(1,128)S(1)}, f32[128,1,8]{2,1,0:T(1,128)}, u32[]{:S(2)}) copy-start(f32[128,1,8]{2,1,0:T(1,128)} %copy-done.89) | copy-start | bytes 12292
  896.5 17.9 %copy-start.96 = (f32[768,8]{0,1:T(8,128)S(1)}, f32[768,8]{0,1:T(8,128)}, u32[]{:S(2)}) copy-start(f32[768,8]{0,1:T(8,128)} %convolution_select_fusion.5) | copy-start | bytes 73732
  896.5 18.8 %copy-start.196 = (f32[32,6]{0,1:T(8,128)S(1)}, f32[32,6]{0,1:T(8,128)}, u32[]{:S(2)}) copy-start(f32[32,6]{0,1:T(8,128)} %fusion.285) | copy-start | bytes 2308
  896.5 21.6 %copy-start.87 = (bf16[6,64,128]{2,1,0:T(8,128)(2,1)S(1)}, bf16[6,64,128]{2,1,0:T(8,128)(2,1)}, u32[]{:S(2)}) copy-start(bf16[6,64,128]{2,1,0:T(8,128)(2,1)} %convolution_convert_fusion.10) | copy-start | bytes 294916
  910.0 21.2 %all-to-all-start.17 = ((bf16[8,48,768]{2,1,0:T(8,128)(2,1)}), bf16[8,48,768]{2,1,0:T(8,128)(2,1)}, u32[]{:S(2)}, u32[]{:S(2)}) async-start(bf16[8,48,768]{2,1,0:T(8,128)(2,1)} %bitcast.1421), calls=%async_computation.17 | async-start | bytes 1179648 | tf_op jit(solution)/shard_map/all_to_all | solution.py:34
  920.8 14.6 %copy-start.17 = (f32[128,768]{1,0:T(8,128)S(1)}, f32[128,768]{1,0:T(8,128)}, u32[]{:S(2)}) copy-start(f32[128,768]{1,0:T(8,128)} %copy-done.15) | copy-start | bytes 1179652
  931.2 20.3 %all-to-all-start.15 = ((bf16[8,48,768]{2,1,0:T(8,128)(2,1)}), bf16[8,48,768]{2,1,0:T(8,128)(2,1)}, u32[]{:S(2)}, u32[]{:S(2)}) async-start(bf16[8,48,768]{2,1,0:T(8,128)(2,1)} %bitcast.1418), calls=%async_computation.15 | async-start | bytes 1179648 | tf_op jit(solution)/shard_map/all_to_all | solution.py:34
  951.5 64.4 %all-to-all-start.5 = ((bf16[8,48,768]{2,1,0:T(8,128)(2,1)}), bf16[8,48,768]{2,1,0:T(8,128)(2,1)}, u32[]{:S(2)}, u32[]{:S(2)}) async-start(bf16[8,48,768]{2,1,0:T(8,128)(2,1)} %bitcast.1272), calls=%async_computation.5 | async-start | bytes 1179648 | tf_op jit(solution)/shard_map/all_to_all | solution.py:34
  955.8 75.6 %all-reduce.33.cloned.1.call-start = ((), (), s32[]{:S(2)}) async-start(), calls=%async_computation.24 | async-start | bytes 786432 | tf_op jit(solution)/shard_map/psum | solution.py:238
  988.7 197.5 %all-reduce.35.cloned.1.call-start = ((), (), s32[]{:S(2)}) async-start(), calls=%async_computation.25 | async-start | bytes 9437184 | tf_op jit(solution)/shard_map/psum | solution.py:346
  1028.2 46.8 %copy-start.153 = (f32[128]{0:T(128)S(1)}, f32[128]{0:T(128)}, u32[]{:S(2)}) copy-start(f32[128]{0:T(128)} %copy-done.151) | copy-start | bytes 1540
  (165 other events, 871.3 us)
Sparse Core Ops, SparseCore 0:
  119.1 21.1 all-reduce.20
  240.2 18.9 all-reduce.22
  360.1 19.0 all-reduce.24
  540.5 17.4 all-reduce.26
  575.3 19.6 all-reduce.28
  758.6 17.4 all-reduce.30
  791.1 20.4 all-reduce.36
  988.8 20.5 all-reduce.32
  1013.6 172.4 all-reduce.34
where the time goes:
time: 1210 us; the launch traced here: 1200 us
  waiting for transfers between devices  316 us (26%)
  local copies, waits for them, and re-layouts  275 us (23%)
  matrix products  250 us (21%)
  other arithmetic  153 us (13%)
  starting transfers between devices  95.6 us (8%)
  blocking collectives  91.5 us (8%)
  between operations  16.8 us (1%)
    all_to_all x18, waiting for transfers between devices, send_rows(): return lax.all_to_all(rows, 'dp', split_axis=0, concat_axis=0, tiled=True)  117 us
    psum x1, waiting for transfers between devices, local(): lax.psum((totals[0], totals[1], totals[2], totals[3], totals[4]), 'dp')  107 us
    gather x1, local copies, waits for them, and re-layouts, score_context(): bucket_grid = jnp.take(dist_bucket, offsets)  97.2 us
    all_to_all x18, starting transfers between devices, send_rows(): return lax.all_to_all(rows, 'dp', split_axis=0, concat_axis=0, tiled=True)  84.2 us
    psum x5, waiting for transfers between devices, forward_rest(): lax.psum(jnp.dot(mixed_rows, out_weight, preferred_element_type=jnp.float...  57.2 us
    psum x5, blocking collectives, sum_slots(): return lax.psum(partial_rows, 'tensor')  49.8 us
    dot_general x6, matrix products, forward_rest(): jnp.einsum('secf,efd->secd', hidden, lower_weight, preferred_element_type...  49.3 us
    psum x1, blocking collectives, local(): lax.psum((totals[0], totals[1], totals[2], totals[3], totals[4]), 'dp')  41.6 us
  transfers between devices with their start and end apart: 31, of which 28 were waited for; matrix products, arithmetic and copies ran while one was open for 25% of the time, Pallas kernels for 0%

commit v1 on v0

--- a/solution.py
+++ b/solution.py
@@ -3,6 +3,8 @@
 import jax
 import jax.numpy as jnp
 from jax import lax
+from jax.experimental import pallas as pl
+from jax.experimental.pallas import tpu as pltpu
 from jax.sharding import PartitionSpec as P
 
 norm_eps = 1e-06
@@ -359,6 +361,654 @@
     )
 
 
+def gelu_parts(values):
+    size = jnp.abs(values)
+    turn = 1.0 / (1.0 + 0.23164190 * size)
+    bell = jnp.exp(-0.5 * values * values)
+    poly = turn * (
+        0.127414796
+        + turn * (-0.142248368 + turn * (0.7107068705 + turn * (-0.7265760135 + turn * 0.5307027145)))
+    )
+    tail = poly * bell
+    share = jnp.where(values >= 0.0, 1.0 - tail, tail)
+    return (values * share, share + values * (0.3989422804 * bell))
+
+
+def nn(left, right):
+    return lax.dot_general(left, right, (((1,), (0,)), ((), ())), preferred_element_type=jnp.float32)
+
+
+def nt(left, right):
+    return lax.dot_general(left, right, (((1,), (1,)), ((), ())), preferred_element_type=jnp.float32)
+
+
+def tn(left, right):
+    return lax.dot_general(left, right, (((0,), (0,)), ((), ())), preferred_element_type=jnp.float32)
+
+
+def tn_exact(left, right):
+    return lax.dot_general(
+        left, right, (((0,), (0,)), ((), ())), preferred_element_type=jnp.float32, precision=highest
+    )
+
+
+def split_low(values):
+    high = values.astype(jnp.bfloat16)
+    return (high, (values - high.astype(jnp.float32)).astype(jnp.bfloat16))
+
+
+def inverse_rms(values):
+    return lax.rsqrt(jnp.mean(values * values, axis=-1, keepdims=True) + norm_eps)
+
+
+class Layout:
+    pass
+
+
+def layer_kernel(lay, *refs):
+    (
+        tok_ref, cot_ref, seg_ref, pad_ref, routes_ref, dist_ref, gains_ref, qkvw_ref, outw_ref, relb_ref, wr_ref,
+        up_ref, down_ref,
+        secout_ref, ingrad_ref, ggain_ref, gqkv_ref, gout_ref, gbias_ref, grouter_ref, gup_ref, gdown_ref,
+        upv, downv, xb, dyb, rr, place, bias_buf, probs_buf, no1, qkvb, mixed, att_send, att_recv, mid, ntb,
+        gate_t, hit_t, score_sum, disp_x, xrows, disp_y, dyrows, hidden, dgelu, eo_send, eo_recv, eob, eoret, out_own, x_send,
+        other, og, gg_send, gg_recv, pg, cg_send, cg_recv, cgb, cgret, mgrad, ag, mg, qkvg,
+        no_send, no_recv, ig_own, dy_send, guv, gdv, wsem, gsem, ss, rs,
+    ) = refs
+    bf = jnp.bfloat16
+    f32 = jnp.float32
+    micro, length, width = tok_ref.shape
+    experts = lay.experts
+    cap = lay.cap
+    cols = outw_ref.shape[0]
+    pairs = cols // 128
+    ffn = up_ref.shape[1]
+    slots = experts * cap
+    half = width // 2
+    s = lax.axis_index("section")
+    d = lax.axis_index("dp")
+    t = lax.axis_index("tensor")
+    u = 1 - t
+    sib = (s, d, u)
+    across = (1 - s, d, t)
+    steps = range(1, experts)
+    ahead = [lax.rem(d + k, experts) for k in range(experts)]
+    behind = [lax.rem(d + experts - k, experts) for k in range(experts)]
+
+    def remote(src, dst, index, device):
+        return pltpu.make_async_remote_copy(
+            src_ref=src,
+            dst_ref=dst,
+            send_sem=ss.at[index],
+            recv_sem=rs.at[index],
+            device_id=device,
+            device_id_type=pl.DeviceIdType.MESH,
+        )
+
+    counter = [0]
+
+    def take(amount):
+        counter[0] += amount
+        return counter[0] - amount
+
+    sent = []
+
+    def fire(copy):
+        copy.start()
+        sent.append(copy)
+
+    sem_routes = take(experts)
+    sem_x = take(1)
+    sem_xf = take(1)
+    sem_dy = take(1)
+    sem_att = take(1)
+    sem_eo = take(1)
+    sem_cg = take(1)
+    sem_ag = take(1)
+    sem_no = take(1)
+    sem_so = take(1)
+    sem_ig = take(1)
+    sem_dx = take(experts)
+    sem_dxf = take(experts)
+    sem_ddy = take(experts)
+    sem_ddyf = take(experts)
+    sem_re = take(experts)
+    sem_rc = take(experts)
+    sem_gg = take(experts)
+    assert counter[0] == lay.sems
+
+    def block(index, rows):
+        return pl.ds(pl.multiple_of(index * rows, rows), rows)
+
+    load_up = pltpu.make_async_copy(up_ref, upv, wsem.at[0])
+    load_down = pltpu.make_async_copy(down_ref, downv, wsem.at[1])
+    load_up.start()
+    load_down.start()
+
+    barrier = pltpu.get_barrier_semaphore()
+    for k in steps:
+        pl.semaphore_signal(barrier, inc=1, device_id=(s, ahead[k], t), device_id_type=pl.DeviceIdType.MESH)
+    pl.semaphore_signal(barrier, inc=1, device_id=sib, device_id_type=pl.DeviceIdType.MESH)
+    pl.semaphore_signal(barrier, inc=1, device_id=across, device_id_type=pl.DeviceIdType.MESH)
+    pl.semaphore_wait(barrier, experts + 1)
+
+    for k in steps:
+        fire(remote(routes_ref, rr.at[d], sem_routes + k, (s, ahead[k], t)))
+    rr[d] = routes_ref[...]
+
+    lanes8 = lax.broadcasted_iota(jnp.int32, (experts, length), 0)
+    row_at = lax.broadcasted_iota(jnp.int32, (length, length), 0)
+    col_at = lax.broadcasted_iota(jnp.int32, (length, length), 1)
+    before = (row_at < col_at).astype(bf)
+    slot_at = lax.broadcasted_iota(jnp.int32, (cap, length), 0).astype(f32)
+
+    own_routes = routes_ref[t]
+    hits = (lanes8 == own_routes[0:1, :]) | (lanes8 == own_routes[1:2, :])
+    hit_f = hits.astype(f32)
+    hit_t[...] = hit_f
+    spot = jnp.where(hits, nn(hit_f.astype(bf), before), -1.0)
+    for e in range(experts):
+        place[e * cap : (e + 1) * cap, :] = (slot_at == spot[e : e + 1, :]).astype(f32).astype(bf)
+
+    def dispatch(rows, send, landing, base, base_fwd):
+        send[...] = nn(place[...], rows).astype(bf)
+        mine = block(d, cap)
+        out = [remote(send.at[block(ahead[k], cap)], landing.at[t, mine], base + k, (s, ahead[k], t)) for k in steps]
+        for copy in out:
+            copy.start()
+        first = remote(send.at[mine], landing.at[t, mine], base_fwd, sib)
+        first.start()
+        landing[t, mine, :] = send[mine, :]
+        passed = [first]
+        for k in steps:
+            out[k - 1].wait_recv()
+            from_block = block(behind[k], cap)
+            copy = remote(landing.at[t, from_block], landing.at[t, from_block], base_fwd + k, sib)
+            copy.start()
+            passed.append(copy)
+        for copy in passed:
+            copy.wait()
+        for copy in out:
+            copy.wait_send()
+
+    @pl.when(s == 0)
+    def _():
+        xb[...] = tok_ref[...]
+
+    @pl.when(s == 1)
+    def _():
+        dyb[...] = cot_ref[t]
+        dispatch(dyb[...], disp_y, dyrows, sem_ddy, sem_ddyf)
+
+    dist_rows = (
+        lax.broadcasted_iota(jnp.int32, (lay.buckets, length), 0) == dist_ref[...]
+    ).astype(f32).astype(bf)
+    bias_rows = nn(relb_ref[...], dist_rows).astype(bf)
+    mirror = ((row_at + col_at == length) | (row_at + col_at == 0)).astype(f32).astype(bf)
+    bias_back = nn(bias_rows, mirror)
+    for m in range(micro):
+        seg_rows = jnp.broadcast_to(seg_ref[m : m + 1, :].astype(f32), (length, length))
+        pads = jnp.broadcast_to(pad_ref[m : m + 1, :], (length, length))
+        allowed = (col_at <= row_at) & (seg_rows == jnp.transpose(seg_rows))
+        allowed = allowed & ((pads == 1) | (col_at == row_at))
+        for p in range(pairs):
+            for h in range(2):
+                head = 2 * p + h
+                grid = pltpu.roll(
+                    jnp.broadcast_to(bias_back[head : head + 1, :], (length, length)), 0, 1, stride=1, stride_axis=0
+                )
+                bias_buf[m, p, :, h * length : (h + 1) * length] = jnp.where(allowed, grid, masked_score)
+
+    @pl.when(s == 1)
+    def _():
+        remote(x_send, xb.at[t], sem_x, across).wait_recv()
+        copy = remote(xb.at[t], xb.at[t], sem_xf, sib)
+        copy.start()
+        copy.wait()
+
+    gain_one = gains_ref[0:1, :].astype(f32)
+    gain_two = gains_ref[1:2, :].astype(f32)
+    low_lanes = lax.broadcasted_iota(jnp.int32, (length, 128), 1) < 64
+
+    def both_heads(pair_block):
+        zero = jnp.zeros((), bf)
+        return jnp.concatenate(
+            [jnp.where(low_lanes, pair_block, zero), jnp.where(low_lanes, zero, pair_block)], axis=0
+        )
+
+    for m in range(micro):
+        x_rows = xb[m].astype(f32)
+        no1[m] = (x_rows * inverse_rms(x_rows) * gain_one).astype(bf)
+    for c in range(3):
+        w = qkvw_ref[c]
+        for m in range(micro):
+            qkvb[c, m] = nn(no1[m], w).astype(bf)
+    for m in range(micro):
+        for p in range(pairs):
+            at = slice(p * 128, (p + 1) * 128)
+            scores = 0.125 * nt(qkvb[0, m, :, at], both_heads(qkvb[1, m, :, at])) + bias_buf[m, p]
+            for h in range(2):
+                part = scores[:, h * length : (h + 1) * length]
+                terms = jnp.exp(part - jnp.max(part, axis=-1, keepdims=True))
+                probs_buf[m, p, :, h * length : (h + 1) * length] = terms * (
+                    1.0 / jnp.sum(terms, axis=-1, keepdims=True)
+                )
+            mixed[m, :, at] = nn(probs_buf[m, p].astype(bf), both_heads(qkvb[2, m, :, at])).astype(bf)
+
+    att_send[...] = nn(mixed[u], outw_ref[...])
+    att_copy = remote(att_send, att_recv, sem_att, sib)
+    att_copy.start()
+    part_own = nn(mixed[t], outw_ref[...])
+    att_copy.wait()
+    middle = xb[t].astype(f32) + part_own + att_recv[...]
+    mid[...] = middle
+    ntb[...] = (middle * inverse_rms(middle) * gain_two).astype(bf)
+    logits_t = jnp.where(hit_t[...] > 0.0, nt(wr_ref[...], ntb[...]), masked_score)
+    terms = jnp.exp(logits_t - jnp.max(logits_t, axis=0, keepdims=True))
+    gate_t[...] = terms / jnp.sum(terms, axis=0, keepdims=True)
+
+    dispatch(ntb[...], disp_x, xrows, sem_dx, sem_dxf)
+
+    load_up.wait()
+    load_down.wait()
+    flat = micro * slots
+    row_tile = lay.row_tile
+    col_tile = lay.col_tile
+    per_micro = slots // row_tile
+
+    def forward_tile(i, carry):
+        at = pl.ds(pl.multiple_of((i % (ffn // col_tile)) * col_tile, col_tile), col_tile)
+        j = i // (ffn // col_tile)
+        m = j // per_micro
+        rows = block(j % per_micro, row_tile)
+        value, slope = gelu_parts(nn(xrows[m, rows, :], upv[:, at]))
+        hidden[m, rows, at] = value.astype(bf)
+        dgelu[m, rows, at] = slope.astype(bf)
+        return carry
+
+    lax.fori_loop(0, (flat // row_tile) * (ffn // col_tile), forward_tile, 0)
+
+    eo_send[...] = nn(hidden[u], downv[...]).astype(bf)
+    eo_copy = remote(eo_send, eo_recv, sem_eo, sib)
+    eo_copy.start()
+    part_own = nn(hidden[t], downv[...])
+    eo_copy.wait()
+    eob[...] = (part_own + eo_recv[...].astype(f32)).astype(bf)
+
+    def send_back(source, landing, base):
+        mine = block(d, cap)
+        out = [remote(source.at[block(ahead[k], cap)], landing.at[mine], base + k, (s, ahead[k], t)) for k in steps]
+        for copy in out:
+            copy.start()
+        landing[mine, :] = source[mine, :]
+        return out
+
+    def finish(copies):
+        for copy in copies:
+            copy.wait()
+
+    def spread_gates():
+        return jnp.concatenate(
+            [
+                jnp.broadcast_to(gate_t[e : e + 1, :], (cap, length)) * place[e * cap : (e + 1) * cap, :].astype(f32)
+                for e in range(experts)
+            ],
+            axis=0,
+        ).astype(bf)
+
+    def layer_output():
+        result = mid[...] + tn(spread_gates(), eoret[...])
+        out_own[...] = result
+        return result
+
+    def own_half():
+        return pl.ds(pl.multiple_of(t * half, half), half)
+
+    def other_half():
+        return pl.ds(pl.multiple_of(u * half, half), half)
+
+    def hand_out(rows_ref, out_ref, index):
+        copy = remote(rows_ref.at[:, other_half()], out_ref.at[t], index, sib)
+        copy.start()
+        out_ref[t] = rows_ref[:, own_half()]
+        copy.wait()
+
+    @pl.when(s == 0)
+    def _():
+        finish(send_back(eob, eoret, sem_re))
+        x_send[...] = layer_output().astype(bf)
+        copy = remote(x_send, xb.at[t], sem_x, across)
+        copy.start()
+        hand_out(out_own, secout_ref, sem_so)
+        copy.wait_send()
+        remote(dy_send, dyb, sem_dy, across).wait_recv()
+        dispatch(dyb[...], disp_y, dyrows, sem_ddy, sem_ddyf)
+
+    for k in steps:
+        remote(routes_ref, rr.at[behind[k]], sem_routes + k, (s, ahead[k], t)).wait_recv()
+
+    def other_experts(i, carry):
+        q = i // micro
+        m = i % micro
+        pair = rr[q, m]
+        first = pair[0:1, :] == d
+        mine = first | (pair[1:2, :] == d)
+        mine_f = jnp.broadcast_to(mine.astype(f32), (experts, length))
+        spots = jnp.where(mine_f > 0.0, nn(mine_f.astype(bf), before), -1.0)
+        where_slot = (slot_at == spots[0:1, :]).astype(f32).astype(bf)
+        partner = jnp.where(first, pair[1:2, :], pair[0:1, :])
+        partner_hot = (lanes8 == partner).astype(f32).astype(bf)
+        other[m, block(q, cap), :] = nt(where_slot, partner_hot)
+        return carry
+
+    lax.fori_loop(0, experts * micro, other_experts, 0)
+    mine_hot = (lax.broadcasted_iota(jnp.int32, (slots, experts), 1) == d).astype(f32)
+    for m in range(micro):
+        slot_logits = nt(xrows[m], wr_ref[...])
+        own_logit = jnp.sum(slot_logits * mine_hot, axis=-1, keepdims=True)
+        other_logit = jnp.sum(slot_logits * other[m], axis=-1, keepdims=True)
+        gate = 1.0 / (1.0 + jnp.exp(other_logit - own_logit))
+        og[m] = (dyrows[m].astype(f32) * gate).astype(bf)
+
+    gg_send[...] = jnp.zeros_like(gg_send)
+    ones = jnp.ones((8, width), bf)
+    for q in range(experts):
+        at = slice(q * cap, (q + 1) * cap)
+        high, low = split_low(dyrows[t, at, :].astype(f32) * eob[at, :].astype(f32))
+        gg_send[q, :, 0:cap] = nt(ones, high) + nt(ones, low)
+
+    def backward_tile(i, carry):
+        at = pl.ds(pl.multiple_of((i % (ffn // col_tile)) * col_tile, col_tile), col_tile)
+        j = i // (ffn // col_tile)
+        m = j // per_micro
+        rows = block(j % per_micro, row_tile)
+        grad = nt(og[m, rows, :], downv[at, :])
+        pg[m, rows, at] = (grad * dgelu[m, rows, at].astype(f32)).astype(bf)
+        return carry
+
+    lax.fori_loop(0, (flat // row_tile) * (ffn // col_tile), backward_tile, 0)
+    cg_send[...] = nt(pg[u], upv[...]).astype(bf)
+    cg_copy = remote(cg_send, cg_recv, sem_cg, sib)
+    cg_copy.start()
+    gg_out = [remote(gg_send.at[ahead[k]], gg_recv.at[d], sem_gg + k, (s, ahead[k], t)) for k in steps]
+    for copy in gg_out:
+        copy.start()
+    gg_recv[d] = gg_send[d]
+    part_own = nt(pg[t], upv[...])
+    cg_copy.wait()
+    cgb[...] = (part_own + cg_recv[...].astype(f32)).astype(bf)
+    cg_out = send_back(cgb, cgret, sem_rc)
+
+    wide = lay.wide
+    for n in range(ffn // wide):
+        at = slice(n * wide, (n + 1) * wide)
+        total = tn(xrows[0], pg[0, :, at])
+        for m in range(1, micro):
+            total = total + tn(xrows[m], pg[m, :, at])
+        guv[:, at] = total
+        pltpu.make_async_copy(guv.at[:, at], gup_ref.at[:, at], gsem.at[n]).start()
+        total = tn(hidden[0, :, at], og[0])
+        for m in range(1, micro):
+            total = total + tn(hidden[m, :, at], og[m])
+        gdv[at, :] = total
+        pltpu.make_async_copy(gdv.at[at, :], gdown_ref.at[at, :], gsem.at[ffn // wide + n]).start()
+
+    finish(gg_out)
+    finish(cg_out)
+    gg_rows = []
+    for e in range(experts):
+        high, low = split_low(gg_recv[e][:, 0:cap])
+        spot_rows = place[e * cap : (e + 1) * cap, :]
+        gg_rows.append((nn(high, spot_rows) + nn(low, spot_rows))[0:1, :])
+    gate_grad = jnp.concatenate(gg_rows, axis=0)
+    gates = gate_t[...]
+    logit_grad = (gates * (gate_grad - jnp.sum(gates * gate_grad, axis=0, keepdims=True))).astype(bf)
+    grouter_ref[...] = nn(logit_grad, ntb[...])
+    two_grad = tn(logit_grad, wr_ref[...]) + tn(place[...], cgret[...])
+    dy = dyb[...].astype(f32)
+    middle = mid[...]
+    scale = inverse_rms(middle)
+    normed = middle * scale
+    ggain_ref[1:2, :] = jnp.sum(two_grad * normed, axis=0, keepdims=True)
+    scaled = two_grad * gain_two
+    middle_grad = dy + scale * (scaled - normed * jnp.mean(scaled * normed, axis=-1, keepdims=True))
+    mgrad[...] = middle_grad
+    ag[t] = middle_grad.astype(bf)
+    ag_copy = remote(ag.at[t], ag.at[t], sem_ag, sib)
+    ag_copy.start()
+    ag_copy.wait()
+
+    for m in range(micro):
+        mg[m] = nt(ag[m], outw_ref[...]).astype(bf)
+    gout_ref[...] = tn(mixed[0], ag[0]) + tn(mixed[1], ag[1])
+    for m in range(micro):
+        for p in range(pairs):
+            at = slice(p * 128, (p + 1) * 128)
+            mg_pair = mg[m, :, at]
+            probs = probs_buf[m, p]
+            keys2 = both_heads(qkvb[1, m, :, at])
+            queries2 = both_heads(qkvb[0, m, :, at])
+            mg2 = both_heads(mg_pair)
+            prob_grad = nt(mg_pair, both_heads(qkvb[2, m, :, at]))
+            raws = []
+            key_grad = jnp.zeros((length, 128), f32)
+            value_grad = jnp.zeros((length, 128), f32)
+            for h in range(2):
+                lane = slice(h * length, (h + 1) * length)
+                part = probs[:, lane]
+                step = prob_grad[:, lane]
+                score_grad = part * (step - jnp.sum(part * step, axis=-1, keepdims=True))
+                score_sum[2 * p + h] = score_grad if m == 0 else score_sum[2 * p + h] + score_grad
+                raw = (0.125 * score_grad).astype(bf)
+                raws.append(raw)
+                key_grad = key_grad + tn(raw, queries2[h * length : (h + 1) * length])
+                value_grad = value_grad + tn(part.astype(bf), mg2[h * length : (h + 1) * length])
+            qkvg[0, m, :, at] = nn(jnp.concatenate(raws, axis=1), keys2).astype(bf)
+            qkvg[1, m, :, at] = key_grad.astype(bf)
+            qkvg[2, m, :, at] = value_grad.astype(bf)
+    def project_back(m):
+        total = nt(qkvg[0, m], qkvw_ref[0])
+        for c in range(1, 3):
+            total = total + nt(qkvg[c, m], qkvw_ref[c])
+        return total
+
+    no_send[...] = project_back(u).astype(bf)
+    no_copy = remote(no_send, no_recv, sem_no, sib)
+    no_copy.start()
+    one_grad = project_back(t)
+    no_copy.wait()
+    one_grad = one_grad + no_recv[...].astype(f32)
+    x_rows = xb[t].astype(f32)
+    scale = inverse_rms(x_rows)
+    normed = x_rows * scale
+    ggain_ref[0:1, :] = jnp.sum(one_grad * normed, axis=0, keepdims=True)
+    scaled = one_grad * gain_one
+    input_grad = mgrad[...] + scale * (scaled - normed * jnp.mean(scaled * normed, axis=-1, keepdims=True))
+    ig_own[...] = input_grad
+
+    @pl.when(s == 1)
+    def _():
+        dy_send[...] = input_grad.astype(bf)
+        copy = remote(dy_send, dyb, sem_dy, across)
+        copy.start()
+        copy.wait_send()
+
+    hand_out(ig_own, ingrad_ref, sem_ig)
+
+    for c in range(3):
+        gqkv_ref[c] = tn(no1[0], qkvg[c, 0]) + tn(no1[1], qkvg[c, 1])
+
+    sums = []
+    for head in range(2 * pairs):
+        high, low = split_low(score_sum[head])
+        turned = pltpu.roll(nn(high, mirror) + nn(low, mirror), 0, 1, stride=1, stride_axis=0)
+        sums.append(jnp.sum(turned, axis=0, keepdims=True))
+    high, low = split_low(jnp.concatenate(sums, axis=0))
+    gbias_ref[...] = nt(high, dist_rows) + nt(low, dist_rows)
+
+    @pl.when(s == 1)
+    def _():
+        finish(send_back(eob, eoret, sem_re))
+        layer_output()
+        hand_out(out_own, secout_ref, sem_so)
+
+    for copy in sent:
+        copy.wait_send()
+    for n in range(ffn // wide):
+        at = slice(n * wide, (n + 1) * wide)
+        pltpu.make_async_copy(guv.at[:, at], gup_ref.at[:, at], gsem.at[n]).wait()
+        pltpu.make_async_copy(gdv.at[at, :], gdown_ref.at[at, :], gsem.at[ffn // wide + n]).wait()
+
+
+def fused_local(
+    tokens,
+    cotangent,
+    segments,
+    pad_mask,
+    routes,
+    dist_bucket,
+    norm_gains,
+    qkv_weight,
+    out_weight,
+    rel_bias,
+    router_weight,
+    expert_up,
+    expert_down,
+):
+    micro, _, length, width = tokens.shape
+    experts = router_weight.shape[2]
+    cap = max(2, 3 * length // experts)
+    cols = out_weight.shape[1]
+    heads = rel_bias.shape[2]
+    ffn = expert_up.shape[3]
+    slots = experts * cap
+    pairs = cols // 128
+    lay = Layout()
+    lay.experts = experts
+    lay.cap = cap
+    lay.buckets = rel_bias.shape[1]
+    lay.row_tile = min(slots, 192)
+    lay.col_tile = min(ffn, 256)
+    lay.wide = min(ffn, 256)
+    lay.sems = 8 * experts + 10
+    bf = jnp.bfloat16
+    f32 = jnp.float32
+    vm = pltpu.VMEM
+    shape = jax.ShapeDtypeStruct
+    dma = pltpu.SemaphoreType.DMA
+    scratch = [
+        vm((width, ffn), bf),
+        vm((ffn, width), bf),
+        vm((micro, length, width), bf),
+        vm((length, width), bf),
+        vm((experts, micro, 2, length), jnp.int32),
+        vm((slots, length), bf),
+        vm((micro, pairs, length, 2 * length), f32),
+        vm((micro, pairs, length, 2 * length), f32),
+        vm((micro, length, width), bf),
+        vm((3, micro, length, cols), bf),
+        vm((micro, length, cols), bf),
+        vm((length, width), f32),
+        vm((length, width), f32),
+        vm((length, width), f32),
+        vm((length, width), bf),
+        vm((experts, length), f32),
+        vm((experts, length), f32),
+        vm((2 * pairs, length, length), f32),
+        vm((slots, width), bf),
+        vm((micro, slots, width), bf),
+        vm((slots, width), bf),
+        vm((micro, slots, width), bf),
+        vm((micro, slots, ffn), bf),
+        vm((micro, slots, ffn), bf),
+        vm((slots, width), bf),
+        vm((slots, width), bf),
+        vm((slots, width), bf),
+        vm((slots, width), bf),
+        vm((length, width), f32),
+        vm((length, width), bf),
+        vm((micro, slots, experts), f32),
+        vm((micro, slots, width), bf),
+        vm((experts, 8, 128), f32),
+        vm((experts, 8, 128), f32),
+        vm((micro, slots, ffn), bf),
+        vm((slots, width), bf),
+        vm((slots, width), bf),
+        vm((slots, width), bf),
+        vm((slots, width), bf),
+        vm((length, width), f32),
+        vm((micro, length, width), bf),
+        vm((micro, length, cols), bf),
+        vm((3, micro, length, cols), bf),
+        vm((length, width), bf),
+        vm((length, width), bf),
+        vm((length, width), f32),
+        vm((length, width), bf),
+        vm((width, ffn), f32),
+        vm((ffn, width), f32),
+        dma((2,)),
+        dma((2 * (ffn // lay.wide),)),
+        dma((lay.sems,)),
+        dma((lay.sems,)),
+    ]
+    whole = pl.BlockSpec(memory_space=pltpu.VMEM)
+    anywhere = pl.BlockSpec(memory_space=pl.ANY)
+    out_shape = (
+        shape((micro, length, width // 2), f32),
+        shape((micro, length, width // 2), f32),
+        shape((2, width), f32),
+        shape((3, width, cols), f32),
+        shape((cols, width), f32),
+        shape((heads, lay.buckets), f32),
+        shape((experts, width), f32),
+        shape((width, ffn), f32),
+        shape((ffn, width), f32),
+    )
+    results = pl.pallas_call(
+        partial(layer_kernel, lay),
+        out_shape=out_shape,
+        in_specs=[whole] * 11 + [anywhere] * 2,
+        out_specs=[whole] * 7 + [anywhere] * 2,
+        scratch_shapes=scratch,
+        name="two_sections",
+        compiler_params=pltpu.CompilerParams(
+            collective_id=0, has_side_effects=True, vmem_limit_bytes=60 * 1024 * 1024
+        ),
+    )(
+        tokens[:, 0],
+        cotangent[:, 0],
+        segments[:, 0],
+        pad_mask[:, 0],
+        routes[:, 0].transpose(0, 2, 1),
+        dist_bucket[None],
+        norm_gains[0],
+        qkv_weight[0].transpose(1, 0, 2),
+        out_weight[0],
+        rel_bias[0].T,
+        router_weight[0].T,
+        expert_up[0, 0],
+        expert_down[0, 0],
+    )
+    section_out, input_grads, gains, qkv, out, bias, router, up, down = results
+    qkv, out, bias = lax.psum((qkv, out, bias), "dp")
+    gains, router = lax.psum((gains, router), ("dp", "tensor"))
+    return (
+        section_out[None, :, None],
+        input_grads[None, :, None],
+        gains[None],
+        qkv.transpose(1, 0, 2)[None],
+        out[None],
+        bias.T[None],
+        router.T[None],
+        up[None, None],
+        down[None, None],
+    )
+
+
+def fits_kernel(mesh):
+    return mesh.shape["section"] == 2 and mesh.shape["tensor"] == 2 and mesh.shape["dp"] == 8
+
+
 def solution(mesh):
     in_specs = (
         P(None, "dp", None, None),
@@ -386,4 +1036,5 @@
         P("section", "dp", None, "tensor"),
         P("section", "dp", "tensor", None),
     )
-    return jax.shard_map(local, mesh=mesh, in_specs=in_specs, out_specs=out_specs, check_vma=False)
+    body = fused_local if fits_kernel(mesh) else local
+    return jax.shard_map(body, mesh=mesh, in_specs=in_specs, out_specs=out_specs, check_vma=False)

time: 1210 us -> 395 us (0.33)
  local copies, waits for them, and re-layouts: 275 us -> 14.3 us
  matrix products: 250 us -> 0 us
  waiting for transfers between devices: 316 us -> 85.4 us
  Pallas kernels: 0 us -> 194 us
  other arithmetic: 153 us -> 0.01 us
  starting transfers between devices: 95.6 us -> 0.04 us
    dot_general x94 -> x0, matrix products: 250 us -> none  [the longest x6 49.3 us: forward_rest(): jnp.einsum('secf,efd->secd', hidden, lower_weight, preferred_element_type...]
    pallas_call x0 -> x1, Pallas kernels: none -> 194 us  [fused_local(): pl.pallas_call(partial(layer_kernel, lay), out_shape=out_shape, in_specs=...]
    gather x19 -> x0, local copies, waits for them, and re-layouts: 150 us -> none  [the longest x1 97.2 us: score_context(): bucket_grid = jnp.take(dist_bucket, offsets)]
    all_to_all x18 -> x0, waiting for transfers between devices: 117 us -> none  [send_rows(): return lax.all_to_all(rows, 'dp', split_axis=0, concat_axis=0, tiled=True)]
    psum x9 -> x1, waiting for transfers between devices: 190 us -> 85.4 us  [fused_local(): qkv, out, bias = lax.psum((qkv, out, bias), 'dp')]
    all_to_all x18 -> x0, starting transfers between devices: 84.2 us -> none  [send_rows(): return lax.all_to_all(rows, 'dp', split_axis=0, concat_axis=0, tiled=True)]
    reduce_sum x43 -> x0, other arithmetic: 42.6 us -> none  [the longest x3 8.44 us: backward_layer(): normed_two_grad = normed_two_grad + jnp.sum(copy_grads, axis=1)]
    convert_element_type x26 -> x0, other arithmetic: 25.8 us -> none  [the longest x3 6.2 us: forward_rest(): back_rows.astype(jnp.float32)]
  transfers between devices with their start and end apart: 31 -> 1, of which waited for: 28 -> 1; matrix products, arithmetic and copies ran while one was open for 25% -> 0% of each run, Pallas kernels for 0% -> 0%
where the time goes in v1:
time: 395 us
  Pallas kernels  194 us (49%)
  blocking collectives  87.1 us (22%)
  waiting for transfers between devices  85.4 us (22%)
  local copies, waits for them, and re-layouts  14.3 us (4%)
  between operations  14.1 us (4%)
    pallas_call x1, Pallas kernels, fused_local(): pl.pallas_call(partial(layer_kernel, lay), out_shape=out_shape, in_specs=...  194 us
    psum x1, waiting for transfers between devices, fused_local(): qkv, out, bias = lax.psum((qkv, out, bias), 'dp')  85.4 us
    psum x1, blocking collectives, fused_local(): gains, router = lax.psum((gains, router), ('dp', 'tensor'))  61.8 us
    psum x1, blocking collectives, fused_local(): qkv, out, bias = lax.psum((qkv, out, bias), 'dp')  25.2 us
    unnamed x27, local copies, waits for them, and re-layouts  14.3 us
  transfers between devices with their start and end apart: 1, of which 1 were waited for; matrix products, arithmetic and copies ran while one was open for 0% of the time, Pallas kernels for 0%

profile of v1, /device:TPU:0, one launch (start us, length us, event | category | flops | bytes accessed | tf_op | source)
XLA Modules:
  0.0 394.8 jit_solution(10982289245793418757)
XLA Ops:
  7.2 0.0 all-reduce.4.cloned.1.call-start
  7.2 193.8 %two_sections.1 = (f32[2,128,384]{2,1,0:T(8,128)}, f32[2,128,384]{2,1,0:T(8,128)}, f32[2,768]{1,0:T(2,128)}, f32[3,768,384]{2,1,0:T(8,128)}, f32[384,768]{1,0:T(...) custom-call(bf16[2,128,768]{2,1,0:T(8,128)(2,1)} %bitcast.52, ...), custom_call_target="tpu_custom_call" | custom-call | tf_op jit(solution)/shard_map/two_sections/pallas_call | solution.py:967
  201.1 0.0 copy-start.5
  201.1 0.0 copy-start.3
  201.1 0.0 copy-start.4
  201.1 0.0 copy-start.2
  201.1 0.0 copy-start.1
  201.1 0.0 all-reduce.4.cloned.1.call-update
  201.2 0.6 copy-done.5
  201.8 25.2 %psum.38 = f32[1,32,6]{1,2,0:T(8,128)S(1)} all-reduce(f32[1,32,6]{1,2,0:T(8,128)S(1)} %bitcast.59), channel_id=1, replica_groups=mesh['section'=2,'dp'=8,'tensor'=2] {'dp'}, use_global_device_ids=true, to_apply=%region_3.0 | all-reduce | flops 192 | bytes 1536 | tf_op jit(solution)/shard_map/psum | solution.py:993
  227.0 0.6 copy.24
  227.6 0.0 copy-done.3
  227.6 0.0 copy-done.4
  227.6 61.8 %all-reduce = (f32[1,2,768]{2,1,0:T(2,128)}, f32[1,768,8]{1,2,0:T(8,128)}) all-reduce(f32[1,2,768]{2,1,0:T(2,128)S(1)} %bitcast.58, f32[1,768,8]{1,2,0:T(8,128)S(1)} %bitcast.56), channel_id=1, replica_groups=mesh['section'=2,'dp'=8,'tensor'=2] {'dp','tensor'}, use_global_device_ids=true, to_apply=%region_0.0 | all-reduce | flops 7680 | bytes 61440 | tf_op jit(solution)/shard_map/psum | solution.py:994
  289.4 85.4 %all-reduce.4.cloned.1.call-done = (f32[1,768,3,384]{3,1,2,0:T(8,128)}, f32[1,384,768]{2,1,0:T(8,128)}) async-done(((f32[1,768,3,384]{3,1,2,0:T(8,128)}, f32[1,384,768]{2,1,0:T(8,128)}), (f32[1,768,3,384]{3,1,2,0:T(8,128)}, f32[1,384,768]{2,1,0:T(8,128)})) %all-reduce.4.cloned.1.call-update) | async-done | bytes 4718608 | tf_op jit(solution)/shard_map/psum | solution.py:993
  374.8 0.0 copy-done.2
  374.8 0.7 copy.33
  375.6 0.0 copy-done.1
  375.6 0.0 slice-start.2
  375.6 0.7 copy.34
  376.3 0.0 copy-start
  376.3 0.0 slice-start.3
  376.3 4.9 %copy.35 = f32[1,768,3,384]{3,1,2,0:T(8,128)} copy(f32[1,768,3,384]{3,1,2,0:T(8,128)} %get-tuple-element.52) | data formatting | bytes 7077888
  381.2 0.0 copy-done
  381.2 0.0 slice-start
  381.2 1.0 copy.36
  382.2 0.0 slice-done.2
  382.2 0.0 slice-done.3
  382.2 0.0 slice-start.1
  382.2 2.4 copy.37
  384.6 0.8 slice-done
  385.4 0.3 slice-done.1
  385.8 2.2 copy.38
  (2 shorter events, 0.0 us)
Async XLA Ops:
  7.2 367.7 %all-reduce.4.cloned.1.call-start = ((), (), s32[]{:S(2)}) async-start(), calls=%async_computation | async-start | bytes 9437184 | tf_op jit(solution)/shard_map/psum | solution.py:993
  201.1 0.7 copy-start.5
  201.1 26.5 %copy-start.3 = (f32[8,768]{1,0:T(8,128)S(1)}, f32[8,768]{1,0:T(8,128)}, u32[]{:S(2)}) copy-start(f32[8,768]{1,0:T(8,128)} %get-tuple-element.24) | copy-start | bytes 73732
  201.1 26.5 %copy-start.4 = (f32[2,768]{1,0:T(2,128)S(1)}, f32[2,768]{1,0:T(2,128)}, u32[]{:S(2)}) copy-start(f32[2,768]{1,0:T(2,128)} %get-tuple-element.20) | copy-start | bytes 18436
  201.1 173.7 %copy-start.2 = (f32[2,128,384]{2,1,0:T(8,128)S(1)}, f32[2,128,384]{2,1,0:T(8,128)}, u32[]{:S(2)}) copy-start(f32[2,128,384]{2,1,0:T(8,128)} %get-tuple-element.18) | copy-start | bytes 1179652
  201.1 174.5 %copy-start.1 = (f32[2,128,384]{2,1,0:T(8,128)S(1)}, f32[2,128,384]{2,1,0:T(8,128)}, u32[]{:S(2)}) copy-start(f32[2,128,384]{2,1,0:T(8,128)} %get-tuple-element.19) | copy-start | bytes 1179652
  375.6 6.6 %slice-start.2 = ((s8[4718592]{0:T(1024)(128)(4,1)}), s8[4194304]{0:T(1024)(128)(4,1)S(1)}, s32[]{:S(2)}) async-start(s8[4718592]{0:T(1024)(128)(4,1)} %bitcast.43), calls=%async_computation.3 | async-start | bytes 8388608
  376.3 4.9 %copy-start = (f32[1,384,768]{2,1,0:T(8,128)S(1)}, f32[1,384,768]{2,1,0:T(8,128)}, u32[]{:S(2)}) copy-start(f32[1,384,768]{2,1,0:T(8,128)} %get-tuple-element.53) | copy-start | bytes 3538948
  376.3 5.9 %slice-start.3 = ((s8[4718592]{0:T(1024)(128)(4,1)}), s8[524288]{0:T(1024)(128)(4,1)S(1)}, s32[]{:S(2)}) async-start(s8[4718592]{0:T(1024)(128)(4,1)} %bitcast.43), calls=%async_computation.4 | async-start | bytes 1048576
  381.2 4.2 %slice-start = ((s8[4718592]{0:T(1024)(128)(4,1)}), s8[4194304]{0:T(1024)(128)(4,1)S(1)}, s32[]{:S(2)}) async-start(s8[4718592]{0:T(1024)(128)(4,1)} %bitcast.40), calls=%async_computation.1 | async-start | bytes 8388608
  382.2 3.5 slice-start.1
Sparse Core Ops, SparseCore 0:
  201.3 173.5 all-reduce.3

commit v2 on v1

--- a/solution.py
+++ b/solution.py
@@ -362,16 +362,8 @@
 
 
 def gelu_parts(values):
-    size = jnp.abs(values)
-    turn = 1.0 / (1.0 + 0.23164190 * size)
-    bell = jnp.exp(-0.5 * values * values)
-    poly = turn * (
-        0.127414796
-        + turn * (-0.142248368 + turn * (0.7107068705 + turn * (-0.7265760135 + turn * 0.5307027145)))
-    )
-    tail = poly * bell
-    share = jnp.where(values >= 0.0, 1.0 - tail, tail)
-    return (values * share, share + values * (0.3989422804 * bell))
+    share = 0.5 + 0.5 * lax.erf(values * 0.7071067811865476)
+    return (values * share, share + values * (0.3989422804014327 * jnp.exp(-0.5 * values * values)))
 
 
 def nn(left, right):
@@ -384,12 +376,6 @@
 
 def tn(left, right):
     return lax.dot_general(left, right, (((0,), (0,)), ((), ())), preferred_element_type=jnp.float32)
-
-
-def tn_exact(left, right):
-    return lax.dot_general(
-        left, right, (((0,), (0,)), ((), ())), preferred_element_type=jnp.float32, precision=highest
-    )
 
 
 def split_low(values):
@@ -409,11 +395,13 @@
     (
         tok_ref, cot_ref, seg_ref, pad_ref, routes_ref, dist_ref, gains_ref, qkvw_ref, outw_ref, relb_ref, wr_ref,
         up_ref, down_ref,
-        secout_ref, ingrad_ref, ggain_ref, gqkv_ref, gout_ref, gbias_ref, grouter_ref, gup_ref, gdown_ref,
+        secout_ref, ingrad_ref, ggain_ref, shared_ref, gbias_ref, grouter_ref, gup_ref, gdown_ref,
         upv, downv, xb, dyb, rr, place, bias_buf, probs_buf, no1, qkvb, mixed, att_send, att_recv, mid, ntb,
         gate_t, hit_t, score_sum, disp_x, xrows, disp_y, dyrows, hidden, dgelu, eo_send, eo_recv, eob, eoret, out_own, x_send,
         other, og, gg_send, gg_recv, pg, cg_send, cg_recv, cgb, cgret, mgrad, ag, mg, qkvg,
-        no_send, no_recv, ig_own, dy_send, guv, gdv, wsem, gsem, ss, rs,
+        no_send, no_recv, ig_own, dy_send, guv, gdv,
+        no_all, mix_all, qgt, qt_all, agt, agt_all, early_send, early_all, late_send, late_all, sums_send, sums_recv,
+        wsem, gsem, ss, rs,
     ) = refs
     bf = jnp.bfloat16
     f32 = jnp.float32
@@ -475,10 +463,42 @@
     sem_re = take(experts)
     sem_rc = take(experts)
     sem_gg = take(experts)
+    sem_agt = take(experts)
+    sem_qgt = take(experts)
+    sem_early = take(experts)
+    sem_late = take(experts)
+    sem_sums = take(1)
+    sem_noall = take(1)
+    sem_ring_no = take(2 * experts)
+    sem_ring_mix = take(2 * experts)
+    sem_ring_out = take(4 * experts)
     assert counter[0] == lay.sems
 
     def block(index, rows):
         return pl.ds(pl.multiple_of(index * rows, rows), rows)
+
+    place_y = lax.rem(d, 2)
+    place_z = d // 2
+    ring_at = place_z + place_y * (experts - 1 - 2 * place_z)
+
+    def ring_device(position):
+        p = lax.rem(position + 2 * experts, experts)
+        return 2 * p + (p // (experts // 2)) * (2 * experts - 1 - 4 * p)
+
+    def ring_gather(streams):
+        moved = []
+        for k in range(experts - 1):
+            for number, (view, direction, base) in enumerate(streams):
+                if k > 0:
+                    moved[(k - 1) * len(streams) + number].wait_recv()
+                held = view(ring_device(ring_at - direction * k))
+                copy = remote(held, held, base + k, (s, ring_device(ring_at + direction), t))
+                copy.start()
+                moved.append(copy)
+        for copy in moved[(experts - 2) * len(streams) :]:
+            copy.wait_recv()
+        for copy in moved:
+            copy.wait_send()
 
     load_up = pltpu.make_async_copy(up_ref, upv, wsem.at[0])
     load_down = pltpu.make_async_copy(down_ref, downv, wsem.at[1])
@@ -531,6 +551,26 @@
         for copy in out:
             copy.wait_send()
 
+    def other_experts():
+        for k in steps:
+            remote(routes_ref, rr.at[behind[k]], sem_routes + k, (s, ahead[k], t)).wait_recv()
+
+        def one(i, carry):
+            q = i // micro
+            m = i % micro
+            pair = rr[q, m]
+            first = pair[0:1, :] == d
+            mine = first | (pair[1:2, :] == d)
+            mine_f = jnp.broadcast_to(mine.astype(f32), (experts, length))
+            spots = jnp.where(mine_f > 0.0, nn(mine_f.astype(bf), before), -1.0)
+            where_slot = (slot_at == spots[0:1, :]).astype(f32).astype(bf)
+            partner = jnp.where(first, pair[1:2, :], pair[0:1, :])
+            partner_hot = (lanes8 == partner).astype(f32).astype(bf)
+            other[m, block(q, cap), :] = nt(where_slot, partner_hot)
+            return carry
+
+        lax.fori_loop(0, experts * micro, one, 0)
+
     @pl.when(s == 0)
     def _():
         xb[...] = tok_ref[...]
@@ -539,6 +579,7 @@
     def _():
         dyb[...] = cot_ref[t]
         dispatch(dyb[...], disp_y, dyrows, sem_ddy, sem_ddyf)
+        other_experts()
 
     dist_rows = (
         lax.broadcasted_iota(jnp.int32, (lay.buckets, length), 0) == dist_ref[...]
@@ -611,29 +652,20 @@
 
     load_up.wait()
     load_down.wait()
-    flat = micro * slots
     row_tile = lay.row_tile
-    col_tile = lay.col_tile
-    per_micro = slots // row_tile
-
-    def forward_tile(i, carry):
-        at = pl.ds(pl.multiple_of((i % (ffn // col_tile)) * col_tile, col_tile), col_tile)
-        j = i // (ffn // col_tile)
-        m = j // per_micro
-        rows = block(j % per_micro, row_tile)
-        value, slope = gelu_parts(nn(xrows[m, rows, :], upv[:, at]))
-        hidden[m, rows, at] = value.astype(bf)
-        dgelu[m, rows, at] = slope.astype(bf)
-        return carry
-
-    lax.fori_loop(0, (flat // row_tile) * (ffn // col_tile), forward_tile, 0)
-
-    eo_send[...] = nn(hidden[u], downv[...]).astype(bf)
-    eo_copy = remote(eo_send, eo_recv, sem_eo, sib)
-    eo_copy.start()
-    part_own = nn(hidden[t], downv[...])
-    eo_copy.wait()
-    eob[...] = (part_own + eo_recv[...].astype(f32)).astype(bf)
+    tiles = [(m, slice(r, r + row_tile)) for m in range(micro) for r in range(0, slots, row_tile)]
+    for m, rows in tiles:
+        value, slope = gelu_parts(nn(xrows[m, rows, :], upv[...]))
+        hidden[m, rows, :] = value.astype(bf)
+        dgelu[m, rows, :] = slope.astype(bf)
+
+    def expert_rows():
+        eo_send[...] = nn(hidden[u], downv[...]).astype(bf)
+        eo_copy = remote(eo_send, eo_recv, sem_eo, sib)
+        eo_copy.start()
+        part = nn(hidden[t], downv[...])
+        eo_copy.wait()
+        eob[...] = (part + eo_recv[...].astype(f32)).astype(bf)
 
     def send_back(source, landing, base):
         mine = block(d, cap)
@@ -673,35 +705,35 @@
         out_ref[t] = rows_ref[:, own_half()]
         copy.wait()
 
+    def gather_factors():
+        no_all[t, d] = no1[t]
+        mix_all[d] = jnp.concatenate([mixed[m] for m in range(micro)], axis=0)
+        ring_gather(
+            [
+                (lambda q: no_all.at[t, q, 0 : length // 2], 1, sem_ring_no),
+                (lambda q: no_all.at[t, q, length // 2 : length], -1, sem_ring_no + experts),
+                (lambda q: mix_all.at[q, 0:length], 1, sem_ring_mix),
+                (lambda q: mix_all.at[q, length : 2 * length], -1, sem_ring_mix + experts),
+            ]
+        )
+        copy = remote(no_all.at[t], no_all.at[t], sem_noall, sib)
+        copy.start()
+        copy.wait()
+
     @pl.when(s == 0)
     def _():
+        expert_rows()
         finish(send_back(eob, eoret, sem_re))
         x_send[...] = layer_output().astype(bf)
         copy = remote(x_send, xb.at[t], sem_x, across)
         copy.start()
         hand_out(out_own, secout_ref, sem_so)
         copy.wait_send()
+        other_experts()
+        gather_factors()
         remote(dy_send, dyb, sem_dy, across).wait_recv()
         dispatch(dyb[...], disp_y, dyrows, sem_ddy, sem_ddyf)
 
-    for k in steps:
-        remote(routes_ref, rr.at[behind[k]], sem_routes + k, (s, ahead[k], t)).wait_recv()
-
-    def other_experts(i, carry):
-        q = i // micro
-        m = i % micro
-        pair = rr[q, m]
-        first = pair[0:1, :] == d
-        mine = first | (pair[1:2, :] == d)
-        mine_f = jnp.broadcast_to(mine.astype(f32), (experts, length))
-        spots = jnp.where(mine_f > 0.0, nn(mine_f.astype(bf), before), -1.0)
-        where_slot = (slot_at == spots[0:1, :]).astype(f32).astype(bf)
-        partner = jnp.where(first, pair[1:2, :], pair[0:1, :])
-        partner_hot = (lanes8 == partner).astype(f32).astype(bf)
-        other[m, block(q, cap), :] = nt(where_slot, partner_hot)
-        return carry
-
-    lax.fori_loop(0, experts * micro, other_experts, 0)
     mine_hot = (lax.broadcasted_iota(jnp.int32, (slots, experts), 1) == d).astype(f32)
     for m in range(micro):
         slot_logits = nt(xrows[m], wr_ref[...])
@@ -710,34 +742,34 @@
         gate = 1.0 / (1.0 + jnp.exp(other_logit - own_logit))
         og[m] = (dyrows[m].astype(f32) * gate).astype(bf)
 
-    gg_send[...] = jnp.zeros_like(gg_send)
-    ones = jnp.ones((8, width), bf)
-    for q in range(experts):
-        at = slice(q * cap, (q + 1) * cap)
-        high, low = split_low(dyrows[t, at, :].astype(f32) * eob[at, :].astype(f32))
-        gg_send[q, :, 0:cap] = nt(ones, high) + nt(ones, low)
-
-    def backward_tile(i, carry):
-        at = pl.ds(pl.multiple_of((i % (ffn // col_tile)) * col_tile, col_tile), col_tile)
-        j = i // (ffn // col_tile)
-        m = j // per_micro
-        rows = block(j % per_micro, row_tile)
-        grad = nt(og[m, rows, :], downv[at, :])
-        pg[m, rows, at] = (grad * dgelu[m, rows, at].astype(f32)).astype(bf)
-        return carry
-
-    lax.fori_loop(0, (flat // row_tile) * (ffn // col_tile), backward_tile, 0)
+    for m, rows in tiles:
+        pg[m, rows, :] = (nt(og[m, rows, :], downv[...]) * dgelu[m, rows, :].astype(f32)).astype(bf)
     cg_send[...] = nt(pg[u], upv[...]).astype(bf)
     cg_copy = remote(cg_send, cg_recv, sem_cg, sib)
     cg_copy.start()
-    gg_out = [remote(gg_send.at[ahead[k]], gg_recv.at[d], sem_gg + k, (s, ahead[k], t)) for k in steps]
-    for copy in gg_out:
-        copy.start()
-    gg_recv[d] = gg_send[d]
     part_own = nt(pg[t], upv[...])
     cg_copy.wait()
     cgb[...] = (part_own + cg_recv[...].astype(f32)).astype(bf)
     cg_out = send_back(cgb, cgret, sem_rc)
+
+    @pl.when(s == 1)
+    def _():
+        expert_rows()
+
+    def send_gate_grads():
+        gg_send[...] = jnp.zeros_like(gg_send)
+        ones = jnp.ones((8, width), bf)
+        for q in range(experts):
+            at = slice(q * cap, (q + 1) * cap)
+            high, low = split_low(dyrows[t, at, :].astype(f32) * eob[at, :].astype(f32))
+            gg_send[q, :, 0:cap] = nt(ones, high) + nt(ones, low)
+        out = [remote(gg_send.at[ahead[k]], gg_recv.at[d], sem_gg + k, (s, ahead[k], t)) for k in steps]
+        for copy in out:
+            copy.start()
+        gg_recv[d] = gg_send[d]
+        return out
+
+    gg_out = send_gate_grads()
 
     wide = lay.wide
     for n in range(ffn // wide):
@@ -763,24 +795,45 @@
     gate_grad = jnp.concatenate(gg_rows, axis=0)
     gates = gate_t[...]
     logit_grad = (gates * (gate_grad - jnp.sum(gates * gate_grad, axis=0, keepdims=True))).astype(bf)
-    grouter_ref[...] = nn(logit_grad, ntb[...])
+    early_send[0:experts, :] = nn(logit_grad, ntb[...]).astype(bf)
     two_grad = tn(logit_grad, wr_ref[...]) + tn(place[...], cgret[...])
     dy = dyb[...].astype(f32)
     middle = mid[...]
     scale = inverse_rms(middle)
     normed = middle * scale
-    ggain_ref[1:2, :] = jnp.sum(two_grad * normed, axis=0, keepdims=True)
+    early_send[experts : 2 * experts, :] = jnp.broadcast_to(
+        jnp.sum(two_grad * normed, axis=0, keepdims=True), (experts, width)
+    ).astype(bf)
     scaled = two_grad * gain_two
     middle_grad = dy + scale * (scaled - normed * jnp.mean(scaled * normed, axis=-1, keepdims=True))
     mgrad[...] = middle_grad
     ag[t] = middle_grad.astype(bf)
     ag_copy = remote(ag.at[t], ag.at[t], sem_ag, sib)
     ag_copy.start()
+
+    def to_all(source, landing, base):
+        out = [remote(source, landing.at[d], base + k, (s, ahead[k], t)) for k in steps]
+        for copy in out:
+            copy.start()
+        landing[d] = source[...]
+        return out
+
+    early_out = to_all(early_send, early_all, sem_early)
     ag_copy.wait()
+
+    def spread(source, landing, rows, base):
+        out = [remote(source.at[block(ahead[k], rows)], landing.at[d], base + k, (s, ahead[k], t)) for k in steps]
+        for copy in out:
+            copy.start()
+        landing[d] = source[block(d, rows), :]
+        return out
+
+    for m in range(micro):
+        agt[:, m * length : (m + 1) * length] = jnp.transpose(ag[m])
+    agt_out = spread(agt, agt_all, width // experts, sem_agt)
 
     for m in range(micro):
         mg[m] = nt(ag[m], outw_ref[...]).astype(bf)
-    gout_ref[...] = tn(mixed[0], ag[0]) + tn(mixed[1], ag[1])
     for m in range(micro):
         for p in range(pairs):
             at = slice(p * 128, (p + 1) * 128)
@@ -803,9 +856,13 @@
                 raws.append(raw)
                 key_grad = key_grad + tn(raw, queries2[h * length : (h + 1) * length])
                 value_grad = value_grad + tn(part.astype(bf), mg2[h * length : (h + 1) * length])
-            qkvg[0, m, :, at] = nn(jnp.concatenate(raws, axis=1), keys2).astype(bf)
-            qkvg[1, m, :, at] = key_grad.astype(bf)
-            qkvg[2, m, :, at] = value_grad.astype(bf)
+            query_grad = nn(jnp.concatenate(raws, axis=1), keys2)
+            for c, grad in enumerate((query_grad, key_grad, value_grad)):
+                qkvg[c, m, :, at] = grad.astype(bf)
+                qgt[c * cols + p * 128 : c * cols + (p + 1) * 128, m * length : (m + 1) * length] = jnp.transpose(
+                    grad
+                ).astype(bf)
+    qgt_out = spread(qgt, qt_all, 3 * cols // experts, sem_qgt)
     def project_back(m):
         total = nt(qkvg[0, m], qkvw_ref[0])
         for c in range(1, 3):
@@ -821,7 +878,7 @@
     x_rows = xb[t].astype(f32)
     scale = inverse_rms(x_rows)
     normed = x_rows * scale
-    ggain_ref[0:1, :] = jnp.sum(one_grad * normed, axis=0, keepdims=True)
+    gain_one_grad = jnp.sum(one_grad * normed, axis=0, keepdims=True)
     scaled = one_grad * gain_one
     input_grad = mgrad[...] + scale * (scaled - normed * jnp.mean(scaled * normed, axis=-1, keepdims=True))
     ig_own[...] = input_grad
@@ -835,16 +892,57 @@
 
     hand_out(ig_own, ingrad_ref, sem_ig)
 
-    for c in range(3):
-        gqkv_ref[c] = tn(no1[0], qkvg[c, 0]) + tn(no1[1], qkvg[c, 1])
-
     sums = []
     for head in range(2 * pairs):
         high, low = split_low(score_sum[head])
         turned = pltpu.roll(nn(high, mirror) + nn(low, mirror), 0, 1, stride=1, stride_axis=0)
         sums.append(jnp.sum(turned, axis=0, keepdims=True))
     high, low = split_low(jnp.concatenate(sums, axis=0))
-    gbias_ref[...] = nt(high, dist_rows) + nt(low, dist_rows)
+    late_send[...] = jnp.zeros_like(late_send)
+    late_send[0 : 2 * pairs, 0 : lay.buckets] = nt(high, dist_rows) + nt(low, dist_rows)
+    late_send[7:8, :] = gain_one_grad
+    late_out = to_all(late_send, late_all, sem_late)
+
+    @pl.when(s == 1)
+    def _():
+        gather_factors()
+
+    finish(agt_out)
+    total = nn(agt_all[0], mix_all[0])
+    for q in range(1, experts):
+        total = total + nn(agt_all[q], mix_all[q])
+    qkv_rows = 3 * cols // experts
+    out_rows = width // experts
+    shared_ref[d, qkv_rows:, 0:cols] = total[0 : out_rows // 2].astype(bf)
+    shared_ref[d, qkv_rows:, cols:] = total[out_rows // 2 :].astype(bf)
+    finish(qgt_out)
+    total = jnp.zeros((qkv_rows, width), f32)
+    for q in range(experts):
+        total = total + nn(qt_all[q], jnp.concatenate([no_all[0, q], no_all[1, q]], axis=0))
+    shared_ref[d, 0:qkv_rows, :] = total.astype(bf)
+    share = shared_ref.shape[1] // 4
+    ring_gather(
+        [
+            (lambda q, c=c: shared_ref.at[q, c * share : (c + 1) * share], 1 if c < 2 else -1, sem_ring_out + c * experts)
+            for c in range(4)
+        ]
+    )
+    finish(early_out)
+    finish(late_out)
+    early_sum = early_all[0].astype(f32)
+    late_sum = late_all[0]
+    for q in range(1, experts):
+        early_sum = early_sum + early_all[q].astype(f32)
+        late_sum = late_sum + late_all[q]
+    gbias_ref[...] = late_sum[0 : 2 * pairs, 0 : lay.buckets]
+    sums_send[0 : 2 * experts, :] = early_sum
+    sums_send[2 * experts :, :] = late_sum
+    sums_copy = remote(sums_send, sums_recv, sem_sums, sib)
+    sums_copy.start()
+    sums_copy.wait()
+    grouter_ref[...] = sums_send[0:experts, :] + sums_recv[0:experts, :]
+    ggain_ref[0:1, :] = sums_send[2 * experts + 7 :, :] + sums_recv[2 * experts + 7 :, :]
+    ggain_ref[1:2, :] = sums_send[experts : experts + 1, :] + sums_recv[experts : experts + 1, :]
 
     @pl.when(s == 1)
     def _():
@@ -888,9 +986,8 @@
     lay.cap = cap
     lay.buckets = rel_bias.shape[1]
     lay.row_tile = min(slots, 192)
-    lay.col_tile = min(ffn, 256)
     lay.wide = min(ffn, 256)
-    lay.sems = 8 * experts + 10
+    lay.sems = 20 * experts + 12
     bf = jnp.bfloat16
     f32 = jnp.float32
     vm = pltpu.VMEM
@@ -946,6 +1043,18 @@
         vm((length, width), bf),
         vm((width, ffn), f32),
         vm((ffn, width), f32),
+        vm((micro, experts, length, width), bf),
+        vm((experts, micro * length, cols), bf),
+        vm((3 * cols, micro * length), bf),
+        vm((experts, 3 * cols // experts, micro * length), bf),
+        vm((width, micro * length), bf),
+        vm((experts, width // experts, micro * length), bf),
+        vm((2 * experts, width), bf),
+        vm((experts, 2 * experts, width), bf),
+        vm((8, width), f32),
+        vm((experts, 8, width), f32),
+        vm((2 * experts + 8, width), f32),
+        vm((2 * experts + 8, width), f32),
         dma((2,)),
         dma((2 * (ffn // lay.wide),)),
         dma((lay.sems,)),
@@ -953,12 +1062,12 @@
     ]
     whole = pl.BlockSpec(memory_space=pltpu.VMEM)
     anywhere = pl.BlockSpec(memory_space=pl.ANY)
+    shared_rows = 3 * cols // experts + width // experts // 2
     out_shape = (
         shape((micro, length, width // 2), f32),
         shape((micro, length, width // 2), f32),
         shape((2, width), f32),
-        shape((3, width, cols), f32),
-        shape((cols, width), f32),
+        shape((experts, shared_rows, width), bf),
         shape((heads, lay.buckets), f32),
         shape((experts, width), f32),
         shape((width, ffn), f32),
@@ -968,7 +1077,7 @@
         partial(layer_kernel, lay),
         out_shape=out_shape,
         in_specs=[whole] * 11 + [anywhere] * 2,
-        out_specs=[whole] * 7 + [anywhere] * 2,
+        out_specs=[whole] * 6 + [anywhere] * 2,
         scratch_shapes=scratch,
         name="two_sections",
         compiler_params=pltpu.CompilerParams(
@@ -989,15 +1098,16 @@
         expert_up[0, 0],
         expert_down[0, 0],
     )
-    section_out, input_grads, gains, qkv, out, bias, router, up, down = results
-    qkv, out, bias = lax.psum((qkv, out, bias), "dp")
-    gains, router = lax.psum((gains, router), ("dp", "tensor"))
+    section_out, input_grads, gains, shared, bias, router, up, down = results
+    qkv_rows = 3 * cols // experts
+    qkv = shared[:, :qkv_rows].reshape(3, cols, width).astype(f32)
+    out = shared[:, qkv_rows:].reshape(experts, -1, 2, cols).transpose(0, 2, 1, 3).reshape(width, cols).astype(f32)
     return (
         section_out[None, :, None],
         input_grads[None, :, None],
         gains[None],
-        qkv.transpose(1, 0, 2)[None],
-        out[None],
+        qkv.transpose(2, 0, 1)[None],
+        out.T[None],
         bias.T[None],
         router.T[None],
         up[None, None],

time: 395 us -> 238 us (0.60)
  blocking collectives: 87.1 us -> 0 us
  waiting for transfers between devices: 85.4 us -> 0 us
  Pallas kernels: 194 us -> 219 us
  between operations: 14.1 us -> 0.69 us
    psum x2 -> x0, blocking collectives: 87.1 us -> none  [the longest x1 61.8 us: fused_local(): gains, router = lax.psum((gains, router), ('dp', 'tensor'))]
    psum x1 -> x0, waiting for transfers between devices: 85.4 us -> none  [fused_local(): qkv, out, bias = lax.psum((qkv, out, bias), 'dp')]
    pallas_call x1, Pallas kernels: 194 us -> 219 us  [fused_local(): pl.pallas_call(partial(layer_kernel, lay), out_shape=out_shape, in_specs=...]
    unnamed x27 -> x20, local copies, waits for them, and re-layouts: 14.3 us -> 12.7 us
  transfers between devices with their start and end apart: 1 -> 0, of which waited for: 1 -> 0; matrix products, arithmetic and copies ran while one was open for 0% -> 0% of each run, Pallas kernels for 0% -> 0%
where the time goes in v2:
time: 238 us
  Pallas kernels  219 us (92%)
  local copies, waits for them, and re-layouts  17 us (7%)
    pallas_call x1, Pallas kernels, fused_local(): pl.pallas_call(partial(layer_kernel, lay), out_shape=out_shape, in_specs=...  219 us
    unnamed x20, local copies, waits for them, and re-layouts  12.7 us

profile of v2, /device:TPU:0, one launch (start us, length us, event | category | flops | bytes accessed | tf_op | source)
XLA Modules:
  0.0 237.8 jit_solution(16445777351810203692)
XLA Ops:
  0.6 219.0 %two_sections.1 = (f32[2,128,384]{2,1,0:T(8,128)}, f32[2,128,384]{2,1,0:T(8,128)}, f32[2,768]{1,0:T(2,128)}, bf16[8,192,768]{2,1,0:T(8,128)(2,1)}, f32[6,32]{1,0...) custom-call(bf16[2,128,768]{2,1,0:T(8,128)(2,1)} %bitcast.64, ...), custom_call_target="tpu_custom_call" | custom-call | tf_op jit(solution)/shard_map/two_sections/pallas_call | solution.py:1076
  219.6 1.2 copy.32
  220.9 1.2 slice_convert_fusion
  222.0 1.6 slice.6
  223.6 0.1 copy.35
  223.7 1.4 copy.31
  225.1 0.0 copy-start.1
  225.1 0.0 copy-start
  225.1 0.0 copy-start.3
  225.1 0.0 copy-start.2
  225.1 2.6 %copy.27 = f32[3,384,768]{1,2,0:T(8,128)} copy(bf16[3,384,768]{2,1,0:T(8,128)(2,1)S(1)} %bitcast.52) | data formatting | bytes 5308416 | tf_op jit(solution)/shard_map/broadcast_in_dim | solution.py:1109
  227.7 0.0 copy-done.1
  227.7 0.7 copy.42
  228.5 0.0 copy-done
  228.5 0.7 copy.43
  229.2 0.0 copy-done.3
  229.2 0.6 copy.44
  229.8 0.0 copy-done.2
  229.8 0.0 slice-start
  229.8 0.6 copy.45
  230.4 0.0 slice-start.1
  230.4 5.1 %copy.46 = f32[1,1,768,1536]{3,2,1,0:T(8,128)} copy(f32[1,1,768,1536]{3,2,1,0:T(8,128)} %bitcast.56) | data formatting | bytes 9437184
  235.6 0.0 slice-done
  235.6 0.0 slice-done.1
  235.6 2.2 copy.47
  (1 shorter events, 0.0 us)
Async XLA Ops:
  225.1 2.6 %copy-start.1 = (f32[2,128,384]{2,1,0:T(8,128)S(1)}, f32[2,128,384]{2,1,0:T(8,128)}, u32[]{:S(2)}) copy-start(f32[2,128,384]{2,1,0:T(8,128)} %get-tuple-element.17) | copy-start | bytes 1179652
  225.1 3.4 %copy-start = (f32[2,128,384]{2,1,0:T(8,128)S(1)}, f32[2,128,384]{2,1,0:T(8,128)}, u32[]{:S(2)}) copy-start(f32[2,128,384]{2,1,0:T(8,128)} %get-tuple-element.18) | copy-start | bytes 1179652
  225.1 4.1 %copy-start.3 = (f32[2,768]{1,0:T(2,128)S(1)}, f32[2,768]{1,0:T(2,128)}, u32[]{:S(2)}) copy-start(f32[2,768]{1,0:T(2,128)} %get-tuple-element.19) | copy-start | bytes 18436
  225.1 4.7 %copy-start.2 = (f32[8,768]{1,0:T(8,128)S(1)}, f32[8,768]{1,0:T(8,128)}, u32[]{:S(2)}) copy-start(f32[8,768]{1,0:T(8,128)} %get-tuple-element.22) | copy-start | bytes 73732
  229.8 5.8 %slice-start = ((s8[4718592]{0:T(1024)(128)(4,1)}), s8[4194304]{0:T(1024)(128)(4,1)S(1)}, s32[]{:S(2)}) async-start(s8[4718592]{0:T(1024)(128)(4,1)} %bitcast.53), calls=%async_computation | async-start | bytes 8388608
  230.4 5.2 %slice-start.1 = ((s8[4718592]{0:T(1024)(128)(4,1)}), s8[524288]{0:T(1024)(128)(4,1)S(1)}, s32[]{:S(2)}) async-start(s8[4718592]{0:T(1024)(128)(4,1)} %bitcast.53), calls=%async_computation.1 | async-start | bytes 1048576

commit v3 on v2

--- a/solution.py
+++ b/solution.py
@@ -393,14 +393,15 @@
 
 def layer_kernel(lay, *refs):
     (
-        tok_ref, cot_ref, seg_ref, pad_ref, routes_ref, dist_ref, gains_ref, qkvw_ref, outw_ref, relb_ref, wr_ref,
+        tok_ref, cot_ref, seg_ref, pad_ref, routes_ref, dist_ref, gains_ref, qkvw_hbm, outw_hbm, relb_ref, wr_ref,
         up_ref, down_ref,
         secout_ref, ingrad_ref, ggain_ref, shared_ref, gbias_ref, grouter_ref, gup_ref, gdown_ref,
-        upv, downv, xb, dyb, rr, place, bias_buf, probs_buf, no1, qkvb, mixed, att_send, att_recv, mid, ntb,
-        gate_t, hit_t, score_sum, disp_x, xrows, disp_y, dyrows, hidden, dgelu, eo_send, eo_recv, eob, eoret, out_own, x_send,
+        upv, downv, qkvw_ref, outw_ref, xb, dyb, rr, place, bias_buf, probs_buf, no1, qkvb, mixed, att_send, att_recv, mid, ntb,
+        gate_t, hit_t, wrp, score_sum, disp_x, xrows, disp_y, dyrows, hidden, dgelu, halves, eo_send, eo_recv, eob, eoret, out_own,
+        x_send,
         other, og, gg_send, gg_recv, pg, cg_send, cg_recv, cgb, cgret, mgrad, ag, mg, qkvg,
         no_send, no_recv, ig_own, dy_send, guv, gdv,
-        no_all, mix_all, qgt, qt_all, agt, agt_all, early_send, early_all, late_send, late_all, sums_send, sums_recv,
+        no_all, mix_all, qgt, qt_all, agt, agt_all, small_send, small_in, small_all, small_sib,
         wsem, gsem, ss, rs,
     ) = refs
     bf = jnp.bfloat16
@@ -419,9 +420,18 @@
     u = 1 - t
     sib = (s, d, u)
     across = (1 - s, d, t)
+    bits = [lax.rem(d // bit, 2) for bit in (1, 2, 4)]
+
+    def partner(flip):
+        index = d
+        for place, bit in enumerate((1, 2, 4)):
+            if flip & bit:
+                index = index + bit - 2 * bit * bits[place]
+        return index
+
+    peer = [partner(flip) for flip in (0, 4, 1, 6, 2, 5, 3, 7)]
     steps = range(1, experts)
-    ahead = [lax.rem(d + k, experts) for k in range(experts)]
-    behind = [lax.rem(d + experts - k, experts) for k in range(experts)]
+    chunks = [slice(c, c + 2) for c in range(0, experts, 2)]
 
     def remote(src, dst, index, device):
         return pltpu.make_async_remote_copy(
@@ -450,8 +460,8 @@
     sem_xf = take(1)
     sem_dy = take(1)
     sem_att = take(1)
-    sem_eo = take(1)
-    sem_cg = take(1)
+    sem_eo = take(experts)
+    sem_cg = take(experts)
     sem_ag = take(1)
     sem_no = take(1)
     sem_so = take(1)
@@ -464,14 +474,15 @@
     sem_rc = take(experts)
     sem_gg = take(experts)
     sem_agt = take(experts)
+    sem_agtf = take(experts)
     sem_qgt = take(experts)
-    sem_early = take(experts)
-    sem_late = take(experts)
+    sem_small = take(experts)
+    sem_back = take(experts)
     sem_sums = take(1)
     sem_noall = take(1)
     sem_ring_no = take(2 * experts)
     sem_ring_mix = take(2 * experts)
-    sem_ring_out = take(4 * experts)
+    sem_ring_out = take(6 * experts)
     assert counter[0] == lay.sems
 
     def block(index, rows):
@@ -485,9 +496,11 @@
         p = lax.rem(position + 2 * experts, experts)
         return 2 * p + (p // (experts // 2)) * (2 * experts - 1 - 4 * p)
 
-    def ring_gather(streams):
+    def ring_gather(streams, at_half=None):
         moved = []
         for k in range(experts - 1):
+            if k == experts // 2 and at_half is not None:
+                at_half()
             for number, (view, direction, base) in enumerate(streams):
                 if k > 0:
                     moved[(k - 1) * len(streams) + number].wait_recv()
@@ -502,19 +515,34 @@
 
     load_up = pltpu.make_async_copy(up_ref, upv, wsem.at[0])
     load_down = pltpu.make_async_copy(down_ref, downv, wsem.at[1])
+    load_qkvw = pltpu.make_async_copy(qkvw_hbm, qkvw_ref, wsem.at[2])
+    load_outw = pltpu.make_async_copy(outw_hbm, outw_ref, wsem.at[3])
+    load_tok = pltpu.make_async_copy(tok_ref, xb, wsem.at[4])
+    load_cot = pltpu.make_async_copy(cot_ref.at[t], dyb, wsem.at[4])
+
+    @pl.when(s == 0)
+    def _():
+        load_tok.start()
+
+    @pl.when(s == 1)
+    def _():
+        load_cot.start()
+
+    load_qkvw.start()
+    load_outw.start()
     load_up.start()
     load_down.start()
 
     barrier = pltpu.get_barrier_semaphore()
     for k in steps:
-        pl.semaphore_signal(barrier, inc=1, device_id=(s, ahead[k], t), device_id_type=pl.DeviceIdType.MESH)
+        pl.semaphore_signal(barrier, inc=1, device_id=(s, peer[k], t), device_id_type=pl.DeviceIdType.MESH)
     pl.semaphore_signal(barrier, inc=1, device_id=sib, device_id_type=pl.DeviceIdType.MESH)
     pl.semaphore_signal(barrier, inc=1, device_id=across, device_id_type=pl.DeviceIdType.MESH)
     pl.semaphore_wait(barrier, experts + 1)
 
     for k in steps:
-        fire(remote(routes_ref, rr.at[d], sem_routes + k, (s, ahead[k], t)))
-    rr[d] = routes_ref[...]
+        fire(remote(routes_ref, rr.at[k], sem_routes + k, (s, peer[k], t)))
+    rr[0] = routes_ref[...]
 
     lanes8 = lax.broadcasted_iota(jnp.int32, (experts, length), 0)
     row_at = lax.broadcasted_iota(jnp.int32, (length, length), 0)
@@ -522,8 +550,13 @@
     before = (row_at < col_at).astype(bf)
     slot_at = lax.broadcasted_iota(jnp.int32, (cap, length), 0).astype(f32)
 
+    expert_of = jnp.zeros((experts, length), jnp.int32)
+    for k in range(experts):
+        expert_of = jnp.where(lanes8 == k, peer[k], expert_of)
+    turn = (lax.broadcasted_iota(jnp.int32, (experts, experts), 1) == expert_of[:, 0:experts]).astype(f32).astype(bf)
+    wrp[...] = nn(turn, wr_ref[...]).astype(bf)
     own_routes = routes_ref[t]
-    hits = (lanes8 == own_routes[0:1, :]) | (lanes8 == own_routes[1:2, :])
+    hits = (expert_of == own_routes[0:1, :]) | (expert_of == own_routes[1:2, :])
     hit_f = hits.astype(f32)
     hit_t[...] = hit_f
     spot = jnp.where(hits, nn(hit_f.astype(bf), before), -1.0)
@@ -531,29 +564,60 @@
         place[e * cap : (e + 1) * cap, :] = (slot_at == spot[e : e + 1, :]).astype(f32).astype(bf)
 
     def dispatch(rows, send, landing, base, base_fwd):
-        send[...] = nn(place[...], rows).astype(bf)
-        mine = block(d, cap)
-        out = [remote(send.at[block(ahead[k], cap)], landing.at[t, mine], base + k, (s, ahead[k], t)) for k in steps]
+        send[...] = nn(place[...], rows).astype(bf).reshape(send.shape)
+        out = [remote(send.at[k], landing.at[k, t], base + k, (s, peer[k], t)) for k in steps]
         for copy in out:
             copy.start()
-        first = remote(send.at[mine], landing.at[t, mine], base_fwd, sib)
+        first = remote(send.at[0], landing.at[0, t], base_fwd, sib)
         first.start()
-        landing[t, mine, :] = send[mine, :]
-        passed = [first]
-        for k in steps:
-            out[k - 1].wait_recv()
-            from_block = block(behind[k], cap)
-            copy = remote(landing.at[t, from_block], landing.at[t, from_block], base_fwd + k, sib)
-            copy.start()
-            passed.append(copy)
-        for copy in passed:
-            copy.wait()
-        for copy in out:
-            copy.wait_send()
+        landing[0, t] = send[0]
+
+        def steps_of():
+            passed = [first]
+
+            def arrive(c):
+                for k in (2 * c, 2 * c + 1):
+                    if k > 0:
+                        out[k - 1].wait_recv()
+                        copy = remote(landing.at[k, t], landing.at[k, t], base_fwd + k, sib)
+                        copy.start()
+                        passed.append(copy)
+
+            def joined(c):
+                for k in (2 * c, 2 * c + 1):
+                    passed[k].wait_recv()
+
+            def drain():
+                for copy in out + passed:
+                    copy.wait_send()
+
+            return arrive, joined, drain
+
+        return steps_of
+
+    def stream(dispatched, first, second, finish_chunk, eager):
+        arrive, joined, drain = dispatched()
+        last = len(chunks) - 1
+        arrive(0)
+        joined(0)
+        for c in range(len(chunks)):
+            first(c)
+            if eager and c > 0:
+                finish_chunk(c - 1)
+            if eager and c < last:
+                arrive(c + 1)
+            second(c)
+            if not eager and c < last:
+                arrive(c + 1)
+                finish_chunk(c)
+            if c < last:
+                joined(c + 1)
+        finish_chunk(last)
+        drain()
 
     def other_experts():
         for k in steps:
-            remote(routes_ref, rr.at[behind[k]], sem_routes + k, (s, ahead[k], t)).wait_recv()
+            remote(routes_ref, rr.at[k], sem_routes + k, (s, peer[k], t)).wait_recv()
 
         def one(i, carry):
             q = i // micro
@@ -566,19 +630,24 @@
             where_slot = (slot_at == spots[0:1, :]).astype(f32).astype(bf)
             partner = jnp.where(first, pair[1:2, :], pair[0:1, :])
             partner_hot = (lanes8 == partner).astype(f32).astype(bf)
-            other[m, block(q, cap), :] = nt(where_slot, partner_hot)
+            other[q, m] = nt(where_slot, partner_hot)
             return carry
 
         lax.fori_loop(0, experts * micro, one, 0)
 
     @pl.when(s == 0)
     def _():
-        xb[...] = tok_ref[...]
+        load_tok.wait()
 
     @pl.when(s == 1)
     def _():
-        dyb[...] = cot_ref[t]
-        dispatch(dyb[...], disp_y, dyrows, sem_ddy, sem_ddyf)
+        load_cot.wait()
+        arrive, joined, drain = dispatch(dyb[...], disp_y, dyrows, sem_ddy, sem_ddyf)()
+        for c in range(len(chunks)):
+            arrive(c)
+        for c in range(len(chunks)):
+            joined(c)
+        drain()
         other_experts()
 
     dist_rows = (
@@ -600,13 +669,17 @@
                 )
                 bias_buf[m, p, :, h * length : (h + 1) * length] = jnp.where(allowed, grid, masked_score)
 
+    x_copy = remote(x_send, xb.at[t], sem_x, across)
+    dy_copy = remote(dy_send, dyb, sem_dy, across)
+    x_forward = remote(xb.at[t], xb.at[t], sem_xf, sib)
+
     @pl.when(s == 1)
     def _():
-        remote(x_send, xb.at[t], sem_x, across).wait_recv()
-        copy = remote(xb.at[t], xb.at[t], sem_xf, sib)
-        copy.start()
-        copy.wait()
-
+        x_copy.wait_recv()
+        x_forward.start()
+
+    load_qkvw.wait()
+    load_outw.wait()
     gain_one = gains_ref[0:1, :].astype(f32)
     gain_two = gains_ref[1:2, :].astype(f32)
     low_lanes = lax.broadcasted_iota(jnp.int32, (length, 128), 1) < 64
@@ -617,14 +690,11 @@
             [jnp.where(low_lanes, pair_block, zero), jnp.where(low_lanes, zero, pair_block)], axis=0
         )
 
-    for m in range(micro):
+    def attend(m):
         x_rows = xb[m].astype(f32)
         no1[m] = (x_rows * inverse_rms(x_rows) * gain_one).astype(bf)
-    for c in range(3):
-        w = qkvw_ref[c]
-        for m in range(micro):
-            qkvb[c, m] = nn(no1[m], w).astype(bf)
-    for m in range(micro):
+        for c in range(3):
+            qkvb[c, m] = nn(no1[m], qkvw_ref[c]).astype(bf)
         for p in range(pairs):
             at = slice(p * 128, (p + 1) * 128)
             scores = 0.125 * nt(qkvb[0, m, :, at], both_heads(qkvb[1, m, :, at])) + bias_buf[m, p]
@@ -636,44 +706,113 @@
                 )
             mixed[m, :, at] = nn(probs_buf[m, p].astype(bf), both_heads(qkvb[2, m, :, at])).astype(bf)
 
-    att_send[...] = nn(mixed[u], outw_ref[...])
     att_copy = remote(att_send, att_recv, sem_att, sib)
-    att_copy.start()
+
+    def project_other():
+        att_send[...] = nn(mixed[u], outw_ref[...])
+        att_copy.start()
+
+    begin = u + s * (t - u)
+    attend(begin)
+
+    @pl.when(s == 0)
+    def _():
+        project_other()
+
+    @pl.when(s == 1)
+    def _():
+        x_forward.wait()
+
+    attend(1 - begin)
+
+    @pl.when(s == 1)
+    def _():
+        project_other()
+
     part_own = nn(mixed[t], outw_ref[...])
     att_copy.wait()
     middle = xb[t].astype(f32) + part_own + att_recv[...]
     mid[...] = middle
     ntb[...] = (middle * inverse_rms(middle) * gain_two).astype(bf)
-    logits_t = jnp.where(hit_t[...] > 0.0, nt(wr_ref[...], ntb[...]), masked_score)
+    logits_t = jnp.where(hit_t[...] > 0.0, nt(wrp[...], ntb[...]), masked_score)
     terms = jnp.exp(logits_t - jnp.max(logits_t, axis=0, keepdims=True))
     gate_t[...] = terms / jnp.sum(terms, axis=0, keepdims=True)
 
-    dispatch(ntb[...], disp_x, xrows, sem_dx, sem_dxf)
-
+    arrivals = dispatch(ntb[...], disp_x, xrows, sem_dx, sem_dxf)
     load_up.wait()
     load_down.wait()
-    row_tile = lay.row_tile
-    tiles = [(m, slice(r, r + row_tile)) for m in range(micro) for r in range(0, slots, row_tile)]
-    for m, rows in tiles:
-        value, slope = gelu_parts(nn(xrows[m, rows, :], upv[...]))
-        hidden[m, rows, :] = value.astype(bf)
-        dgelu[m, rows, :] = slope.astype(bf)
+    rows_of = 2 * micro * cap
+
+    def flat(ref, chunk):
+        return ref[chunk].reshape(rows_of, ref.shape[-1])
+
+    def front_chunk(c):
+        value, slope = gelu_parts(nn(flat(xrows, chunks[c]), upv[...]))
+        hidden[chunks[c]] = value.astype(bf).reshape(2, micro, cap, ffn)
+        dgelu[chunks[c]] = slope.astype(bf).reshape(2, micro, cap, ffn)
+
+    def split_sum(c, total, send, recv, base):
+        for m in range(micro):
+            halves[m] = total.reshape(2, micro, cap, width)[:, m]
+        send[chunks[c]] = halves[u].astype(bf)
+        remote(send.at[chunks[c]], recv.at[chunks[c]], base + c, sib).start()
+
+    def hand_back(c, send, recv, base, total, landing, base_back):
+        remote(send.at[chunks[c]], recv.at[chunks[c]], base + c, sib).wait()
+        total[chunks[c]] = (halves[t] + recv[chunks[c]].astype(f32)).astype(bf)
+        for k in (2 * c, 2 * c + 1):
+            if k == 0:
+                landing[0] = total[0]
+            else:
+                remote(total.at[k], landing.at[k], base_back + k, (s, peer[k], t)).start()
+
+    def wait_back(total, landing, base_back):
+        for k in steps:
+            remote(total.at[k], landing.at[k], base_back + k, (s, peer[k], t)).wait()
+
+    def rows_chunk(c):
+        split_sum(c, nn(flat(hidden, chunks[c]), downv[...]), eo_send, eo_recv, sem_eo)
+
+    def rows_finish(c):
+        hand_back(c, eo_send, eo_recv, sem_eo, eob, eoret, sem_re)
+
+    mine_hot = (lax.broadcasted_iota(jnp.int32, (rows_of, experts), 1) == d).astype(f32)
+
+    def slope_chunk(c):
+        slot_logits = nt(flat(xrows, chunks[c]), wr_ref[...])
+        own_logit = jnp.sum(slot_logits * mine_hot, axis=-1, keepdims=True)
+        other_logit = jnp.sum(slot_logits * flat(other, chunks[c]), axis=-1, keepdims=True)
+        gate = 1.0 / (1.0 + jnp.exp(other_logit - own_logit))
+        out_grad = (flat(dyrows, chunks[c]).astype(f32) * gate).astype(bf)
+        og[chunks[c]] = out_grad.reshape(2, micro, cap, width)
+        grad = (nt(out_grad, downv[...]) * flat(dgelu, chunks[c]).astype(f32)).astype(bf)
+        pg[chunks[c]] = grad.reshape(2, micro, cap, ffn)
+
+    def back_chunk(c):
+        split_sum(c, nt(flat(pg, chunks[c]), upv[...]), cg_send, cg_recv, sem_cg)
+
+    def both_chunk(c):
+        front_chunk(c)
+        slope_chunk(c)
+
+    def back_finish(c):
+        hand_back(c, cg_send, cg_recv, sem_cg, cgb, cgret, sem_rc)
+
+    def hidden_of(m):
+        return jnp.concatenate([hidden[k, m] for k in range(experts)], axis=0)
 
     def expert_rows():
-        eo_send[...] = nn(hidden[u], downv[...]).astype(bf)
+        eo_send[...] = nn(hidden_of(u), downv[...]).astype(bf).reshape(eo_send.shape)
         eo_copy = remote(eo_send, eo_recv, sem_eo, sib)
         eo_copy.start()
-        part = nn(hidden[t], downv[...])
+        total = nn(hidden_of(t), downv[...])
         eo_copy.wait()
-        eob[...] = (part + eo_recv[...].astype(f32)).astype(bf)
+        eob[...] = (total + eo_recv[...].astype(f32).reshape(slots, width)).astype(bf).reshape(eob.shape)
 
     def send_back(source, landing, base):
-        mine = block(d, cap)
-        out = [remote(source.at[block(ahead[k], cap)], landing.at[mine], base + k, (s, ahead[k], t)) for k in steps]
-        for copy in out:
-            copy.start()
-        landing[mine, :] = source[mine, :]
-        return out
+        for k in steps:
+            remote(source.at[k], landing.at[k], base + k, (s, peer[k], t)).start()
+        landing[0] = source[0]
 
     def finish(copies):
         for copy in copies:
@@ -689,7 +828,7 @@
         ).astype(bf)
 
     def layer_output():
-        result = mid[...] + tn(spread_gates(), eoret[...])
+        result = mid[...] + tn(spread_gates(), eoret[...].reshape(slots, width))
         out_own[...] = result
         return result
 
@@ -707,13 +846,13 @@
 
     def gather_factors():
         no_all[t, d] = no1[t]
-        mix_all[d] = jnp.concatenate([mixed[m] for m in range(micro)], axis=0)
+        mix_all[d] = mixed[...]
         ring_gather(
             [
                 (lambda q: no_all.at[t, q, 0 : length // 2], 1, sem_ring_no),
                 (lambda q: no_all.at[t, q, length // 2 : length], -1, sem_ring_no + experts),
-                (lambda q: mix_all.at[q, 0:length], 1, sem_ring_mix),
-                (lambda q: mix_all.at[q, length : 2 * length], -1, sem_ring_mix + experts),
+                (lambda q: mix_all.at[q, 0], 1, sem_ring_mix),
+                (lambda q: mix_all.at[q, 1], -1, sem_ring_mix + experts),
             ]
         )
         copy = remote(no_all.at[t], no_all.at[t], sem_noall, sib)
@@ -722,71 +861,44 @@
 
     @pl.when(s == 0)
     def _():
-        expert_rows()
-        finish(send_back(eob, eoret, sem_re))
+        stream(arrivals, front_chunk, rows_chunk, rows_finish, False)
+        wait_back(eob, eoret, sem_re)
         x_send[...] = layer_output().astype(bf)
-        copy = remote(x_send, xb.at[t], sem_x, across)
-        copy.start()
+        x_copy.start()
         hand_out(out_own, secout_ref, sem_so)
-        copy.wait_send()
+        x_copy.wait_send()
         other_experts()
         gather_factors()
-        remote(dy_send, dyb, sem_dy, across).wait_recv()
-        dispatch(dyb[...], disp_y, dyrows, sem_ddy, sem_ddyf)
-
-    mine_hot = (lax.broadcasted_iota(jnp.int32, (slots, experts), 1) == d).astype(f32)
-    for m in range(micro):
-        slot_logits = nt(xrows[m], wr_ref[...])
-        own_logit = jnp.sum(slot_logits * mine_hot, axis=-1, keepdims=True)
-        other_logit = jnp.sum(slot_logits * other[m], axis=-1, keepdims=True)
-        gate = 1.0 / (1.0 + jnp.exp(other_logit - own_logit))
-        og[m] = (dyrows[m].astype(f32) * gate).astype(bf)
-
-    for m, rows in tiles:
-        pg[m, rows, :] = (nt(og[m, rows, :], downv[...]) * dgelu[m, rows, :].astype(f32)).astype(bf)
-    cg_send[...] = nt(pg[u], upv[...]).astype(bf)
-    cg_copy = remote(cg_send, cg_recv, sem_cg, sib)
-    cg_copy.start()
-    part_own = nt(pg[t], upv[...])
-    cg_copy.wait()
-    cgb[...] = (part_own + cg_recv[...].astype(f32)).astype(bf)
-    cg_out = send_back(cgb, cgret, sem_rc)
+        dy_copy.wait_recv()
+        arrivals_y = dispatch(dyb[...], disp_y, dyrows, sem_ddy, sem_ddyf)
+        stream(arrivals_y, slope_chunk, back_chunk, back_finish, True)
 
     @pl.when(s == 1)
     def _():
+        stream(arrivals, both_chunk, back_chunk, back_finish, True)
         expert_rows()
 
     def send_gate_grads():
         gg_send[...] = jnp.zeros_like(gg_send)
         ones = jnp.ones((8, width), bf)
-        for q in range(experts):
-            at = slice(q * cap, (q + 1) * cap)
-            high, low = split_low(dyrows[t, at, :].astype(f32) * eob[at, :].astype(f32))
-            gg_send[q, :, 0:cap] = nt(ones, high) + nt(ones, low)
-        out = [remote(gg_send.at[ahead[k]], gg_recv.at[d], sem_gg + k, (s, ahead[k], t)) for k in steps]
+        for k in range(experts):
+            high, low = split_low(dyrows[k, t].astype(f32) * eob[k].astype(f32))
+            gg_send[k, :, 0:cap] = nt(ones, high) + nt(ones, low)
+        out = [remote(gg_send.at[k], gg_recv.at[k], sem_gg + k, (s, peer[k], t)) for k in steps]
         for copy in out:
             copy.start()
-        gg_recv[d] = gg_send[d]
+        gg_recv[0] = gg_send[0]
         return out
 
     gg_out = send_gate_grads()
 
-    wide = lay.wide
-    for n in range(ffn // wide):
-        at = slice(n * wide, (n + 1) * wide)
-        total = tn(xrows[0], pg[0, :, at])
-        for m in range(1, micro):
-            total = total + tn(xrows[m], pg[m, :, at])
-        guv[:, at] = total
-        pltpu.make_async_copy(guv.at[:, at], gup_ref.at[:, at], gsem.at[n]).start()
-        total = tn(hidden[0, :, at], og[0])
-        for m in range(1, micro):
-            total = total + tn(hidden[m, :, at], og[m])
-        gdv[at, :] = total
-        pltpu.make_async_copy(gdv.at[at, :], gdown_ref.at[at, :], gsem.at[ffn // wide + n]).start()
-
     finish(gg_out)
-    finish(cg_out)
+    wait_back(cgb, cgret, sem_rc)
+
+    @pl.when(s == 1)
+    def _():
+        send_back(eob, eoret, sem_re)
+
     gg_rows = []
     for e in range(experts):
         high, low = split_low(gg_recv[e][:, 0:cap])
@@ -795,15 +907,18 @@
     gate_grad = jnp.concatenate(gg_rows, axis=0)
     gates = gate_t[...]
     logit_grad = (gates * (gate_grad - jnp.sum(gates * gate_grad, axis=0, keepdims=True))).astype(bf)
-    early_send[0:experts, :] = nn(logit_grad, ntb[...]).astype(bf)
-    two_grad = tn(logit_grad, wr_ref[...]) + tn(place[...], cgret[...])
+    router_grad = nn(tn(turn, logit_grad).astype(bf), ntb[...])
+    two_grad = tn(logit_grad, wrp[...]) + tn(place[...], cgret[...].reshape(slots, width))
     dy = dyb[...].astype(f32)
     middle = mid[...]
     scale = inverse_rms(middle)
     normed = middle * scale
-    early_send[experts : 2 * experts, :] = jnp.broadcast_to(
-        jnp.sum(two_grad * normed, axis=0, keepdims=True), (experts, width)
-    ).astype(bf)
+    gain_two_grad = jnp.sum(two_grad * normed, axis=0, keepdims=True)
+    groups = width // 128
+    small_send[...] = jnp.zeros_like(small_send)
+    for g in range(groups):
+        small_send[g, 0:experts, :] = router_grad[:, g * 128 : (g + 1) * 128]
+        small_send[g, experts + 1 : experts + 2, :] = gain_two_grad[:, g * 128 : (g + 1) * 128]
     scaled = two_grad * gain_two
     middle_grad = dy + scale * (scaled - normed * jnp.mean(scaled * normed, axis=-1, keepdims=True))
     mgrad[...] = middle_grad
@@ -811,30 +926,19 @@
     ag_copy = remote(ag.at[t], ag.at[t], sem_ag, sib)
     ag_copy.start()
 
-    def to_all(source, landing, base):
-        out = [remote(source, landing.at[d], base + k, (s, ahead[k], t)) for k in steps]
-        for copy in out:
-            copy.start()
-        landing[d] = source[...]
-        return out
-
-    early_out = to_all(early_send, early_all, sem_early)
-    ag_copy.wait()
-
-    def spread(source, landing, rows, base):
-        out = [remote(source.at[block(ahead[k], rows)], landing.at[d], base + k, (s, ahead[k], t)) for k in steps]
-        for copy in out:
-            copy.start()
-        landing[d] = source[block(d, rows), :]
-        return out
-
-    for m in range(micro):
-        agt[:, m * length : (m + 1) * length] = jnp.transpose(ag[m])
-    agt_out = spread(agt, agt_all, width // experts, sem_agt)
-
-    for m in range(micro):
+    agt[...] = jnp.transpose(ag[t])
+    agt_rows = width // experts
+    agt_out = []
+    for k in reversed(steps):
+        copy = remote(agt.at[block(peer[k], agt_rows)], agt_all.at[d, t], sem_agt + k, (s, peer[k], t))
+        copy.start()
+        agt_out.append((copy, k))
+    agt_all[d, t] = agt[block(d, agt_rows), :]
+    agt_own = remote(agt.at[block(d, agt_rows)], agt_all.at[d, t], sem_agtf, sib)
+    agt_own.start()
+
+    def attend_back(m, lane_of_m, fresh):
         mg[m] = nt(ag[m], outw_ref[...]).astype(bf)
-    for m in range(micro):
         for p in range(pairs):
             at = slice(p * 128, (p + 1) * 128)
             mg_pair = mg[m, :, at]
@@ -851,7 +955,7 @@
                 part = probs[:, lane]
                 step = prob_grad[:, lane]
                 score_grad = part * (step - jnp.sum(part * step, axis=-1, keepdims=True))
-                score_sum[2 * p + h] = score_grad if m == 0 else score_sum[2 * p + h] + score_grad
+                score_sum[2 * p + h] = score_grad if fresh else score_sum[2 * p + h] + score_grad
                 raw = (0.125 * score_grad).astype(bf)
                 raws.append(raw)
                 key_grad = key_grad + tn(raw, queries2[h * length : (h + 1) * length])
@@ -859,10 +963,18 @@
             query_grad = nn(jnp.concatenate(raws, axis=1), keys2)
             for c, grad in enumerate((query_grad, key_grad, value_grad)):
                 qkvg[c, m, :, at] = grad.astype(bf)
-                qgt[c * cols + p * 128 : c * cols + (p + 1) * 128, m * length : (m + 1) * length] = jnp.transpose(
-                    grad
-                ).astype(bf)
-    qgt_out = spread(qgt, qt_all, 3 * cols // experts, sem_qgt)
+                qgt[c * cols + p * 128 : c * cols + (p + 1) * 128, lane_of_m] = jnp.transpose(grad).astype(bf)
+
+    attend_back(t, slice(0, length), True)
+    ag_copy.wait()
+    attend_back(u, slice(length, 2 * length), False)
+    qgt_rows = 3 * cols // experts
+    qgt_out = []
+    for k in reversed(steps):
+        copy = remote(qgt.at[block(peer[k], qgt_rows)], qt_all.at[d], sem_qgt + k, (s, peer[k], t))
+        copy.start()
+        qgt_out.append(copy)
+    qt_all[d] = qgt[block(d, qgt_rows), :]
     def project_back(m):
         total = nt(qkvg[0, m], qkvw_ref[0])
         for c in range(1, 3):
@@ -886,9 +998,7 @@
     @pl.when(s == 1)
     def _():
         dy_send[...] = input_grad.astype(bf)
-        copy = remote(dy_send, dyb, sem_dy, across)
-        copy.start()
-        copy.wait_send()
+        dy_copy.start()
 
     hand_out(ig_own, ingrad_ref, sem_ig)
 
@@ -898,55 +1008,91 @@
         turned = pltpu.roll(nn(high, mirror) + nn(low, mirror), 0, 1, stride=1, stride_axis=0)
         sums.append(jnp.sum(turned, axis=0, keepdims=True))
     high, low = split_low(jnp.concatenate(sums, axis=0))
-    late_send[...] = jnp.zeros_like(late_send)
-    late_send[0 : 2 * pairs, 0 : lay.buckets] = nt(high, dist_rows) + nt(low, dist_rows)
-    late_send[7:8, :] = gain_one_grad
-    late_out = to_all(late_send, late_all, sem_late)
+    small_send[groups, 0 : 2 * pairs, 0 : lay.buckets] = nt(high, dist_rows) + nt(low, dist_rows)
+    for g in range(groups):
+        small_send[g, experts : experts + 1, :] = gain_one_grad[:, g * 128 : (g + 1) * 128]
+    small_out = [remote(small_send.at[peer[k]], small_in.at[k], sem_small + k, (s, peer[k], t)) for k in steps]
+    for copy in small_out:
+        copy.start()
+    small_in[0] = small_send[d]
+
+    wide = lay.wide
+    every = micro * slots
+    for n in range(ffn // wide):
+        at = slice(n * wide, (n + 1) * wide)
+        guv[:, at] = tn(xrows[...].reshape(every, width), pg[:, :, :, at].reshape(every, wide)).astype(bf)
+        pltpu.make_async_copy(guv.at[:, at], gup_ref.at[:, at], gsem.at[n]).start()
+        gdv[at, :] = tn(hidden[:, :, :, at].reshape(every, wide), og[...].reshape(every, width)).astype(bf)
+        pltpu.make_async_copy(gdv.at[at, :], gdown_ref.at[at, :], gsem.at[ffn // wide + n]).start()
 
     @pl.when(s == 1)
     def _():
         gather_factors()
 
-    finish(agt_out)
-    total = nn(agt_all[0], mix_all[0])
-    for q in range(1, experts):
-        total = total + nn(agt_all[q], mix_all[q])
+    passed = [agt_own]
+    for copy, k in agt_out:
+        copy.wait_recv()
+        forward = remote(agt_all.at[peer[k], t], agt_all.at[peer[k], t], sem_agtf + k, sib)
+        forward.start()
+        passed.append(forward)
+    for copy in passed:
+        copy.wait()
+    for copy, _ in agt_out:
+        copy.wait_send()
+    total = jnp.zeros((agt_rows, cols), f32)
+    for q in range(experts):
+        for m in range(micro):
+            total = total + nn(agt_all[q, m], mix_all[q, m])
     qkv_rows = 3 * cols // experts
-    out_rows = width // experts
-    shared_ref[d, qkv_rows:, 0:cols] = total[0 : out_rows // 2].astype(bf)
-    shared_ref[d, qkv_rows:, cols:] = total[out_rows // 2 :].astype(bf)
-    finish(qgt_out)
-    total = jnp.zeros((qkv_rows, width), f32)
-    for q in range(experts):
-        total = total + nn(qt_all[q], jnp.concatenate([no_all[0, q], no_all[1, q]], axis=0))
+    shared_ref[d, qkv_rows:, 0:cols] = total[0 : agt_rows // 2].astype(bf)
+    shared_ref[d, qkv_rows:, cols:] = total[agt_rows // 2 :].astype(bf)
+    def qkv_slice(q):
+        return nn(qt_all[q], jnp.concatenate([no_all[t, q], no_all[u, q]], axis=0))
+
+    total = qkv_slice(d)
+    for copy, k in zip(qgt_out, reversed(steps)):
+        copy.wait_recv()
+        total = total + qkv_slice(peer[k])
+    for copy in qgt_out:
+        copy.wait_send()
     shared_ref[d, 0:qkv_rows, :] = total.astype(bf)
-    share = shared_ref.shape[1] // 4
+    finish(small_out)
+    small_total = small_in[0]
+    for k in steps:
+        small_total = small_total + small_in[k]
+    small_all[d] = small_total
+    small_back = [remote(small_all.at[d], small_all.at[d], sem_back + k, (s, peer[k], t)) for k in steps]
+    for copy in small_back:
+        copy.start()
+
+    sums_copy = remote(small_all, small_sib, sem_sums, sib)
+
+    def pass_sums():
+        finish(small_back)
+        sums_copy.start()
+
+    share = shared_ref.shape[1] // 6
     ring_gather(
         [
-            (lambda q, c=c: shared_ref.at[q, c * share : (c + 1) * share], 1 if c < 2 else -1, sem_ring_out + c * experts)
-            for c in range(4)
-        ]
-    )
-    finish(early_out)
-    finish(late_out)
-    early_sum = early_all[0].astype(f32)
-    late_sum = late_all[0]
-    for q in range(1, experts):
-        early_sum = early_sum + early_all[q].astype(f32)
-        late_sum = late_sum + late_all[q]
-    gbias_ref[...] = late_sum[0 : 2 * pairs, 0 : lay.buckets]
-    sums_send[0 : 2 * experts, :] = early_sum
-    sums_send[2 * experts :, :] = late_sum
-    sums_copy = remote(sums_send, sums_recv, sem_sums, sib)
-    sums_copy.start()
+            (
+                lambda q, c=c: shared_ref.at[q, c * share : (c + 1) * share],
+                1 if c % 2 == 0 else -1,
+                sem_ring_out + c * experts,
+            )
+            for c in range(6)
+        ],
+        pass_sums,
+    )
     sums_copy.wait()
-    grouter_ref[...] = sums_send[0:experts, :] + sums_recv[0:experts, :]
-    ggain_ref[0:1, :] = sums_send[2 * experts + 7 :, :] + sums_recv[2 * experts + 7 :, :]
-    ggain_ref[1:2, :] = sums_send[experts : experts + 1, :] + sums_recv[experts : experts + 1, :]
-
+    for g in range(groups):
+        lanes = slice(g * 128, (g + 1) * 128)
+        grouter_ref[:, lanes] = small_all[g, 0:experts, :] + small_sib[g, 0:experts, :]
+        ggain_ref[:, lanes] = small_all[g, experts : experts + 2, :] + small_sib[g, experts : experts + 2, :]
+    gbias_ref[...] = small_all[groups, 0 : 2 * pairs, :]
     @pl.when(s == 1)
     def _():
-        finish(send_back(eob, eoret, sem_re))
+        dy_copy.wait_send()
+        wait_back(eob, eoret, sem_re)
         layer_output()
         hand_out(out_own, secout_ref, sem_so)
 
@@ -956,6 +1102,91 @@
         at = slice(n * wide, (n + 1) * wide)
         pltpu.make_async_copy(guv.at[:, at], gup_ref.at[:, at], gsem.at[n]).wait()
         pltpu.make_async_copy(gdv.at[at, :], gdown_ref.at[at, :], gsem.at[ffn // wide + n]).wait()
+
+
+def widen_kernel(
+    sec_ref, ing_ref, gain_ref, shared_ref, bias_ref, router_ref, up_ref, down_ref,
+    sec_out, ing_out, gain_out, bias_out, router_out, qkv_out, out_out, up_out, down_out,
+    up_low, up_wide, down_low, down_wide, shared_low, qkv_wide, out_wide, bias_low, bias_wide,
+    sec_low, ing_low, gain_low, router_low, in_sem, out_sem,
+):
+    f32 = jnp.float32
+    parts = 3
+    experts, shared_rows, width = shared_ref.shape
+    cols = out_wide.shape[0]
+    qkv_rows = 3 * cols // experts
+    low = ((up_ref, up_low), (down_ref, down_low))
+    wide = ((up_low, up_wide, up_out), (down_low, down_wide, down_out))
+    stores = []
+
+    def store(src, dst):
+        copy = pltpu.make_async_copy(src, dst, out_sem.at[len(stores)])
+        copy.start()
+        stores.append(copy)
+
+    def rows(ref, n):
+        size = ref.shape[0] // parts
+        return pl.ds(n * size, size)
+
+    load_shared = pltpu.make_async_copy(shared_ref, shared_low, in_sem.at[2 * parts])
+    load_bias = pltpu.make_async_copy(bias_ref, bias_low, in_sem.at[2 * parts + 1])
+    loads = [
+        pltpu.make_async_copy(src.at[rows(src, n)], dst.at[rows(dst, n)], in_sem.at[i * parts + n])
+        for i, (src, dst) in enumerate(low)
+        for n in range(parts)
+    ]
+    loads[0].start()
+    load_shared.start()
+    for copy in loads[1:]:
+        copy.start()
+    load_bias.start()
+    through = ((sec_ref, sec_low, sec_out), (ing_ref, ing_low, ing_out), (gain_ref, gain_low, gain_out), (router_ref, router_low, router_out))
+    passing = [
+        pltpu.make_async_copy(src, mid, in_sem.at[2 * parts + 2 + i]) for i, (src, mid, _) in enumerate(through)
+    ]
+    for copy in passing:
+        copy.start()
+
+    def widen(i, n):
+        loads[i * parts + n].wait()
+        src, dst, out = wide[i]
+        dst[rows(dst, n), :] = src[rows(src, n), :].astype(f32)
+        store(dst.at[rows(dst, n)], out.at[rows(out, n)])
+
+    def turn_qkv(c):
+        block = shared_low[:, 0:qkv_rows, :].reshape(3 * cols, width)[c * cols : (c + 1) * cols]
+        qkv_wide[c] = jnp.transpose(block.astype(f32))
+        store(qkv_wide.at[c], qkv_out.at[c])
+
+    widen(0, 0)
+    load_shared.wait()
+    turn_qkv(0)
+    widen(0, 1)
+    widen(0, 2)
+    turn_qkv(1)
+    widen(1, 0)
+    widen(1, 1)
+    turn_qkv(2)
+    out_block = jnp.concatenate(
+        [
+            shared_low[e, qkv_rows:, h * cols : (h + 1) * cols].astype(f32)
+            for e in range(experts)
+            for h in range(2)
+        ],
+        axis=0,
+    )
+    out_wide[...] = jnp.transpose(out_block)
+    store(out_wide, out_out)
+    widen(1, 2)
+    for copy, (_, mid, out) in zip(passing, through):
+        copy.wait()
+        store(mid, out)
+    load_bias.wait()
+    for h in range(bias_wide.shape[0]):
+        bias_wide[h] = bias_low[h : h + 1, 0 : bias_wide.shape[2]]
+    store(bias_wide, bias_out)
+    for copy in stores:
+        copy.wait()
 
 
 def fused_local(
@@ -985,9 +1216,8 @@
     lay.experts = experts
     lay.cap = cap
     lay.buckets = rel_bias.shape[1]
-    lay.row_tile = min(slots, 192)
     lay.wide = min(ffn, 256)
-    lay.sems = 20 * experts + 12
+    lay.sems = 25 * experts + 10
     bf = jnp.bfloat16
     f32 = jnp.float32
     vm = pltpu.VMEM
@@ -996,6 +1226,8 @@
     scratch = [
         vm((width, ffn), bf),
         vm((ffn, width), bf),
+        vm((3, width, cols), bf),
+        vm((cols, width), bf),
         vm((micro, length, width), bf),
         vm((length, width), bf),
         vm((experts, micro, 2, length), jnp.int32),
@@ -1011,28 +1243,30 @@
         vm((length, width), bf),
         vm((experts, length), f32),
         vm((experts, length), f32),
+        vm((experts, width), bf),
         vm((2 * pairs, length, length), f32),
-        vm((slots, width), bf),
-        vm((micro, slots, width), bf),
-        vm((slots, width), bf),
-        vm((micro, slots, width), bf),
-        vm((micro, slots, ffn), bf),
-        vm((micro, slots, ffn), bf),
-        vm((slots, width), bf),
-        vm((slots, width), bf),
-        vm((slots, width), bf),
-        vm((slots, width), bf),
+        vm((experts, cap, width), bf),
+        vm((experts, micro, cap, width), bf),
+        vm((experts, cap, width), bf),
+        vm((experts, micro, cap, width), bf),
+        vm((experts, micro, cap, ffn), bf),
+        vm((experts, micro, cap, ffn), bf),
+        vm((micro, 2, cap, width), f32),
+        vm((experts, cap, width), bf),
+        vm((experts, cap, width), bf),
+        vm((experts, cap, width), bf),
+        vm((experts, cap, width), bf),
         vm((length, width), f32),
         vm((length, width), bf),
-        vm((micro, slots, experts), f32),
-        vm((micro, slots, width), bf),
+        vm((experts, micro, cap, experts), f32),
+        vm((experts, micro, cap, width), bf),
         vm((experts, 8, 128), f32),
         vm((experts, 8, 128), f32),
-        vm((micro, slots, ffn), bf),
-        vm((slots, width), bf),
-        vm((slots, width), bf),
-        vm((slots, width), bf),
-        vm((slots, width), bf),
+        vm((experts, micro, cap, ffn), bf),
+        vm((experts, cap, width), bf),
+        vm((experts, cap, width), bf),
+        vm((experts, cap, width), bf),
+        vm((experts, cap, width), bf),
         vm((length, width), f32),
         vm((micro, length, width), bf),
         vm((micro, length, cols), bf),
@@ -1041,21 +1275,19 @@
         vm((length, width), bf),
         vm((length, width), f32),
         vm((length, width), bf),
-        vm((width, ffn), f32),
-        vm((ffn, width), f32),
+        vm((width, ffn), bf),
+        vm((ffn, width), bf),
         vm((micro, experts, length, width), bf),
-        vm((experts, micro * length, cols), bf),
+        vm((experts, micro, length, cols), bf),
         vm((3 * cols, micro * length), bf),
         vm((experts, 3 * cols // experts, micro * length), bf),
-        vm((width, micro * length), bf),
-        vm((experts, width // experts, micro * length), bf),
-        vm((2 * experts, width), bf),
-        vm((experts, 2 * experts, width), bf),
-        vm((8, width), f32),
-        vm((experts, 8, width), f32),
-        vm((2 * experts + 8, width), f32),
-        vm((2 * experts + 8, width), f32),
-        dma((2,)),
+        vm((width, length), bf),
+        vm((experts, micro, width // experts, length), bf),
+        vm((experts, 2 * experts, 128), f32),
+        vm((experts, 2 * experts, 128), f32),
+        vm((experts, 2 * experts, 128), f32),
+        vm((experts, 2 * experts, 128), f32),
+        dma((5,)),
         dma((2 * (ffn // lay.wide),)),
         dma((lay.sems,)),
         dma((lay.sems,)),
@@ -1068,15 +1300,15 @@
         shape((micro, length, width // 2), f32),
         shape((2, width), f32),
         shape((experts, shared_rows, width), bf),
-        shape((heads, lay.buckets), f32),
+        shape((heads, 128), f32),
         shape((experts, width), f32),
-        shape((width, ffn), f32),
-        shape((ffn, width), f32),
+        shape((width, ffn), bf),
+        shape((ffn, width), bf),
     )
     results = pl.pallas_call(
         partial(layer_kernel, lay),
         out_shape=out_shape,
-        in_specs=[whole] * 11 + [anywhere] * 2,
+        in_specs=[anywhere] * 2 + [whole] * 5 + [anywhere] * 2 + [whole] * 2 + [anywhere] * 2,
         out_specs=[whole] * 6 + [anywhere] * 2,
         scratch_shapes=scratch,
         name="two_sections",
@@ -1098,17 +1330,48 @@
         expert_up[0, 0],
         expert_down[0, 0],
     )
-    section_out, input_grads, gains, shared, bias, router, up, down = results
-    qkv_rows = 3 * cols // experts
-    qkv = shared[:, :qkv_rows].reshape(3, cols, width).astype(f32)
-    out = shared[:, qkv_rows:].reshape(experts, -1, 2, cols).transpose(0, 2, 1, 3).reshape(width, cols).astype(f32)
+    section_out, input_grads, gains, bias, router, qkv, out, up, down = pl.pallas_call(
+        widen_kernel,
+        out_shape=(
+            out_shape[0],
+            out_shape[1],
+            out_shape[2],
+            shape((heads, 1, lay.buckets), f32),
+            out_shape[5],
+            shape((3, width, cols), f32),
+            shape((cols, width), f32),
+            shape((width, ffn), f32),
+            shape((ffn, width), f32),
+        ),
+        in_specs=[anywhere] * 8,
+        out_specs=[anywhere] * 9,
+        scratch_shapes=[
+            vm((width, ffn), bf),
+            vm((width, ffn), f32),
+            vm((ffn, width), bf),
+            vm((ffn, width), f32),
+            vm((experts, shared_rows, width), bf),
+            vm((3, width, cols), f32),
+            vm((cols, width), f32),
+            vm((heads, 128), f32),
+            vm((heads, 1, lay.buckets), f32),
+            vm((micro, length, width // 2), f32),
+            vm((micro, length, width // 2), f32),
+            vm((2, width), f32),
+            vm((experts, width), f32),
+            dma((12,)),
+            dma((15,)),
+        ],
+        name="widen",
+        compiler_params=pltpu.CompilerParams(vmem_limit_bytes=60 * 1024 * 1024),
+    )(*results)
     return (
         section_out[None, :, None],
         input_grads[None, :, None],
         gains[None],
-        qkv.transpose(2, 0, 1)[None],
-        out.T[None],
-        bias.T[None],
+        qkv.transpose(1, 0, 2)[None],
+        out[None],
+        bias.transpose(1, 2, 0),
         router.T[None],
         up[None, None],
         down[None, None],

time: 238 us -> 195 us (0.82)
  the two profiles are of different devices: /device:TPU:0 before, /device:TPU:3 now
where the time goes in v3:
time: 195 us; the launch traced here: 192 us
  Pallas kernels  191 us (98%)
    pallas_call x1, Pallas kernels, fused_local(): pl.pallas_call(partial(layer_kernel, lay), out_shape=out_shape, in_specs=...  183 us
    pallas_call x1, Pallas kernels, fused_local(): pl.pallas_call(widen_kernel, out_shape=(out_shape[0], out_shape[1], out_s...  7.43 us

profile of v3, /device:TPU:3, one launch (start us, length us, event | category | flops | bytes accessed | tf_op | source)
XLA Modules:
  0.0 191.7 jit_solution(5544166114413939406)
XLA Ops:
  0.6 183.3 %two_sections.1 = (f32[2,128,384]{2,1,0:T(8,128)}, f32[2,128,384]{2,1,0:T(8,128)}, f32[2,768]{1,0:T(2,128)}, bf16[8,192,768]{2,1,0:T(8,128)(2,1)}, f32[6,128]{1,...) custom-call(bf16[2,128,768]{2,1,0:T(8,128)(2,1)} %bitcast.42, ...), custom_call_target="tpu_custom_call" | custom-call | tf_op jit(solution)/shard_map/two_sections/pallas_call | solution.py:1308
  184.0 7.4 %widen.1 = (f32[2,128,384]{2,1,0:T(8,128)}, f32[2,128,384]{2,1,0:T(8,128)}, f32[2,768]{1,0:T(2,128)}, f32[6,1,32]{2,1,0:T(1,128)}, f32[8,768]{1,0:T(8,128)}, /*i...) custom-call(f32[2,128,384]{2,1,0:T(8,128)} %get-tuple-element.26.sec_ref, ...), custom_call_target="tpu_custom_call" | custom-call | tf_op jit(solution)/shard_map/widen/pallas_call | solution.py:1333

commit v4 on v3

--- a/solution.py
+++ b/solution.py
@@ -395,14 +395,14 @@
     (
         tok_ref, cot_ref, seg_ref, pad_ref, routes_ref, dist_ref, gains_ref, qkvw_hbm, outw_hbm, relb_ref, wr_ref,
         up_ref, down_ref,
-        secout_ref, ingrad_ref, ggain_ref, shared_ref, gbias_ref, grouter_ref, gup_ref, gdown_ref,
+        secout_hbm, ingrad_hbm, ggain_ref, shared_hbm, gbias_ref, grouter_ref, gup_ref, gdown_ref,
         upv, downv, qkvw_ref, outw_ref, xb, dyb, rr, place, bias_buf, probs_buf, no1, qkvb, mixed, att_send, att_recv, mid, ntb,
         gate_t, hit_t, wrp, score_sum, disp_x, xrows, disp_y, dyrows, hidden, dgelu, halves, eo_send, eo_recv, eob, eoret, out_own,
-        x_send,
-        other, og, gg_send, gg_recv, pg, cg_send, cg_recv, cgb, cgret, mgrad, ag, mg, qkvg,
+        other, og, gg_part, gg_other, gg_send, gg_recv, pg, cg_send, cg_recv, cgb, cgret, mgrad, ag, mg, qkvg,
         no_send, no_recv, ig_own, dy_send, guv, gdv,
         no_all, mix_all, qgt, qt_all, agt, agt_all, small_send, small_in, small_all, small_sib,
-        wsem, gsem, ss, rs,
+        secout_ref, ingrad_ref, shared_ref, x_send, rs_buf, rs_in, help_buf, relay_buf,
+        wsem, gsem, osem, ss, rs,
     ) = refs
     bf = jnp.bfloat16
     f32 = jnp.float32
@@ -425,13 +425,21 @@
     def partner(flip):
         index = d
         for place, bit in enumerate((1, 2, 4)):
-            if flip & bit:
-                index = index + bit - 2 * bit * bits[place]
+            index = index + (flip // bit) % 2 * (bit - 2 * bit * bits[place])
         return index
 
     peer = [partner(flip) for flip in (0, 4, 1, 6, 2, 5, 3, 7)]
     steps = range(1, experts)
-    chunks = [slice(c, c + 2) for c in range(0, experts, 2)]
+    relayed = (5, 7)
+    chunks = range(experts // 2)
+
+    def pair(c):
+        return pl.ds(2 * c, 2)
+
+    def partner_at(k):
+        c = k // 2
+        return partner(c + (k % 2) * (4 + 2 * (c % 2) + c // 2 - c))
+
 
     def remote(src, dst, index, device):
         return pltpu.make_async_remote_copy(
@@ -457,6 +465,8 @@
 
     sem_routes = take(experts)
     sem_x = take(1)
+    sem_relay = take(2 * len(relayed))
+    sem_pass = take(2 * len(relayed))
     sem_xf = take(1)
     sem_dy = take(1)
     sem_att = take(1)
@@ -473,16 +483,21 @@
     sem_re = take(experts)
     sem_rc = take(experts)
     sem_gg = take(experts)
-    sem_agt = take(experts)
-    sem_agtf = take(experts)
+    sem_gg_core = take(len(chunks))
+    sem_help = take(2)
+    sem_spread = take(2 * experts)
     sem_qgt = take(experts)
     sem_small = take(experts)
     sem_back = take(experts)
     sem_sums = take(1)
     sem_noall = take(1)
-    sem_ring_no = take(2 * experts)
-    sem_ring_mix = take(2 * experts)
+    sem_section_zero = take(6 * experts)
+    sem_ring_no = sem_section_zero
+    sem_ring_mix = sem_section_zero + 2 * experts
+    sem_agt = sem_section_zero + 4 * experts
+    sem_agtf = sem_section_zero + 5 * experts
     sem_ring_out = take(6 * experts)
+    sem_ring_sum = sem_section_zero
     assert counter[0] == lay.sems
 
     def block(index, rows):
@@ -496,22 +511,48 @@
         p = lax.rem(position + 2 * experts, experts)
         return 2 * p + (p // (experts // 2)) * (2 * experts - 1 - 4 * p)
 
-    def ring_gather(streams, at_half=None):
-        moved = []
-        for k in range(experts - 1):
-            if k == experts // 2 and at_half is not None:
-                at_half()
-            for number, (view, direction, base) in enumerate(streams):
-                if k > 0:
-                    moved[(k - 1) * len(streams) + number].wait_recv()
-                held = view(ring_device(ring_at - direction * k))
-                copy = remote(held, held, base + k, (s, ring_device(ring_at + direction), t))
-                copy.start()
-                moved.append(copy)
-        for copy in moved[(experts - 2) * len(streams) :]:
-            copy.wait_recv()
-        for copy in moved:
-            copy.wait_send()
+    ways = ((1, 0), (-1, 4))
+
+    def hops(number, direction):
+        return experts // 2 - (number % 2 == (direction > 0))
+
+    def ring_gather(parts, at_half=None):
+        def hop(number, direction, shift, k):
+            view, base = parts[number]
+            held = view(ring_device(ring_at - direction * k))
+            return remote(held, held, base + shift + k, (s, ring_device(ring_at + direction), t))
+
+        lines = [(number, direction, shift) for number in range(len(parts)) for direction, shift in ways]
+        for line in lines:
+            hop(*line, 0).start()
+
+        def one(k, carry):
+            for line in lines:
+                hop(*line, k - 1).wait_recv()
+                hop(*line, k).start()
+            return carry
+
+        short = experts // 2 - 1
+        lax.fori_loop(1, short, one, 0)
+        if at_half is not None:
+            at_half()
+        for line in lines:
+            hop(*line, short - 1).wait_recv()
+            if hops(*line[:2]) > short:
+                hop(*line, short).start()
+        for line in lines:
+            if hops(*line[:2]) > short:
+                hop(*line, short).wait_recv()
+
+        def sent_one(k, carry):
+            for line in lines:
+                hop(*line, k).wait_send()
+            return carry
+
+        lax.fori_loop(0, short, sent_one, 0)
+        for line in lines:
+            if hops(*line[:2]) > short:
+                hop(*line, short).wait_send()
 
     load_up = pltpu.make_async_copy(up_ref, upv, wsem.at[0])
     load_down = pltpu.make_async_copy(down_ref, downv, wsem.at[1])
@@ -537,8 +578,9 @@
     for k in steps:
         pl.semaphore_signal(barrier, inc=1, device_id=(s, peer[k], t), device_id_type=pl.DeviceIdType.MESH)
     pl.semaphore_signal(barrier, inc=1, device_id=sib, device_id_type=pl.DeviceIdType.MESH)
-    pl.semaphore_signal(barrier, inc=1, device_id=across, device_id_type=pl.DeviceIdType.MESH)
-    pl.semaphore_wait(barrier, experts + 1)
+    for k in range(experts):
+        pl.semaphore_signal(barrier, inc=1, device_id=(1 - s, peer[k], t), device_id_type=pl.DeviceIdType.MESH)
+    pl.semaphore_wait(barrier, 2 * experts)
 
     for k in steps:
         fire(remote(routes_ref, rr.at[k], sem_routes + k, (s, peer[k], t)))
@@ -563,57 +605,112 @@
     for e in range(experts):
         place[e * cap : (e + 1) * cap, :] = (slot_at == spot[e : e + 1, :]).astype(f32).astype(bf)
 
-    def dispatch(rows, send, landing, base, base_fwd):
+    def to_relay(source, k, leg):
+        slot = leg * len(relayed) + relayed.index(k)
+        return remote(source, relay_buf.at[slot], sem_relay + slot, across)
+
+    def passed_on(landing, base, leg, k):
+        slot = leg * len(relayed) + relayed.index(k)
+        return pltpu.make_async_remote_copy(
+            src_ref=relay_buf.at[slot],
+            dst_ref=landing.at[k, t],
+            send_sem=ss.at[sem_pass + slot],
+            recv_sem=rs.at[base + k],
+            device_id=(0, peer[k], t),
+            device_id_type=pl.DeviceIdType.MESH,
+        )
+
+    def relay(landing, base, leg):
+        for k in relayed:
+            slot = leg * len(relayed) + relayed.index(k)
+            held = relay_buf.at[slot]
+            remote(held, held, sem_relay + slot, across).wait_recv()
+            passed_on(landing, base, leg, k).start()
+
+    def dispatch(rows, send, landing, base, base_fwd, leg=None, both=False):
         send[...] = nn(place[...], rows).astype(bf).reshape(send.shape)
-        out = [remote(send.at[k], landing.at[k, t], base + k, (s, peer[k], t)) for k in steps]
-        for copy in out:
-            copy.start()
-        first = remote(send.at[0], landing.at[0, t], base_fwd, sib)
-        first.start()
+
+        def start_relayed():
+            for k in relayed:
+                to_relay(send.at[k], k, leg).start()
+
+        def start_direct():
+            for k in relayed:
+                remote(send.at[k], landing.at[k, t], base + k, (s, peer[k], t)).start()
+
+        if both:
+            pl.when(s == 0)(start_relayed)
+        elif leg is not None:
+            start_relayed()
+        for k in steps:
+            if k not in relayed:
+                remote(send.at[k], landing.at[k, t], base + k, (s, peer[k], t)).start()
+        if both:
+            pl.when(s == 1)(start_direct)
+        elif leg is None:
+            start_direct()
+        remote(send.at[0], landing.at[0, t], base_fwd, sib).start()
         landing[0, t] = send[0]
 
-        def steps_of():
-            passed = [first]
-
-            def arrive(c):
-                for k in (2 * c, 2 * c + 1):
-                    if k > 0:
-                        out[k - 1].wait_recv()
-                        copy = remote(landing.at[k, t], landing.at[k, t], base_fwd + k, sib)
-                        copy.start()
-                        passed.append(copy)
-
-            def joined(c):
-                for k in (2 * c, 2 * c + 1):
-                    passed[k].wait_recv()
-
-            def drain():
-                for copy in out + passed:
-                    copy.wait_send()
-
-            return arrive, joined, drain
-
-        return steps_of
-
-    def stream(dispatched, first, second, finish_chunk, eager):
-        arrive, joined, drain = dispatched()
+        def arrived(k):
+            own = landing.at[k, t]
+            remote(own, own, base + k, sib).wait_recv()
+            remote(own, own, base_fwd + k, sib).start()
+
+        def joined(k):
+            own = landing.at[k, t]
+            remote(own, own, base_fwd + k, sib).wait_recv()
+
+        def drain(zero):
+            def one(k, carry):
+                remote(send.at[k], landing.at[k, t], base_fwd + k, sib).wait_send()
+                return carry
+
+            lax.fori_loop(0, experts, one, 0)
+            for k in steps:
+                if zero and k in relayed:
+                    to_relay(send.at[k], k, leg).wait_send()
+                else:
+                    remote(send.at[k], landing.at[k, t], base + k, sib).wait_send()
+
+        return arrived, joined, drain
+
+    def stream(dispatched, first, second, finish_chunk, eager, zero):
+        arrived, joined, drain = dispatched
         last = len(chunks) - 1
-        arrive(0)
+        arrived(1)
         joined(0)
-        for c in range(len(chunks)):
+        joined(1)
+
+        def arrive_next(c):
+            arrived(2 * c + 2)
+            arrived(2 * c + 3)
+
+        def one(c, carry):
             first(c)
-            if eager and c > 0:
-                finish_chunk(c - 1)
-            if eager and c < last:
-                arrive(c + 1)
-            second(c)
-            if not eager and c < last:
-                arrive(c + 1)
-                finish_chunk(c)
-            if c < last:
-                joined(c + 1)
+            if eager:
+                pl.when(c > 0)(lambda: finish_chunk(c - 1))
+                pl.when(c < last)(lambda: arrive_next(c))
+                second(c)
+            else:
+                second(c)
+
+                @pl.when(c < last)
+                def _():
+                    arrive_next(c)
+                    finish_chunk(c)
+
+
+            @pl.when(c < last)
+            def _():
+                joined(2 * c + 2)
+                joined(2 * c + 3)
+
+            return carry
+
+        lax.fori_loop(0, len(chunks), one, 0)
         finish_chunk(last)
-        drain()
+        drain(zero)
 
     def other_experts():
         for k in steps:
@@ -642,13 +739,21 @@
     @pl.when(s == 1)
     def _():
         load_cot.wait()
-        arrive, joined, drain = dispatch(dyb[...], disp_y, dyrows, sem_ddy, sem_ddyf)()
-        for c in range(len(chunks)):
-            arrive(c)
-        for c in range(len(chunks)):
-            joined(c)
-        drain()
+        relay(xrows, sem_dx, 0)
         other_experts()
+        arrived, joined, drain = dispatch(dyb[...], disp_y, dyrows, sem_ddy, sem_ddyf)
+
+        def pass_one(k, carry):
+            arrived(k)
+            return carry
+
+        def join_one(k, carry):
+            joined(k)
+            return carry
+
+        lax.fori_loop(1, experts, pass_one, 0)
+        lax.fori_loop(0, experts, join_one, 0)
+        drain(False)
 
     dist_rows = (
         lax.broadcasted_iota(jnp.int32, (lay.buckets, length), 0) == dist_ref[...]
@@ -673,6 +778,15 @@
     dy_copy = remote(dy_send, dyb, sem_dy, across)
     x_forward = remote(xb.at[t], xb.at[t], sem_xf, sib)
 
+    def spread_gates(gates_ref):
+        return jnp.concatenate(
+            [
+                jnp.broadcast_to(gates_ref[e : e + 1, :], (cap, length)) * place[e * cap : (e + 1) * cap, :].astype(f32)
+                for e in range(experts)
+            ],
+            axis=0,
+        ).astype(bf)
+
     @pl.when(s == 1)
     def _():
         x_copy.wait_recv()
@@ -713,17 +827,21 @@
         att_copy.start()
 
     begin = u + s * (t - u)
-    attend(begin)
-
-    @pl.when(s == 0)
-    def _():
-        project_other()
-
-    @pl.when(s == 1)
-    def _():
-        x_forward.wait()
-
-    attend(1 - begin)
+
+    def attend_one(i, carry):
+        @pl.when((s == 1) & (i == 1))
+        def _():
+            x_forward.wait()
+
+        attend(begin + i * (1 - 2 * begin))
+
+        @pl.when((s == 0) & (i == 0))
+        def _():
+            project_other()
+
+        return carry
+
+    lax.fori_loop(0, micro, attend_one, 0)
 
     @pl.when(s == 1)
     def _():
@@ -738,7 +856,7 @@
     terms = jnp.exp(logits_t - jnp.max(logits_t, axis=0, keepdims=True))
     gate_t[...] = terms / jnp.sum(terms, axis=0, keepdims=True)
 
-    arrivals = dispatch(ntb[...], disp_x, xrows, sem_dx, sem_dxf)
+    arrivals = dispatch(ntb[...], disp_x, xrows, sem_dx, sem_dxf, 0, True)
     load_up.wait()
     load_down.wait()
     rows_of = 2 * micro * cap
@@ -747,49 +865,69 @@
         return ref[chunk].reshape(rows_of, ref.shape[-1])
 
     def front_chunk(c):
-        value, slope = gelu_parts(nn(flat(xrows, chunks[c]), upv[...]))
-        hidden[chunks[c]] = value.astype(bf).reshape(2, micro, cap, ffn)
-        dgelu[chunks[c]] = slope.astype(bf).reshape(2, micro, cap, ffn)
+        value, slope = gelu_parts(nn(flat(xrows, pair(c)), upv[...]))
+        hidden[pair(c)] = value.astype(bf).reshape(2, micro, cap, ffn)
+        dgelu[pair(c)] = slope.astype(bf).reshape(2, micro, cap, ffn)
 
     def split_sum(c, total, send, recv, base):
         for m in range(micro):
             halves[m] = total.reshape(2, micro, cap, width)[:, m]
-        send[chunks[c]] = halves[u].astype(bf)
-        remote(send.at[chunks[c]], recv.at[chunks[c]], base + c, sib).start()
+        send[pair(c)] = halves[u].astype(bf)
+        remote(send.at[pair(c)], recv.at[pair(c)], base + c, sib).start()
 
     def hand_back(c, send, recv, base, total, landing, base_back):
-        remote(send.at[chunks[c]], recv.at[chunks[c]], base + c, sib).wait()
-        total[chunks[c]] = (halves[t] + recv[chunks[c]].astype(f32)).astype(bf)
-        for k in (2 * c, 2 * c + 1):
-            if k == 0:
-                landing[0] = total[0]
-            else:
-                remote(total.at[k], landing.at[k], base_back + k, (s, peer[k], t)).start()
+        remote(send.at[pair(c)], recv.at[pair(c)], base + c, sib).wait()
+        total[pair(c)] = (halves[t] + recv[pair(c)].astype(f32)).astype(bf)
+
+        def give(k):
+            remote(total.at[k], landing.at[k], base_back + k, (s, partner_at(k), t)).start()
+
+        def keep():
+            landing[0] = total[0]
+
+        if isinstance(c, int):
+            give(2 * c)
+        else:
+            pl.when(c == 0)(keep)
+            pl.when(c > 0)(lambda: give(2 * c))
+        give(2 * c + 1)
 
     def wait_back(total, landing, base_back):
-        for k in steps:
-            remote(total.at[k], landing.at[k], base_back + k, (s, peer[k], t)).wait()
+        def one(k, carry):
+            remote(total.at[k], landing.at[k], base_back + k, sib).wait()
+            return carry
+
+        lax.fori_loop(1, experts, one, 0)
 
     def rows_chunk(c):
-        split_sum(c, nn(flat(hidden, chunks[c]), downv[...]), eo_send, eo_recv, sem_eo)
+        split_sum(c, nn(flat(hidden, pair(c)), downv[...]), eo_send, eo_recv, sem_eo)
 
     def rows_finish(c):
         hand_back(c, eo_send, eo_recv, sem_eo, eob, eoret, sem_re)
 
     mine_hot = (lax.broadcasted_iota(jnp.int32, (rows_of, experts), 1) == d).astype(f32)
 
+    ones = jnp.ones((8, ffn), bf)
+    gg_part[...] = jnp.zeros_like(gg_part)
+
     def slope_chunk(c):
-        slot_logits = nt(flat(xrows, chunks[c]), wr_ref[...])
+        slot_logits = nt(flat(xrows, pair(c)), wr_ref[...])
         own_logit = jnp.sum(slot_logits * mine_hot, axis=-1, keepdims=True)
-        other_logit = jnp.sum(slot_logits * flat(other, chunks[c]), axis=-1, keepdims=True)
+        other_logit = jnp.sum(slot_logits * flat(other, pair(c)), axis=-1, keepdims=True)
         gate = 1.0 / (1.0 + jnp.exp(other_logit - own_logit))
-        out_grad = (flat(dyrows, chunks[c]).astype(f32) * gate).astype(bf)
-        og[chunks[c]] = out_grad.reshape(2, micro, cap, width)
-        grad = (nt(out_grad, downv[...]) * flat(dgelu, chunks[c]).astype(f32)).astype(bf)
-        pg[chunks[c]] = grad.reshape(2, micro, cap, ffn)
+        dy_flat = flat(dyrows, pair(c))
+        og[pair(c)] = (dy_flat.astype(f32) * gate).astype(bf).reshape(2, micro, cap, width)
+        grad = nt(dy_flat, downv[...])
+        pg[pair(c)] = (grad * gate * flat(dgelu, pair(c)).astype(f32)).astype(bf).reshape(2, micro, cap, ffn)
+        product = (grad * flat(hidden, pair(c)).astype(f32)).astype(bf)
+        for i in range(2):
+            for m in range(micro):
+                at = (i * micro + m) * cap
+                gg_part[m, 2 * c + i, :, 0:cap] = nt(ones, product[at : at + cap])
 
     def back_chunk(c):
-        split_sum(c, nt(flat(pg, chunks[c]), upv[...]), cg_send, cg_recv, sem_cg)
+        remote(gg_part.at[u, pair(c)], gg_other.at[pair(c)], sem_gg_core + c, sib).start()
+        split_sum(c, nt(flat(pg, pair(c)), upv[...]), cg_send, cg_recv, sem_cg)
 
     def both_chunk(c):
         front_chunk(c)
@@ -797,6 +935,21 @@
 
     def back_finish(c):
         hand_back(c, cg_send, cg_recv, sem_cg, cgb, cgret, sem_rc)
+        remote(gg_part.at[u, pair(c)], gg_other.at[pair(c)], sem_gg_core + c, sib).wait()
+        gg_send[pair(c)] = gg_part[t, pair(c)] + gg_other[pair(c)]
+
+        def give(k):
+            remote(gg_send.at[k], gg_recv.at[k], sem_gg + k, (s, partner_at(k), t)).start()
+
+        def keep():
+            gg_recv[0] = gg_send[0]
+
+        if isinstance(c, int):
+            give(2 * c)
+        else:
+            pl.when(c == 0)(keep)
+            pl.when(c > 0)(lambda: give(2 * c))
+        give(2 * c + 1)
 
     def hidden_of(m):
         return jnp.concatenate([hidden[k, m] for k in range(experts)], axis=0)
@@ -818,17 +971,8 @@
         for copy in copies:
             copy.wait()
 
-    def spread_gates():
-        return jnp.concatenate(
-            [
-                jnp.broadcast_to(gate_t[e : e + 1, :], (cap, length)) * place[e * cap : (e + 1) * cap, :].astype(f32)
-                for e in range(experts)
-            ],
-            axis=0,
-        ).astype(bf)
-
     def layer_output():
-        result = mid[...] + tn(spread_gates(), eoret[...].reshape(slots, width))
+        result = mid[...] + tn(spread_gates(gate_t), eoret[...].reshape(slots, width))
         out_own[...] = result
         return result
 
@@ -838,21 +982,22 @@
     def other_half():
         return pl.ds(pl.multiple_of(u * half, half), half)
 
-    def hand_out(rows_ref, out_ref, index):
+    def hand_out(rows_ref, out_ref, index, hbm_ref, index_out):
         copy = remote(rows_ref.at[:, other_half()], out_ref.at[t], index, sib)
         copy.start()
         out_ref[t] = rows_ref[:, own_half()]
         copy.wait()
+        pltpu.make_async_copy(out_ref, hbm_ref, osem.at[index_out]).start()
 
     def gather_factors():
         no_all[t, d] = no1[t]
         mix_all[d] = mixed[...]
         ring_gather(
             [
-                (lambda q: no_all.at[t, q, 0 : length // 2], 1, sem_ring_no),
-                (lambda q: no_all.at[t, q, length // 2 : length], -1, sem_ring_no + experts),
-                (lambda q: mix_all.at[q, 0], 1, sem_ring_mix),
-                (lambda q: mix_all.at[q, 1], -1, sem_ring_mix + experts),
+                (lambda q: no_all.at[t, q, 0 : length // 2], sem_ring_no),
+                (lambda q: no_all.at[t, q, length // 2 : length], sem_ring_no + experts),
+                (lambda q: mix_all.at[q, 0], sem_ring_mix),
+                (lambda q: mix_all.at[q, 1], sem_ring_mix + experts),
             ]
         )
         copy = remote(no_all.at[t], no_all.at[t], sem_noall, sib)
@@ -861,43 +1006,30 @@
 
     @pl.when(s == 0)
     def _():
-        stream(arrivals, front_chunk, rows_chunk, rows_finish, False)
+        stream(arrivals, front_chunk, rows_chunk, rows_finish, True, True)
         wait_back(eob, eoret, sem_re)
         x_send[...] = layer_output().astype(bf)
         x_copy.start()
-        hand_out(out_own, secout_ref, sem_so)
-        x_copy.wait_send()
+        hand_out(out_own, secout_ref, sem_so, secout_hbm, 0)
         other_experts()
         gather_factors()
+        x_copy.wait_send()
         dy_copy.wait_recv()
-        arrivals_y = dispatch(dyb[...], disp_y, dyrows, sem_ddy, sem_ddyf)
-        stream(arrivals_y, slope_chunk, back_chunk, back_finish, True)
+        arrivals_y = dispatch(dyb[...], disp_y, dyrows, sem_ddy, sem_ddyf, 1)
+        stream(arrivals_y, slope_chunk, back_chunk, back_finish, True, True)
 
     @pl.when(s == 1)
     def _():
-        stream(arrivals, both_chunk, back_chunk, back_finish, True)
+        stream(arrivals, both_chunk, back_chunk, back_finish, True, False)
         expert_rows()
 
-    def send_gate_grads():
-        gg_send[...] = jnp.zeros_like(gg_send)
-        ones = jnp.ones((8, width), bf)
-        for k in range(experts):
-            high, low = split_low(dyrows[k, t].astype(f32) * eob[k].astype(f32))
-            gg_send[k, :, 0:cap] = nt(ones, high) + nt(ones, low)
-        out = [remote(gg_send.at[k], gg_recv.at[k], sem_gg + k, (s, peer[k], t)) for k in steps]
-        for copy in out:
-            copy.start()
-        gg_recv[0] = gg_send[0]
-        return out
-
-    gg_out = send_gate_grads()
-
-    finish(gg_out)
+    wait_back(gg_send, gg_recv, sem_gg)
     wait_back(cgb, cgret, sem_rc)
 
     @pl.when(s == 1)
     def _():
         send_back(eob, eoret, sem_re)
+
 
     gg_rows = []
     for e in range(experts):
@@ -926,18 +1058,22 @@
     ag_copy = remote(ag.at[t], ag.at[t], sem_ag, sib)
     ag_copy.start()
 
-    agt[...] = jnp.transpose(ag[t])
     agt_rows = width // experts
-    agt_out = []
-    for k in reversed(steps):
-        copy = remote(agt.at[block(peer[k], agt_rows)], agt_all.at[d, t], sem_agt + k, (s, peer[k], t))
-        copy.start()
-        agt_out.append((copy, k))
-    agt_all[d, t] = agt[block(d, agt_rows), :]
+    agt_out = [
+        (remote(agt.at[block(peer[k], agt_rows)], agt_all.at[d, t], sem_agt + k, (s, peer[k], t)), k)
+        for k in reversed(steps)
+    ]
     agt_own = remote(agt.at[block(d, agt_rows)], agt_all.at[d, t], sem_agtf, sib)
-    agt_own.start()
-
-    def attend_back(m, lane_of_m, fresh):
+
+    @pl.when(s == 0)
+    def _():
+        agt[...] = jnp.transpose(ag[t])
+        for copy, _ in agt_out:
+            copy.start()
+        agt_all[d, t] = agt[block(d, agt_rows), :]
+        agt_own.start()
+
+    def attend_back(m, lane_of_m):
         mg[m] = nt(ag[m], outw_ref[...]).astype(bf)
         for p in range(pairs):
             at = slice(p * 128, (p + 1) * 128)
@@ -955,7 +1091,7 @@
                 part = probs[:, lane]
                 step = prob_grad[:, lane]
                 score_grad = part * (step - jnp.sum(part * step, axis=-1, keepdims=True))
-                score_sum[2 * p + h] = score_grad if fresh else score_sum[2 * p + h] + score_grad
+                score_sum[2 * p + h] += score_grad
                 raw = (0.125 * score_grad).astype(bf)
                 raws.append(raw)
                 key_grad = key_grad + tn(raw, queries2[h * length : (h + 1) * length])
@@ -965,16 +1101,28 @@
                 qkvg[c, m, :, at] = grad.astype(bf)
                 qgt[c * cols + p * 128 : c * cols + (p + 1) * 128, lane_of_m] = jnp.transpose(grad).astype(bf)
 
-    attend_back(t, slice(0, length), True)
-    ag_copy.wait()
-    attend_back(u, slice(length, 2 * length), False)
+    score_sum[...] = jnp.zeros_like(score_sum)
+
+    def back_one(i, carry):
+        @pl.when(i == 1)
+        def _():
+            ag_copy.wait()
+
+        attend_back(t + i * (u - t), pl.ds(pl.multiple_of(i * length, length), length))
+        return carry
+
+    lax.fori_loop(0, micro, back_one, 0)
     qgt_rows = 3 * cols // experts
-    qgt_out = []
-    for k in reversed(steps):
-        copy = remote(qgt.at[block(peer[k], qgt_rows)], qt_all.at[d], sem_qgt + k, (s, peer[k], t))
-        copy.start()
-        qgt_out.append(copy)
-    qt_all[d] = qgt[block(d, qgt_rows), :]
+    qgt_out = [
+        remote(qgt.at[block(peer[k], qgt_rows)], qt_all.at[d], sem_qgt + k, (s, peer[k], t)) for k in reversed(steps)
+    ]
+
+    @pl.when(s == 0)
+    def _():
+        for copy in qgt_out:
+            copy.start()
+        qt_all[d] = qgt[block(d, qgt_rows), :]
+
     def project_back(m):
         total = nt(qkvg[0, m], qkvw_ref[0])
         for c in range(1, 3):
@@ -994,13 +1142,13 @@
     scaled = one_grad * gain_one
     input_grad = mgrad[...] + scale * (scaled - normed * jnp.mean(scaled * normed, axis=-1, keepdims=True))
     ig_own[...] = input_grad
+    dy_send[...] = input_grad.astype(bf)
 
     @pl.when(s == 1)
     def _():
-        dy_send[...] = input_grad.astype(bf)
         dy_copy.start()
 
-    hand_out(ig_own, ingrad_ref, sem_ig)
+    hand_out(ig_own, ingrad_ref, sem_ig, ingrad_hbm, 1)
 
     sums = []
     for head in range(2 * pairs):
@@ -1018,44 +1166,96 @@
 
     wide = lay.wide
     every = micro * slots
-    for n in range(ffn // wide):
-        at = slice(n * wide, (n + 1) * wide)
+
+    def expert_grads(n, carry):
+        at = pl.ds(pl.multiple_of(n * wide, wide), wide)
         guv[:, at] = tn(xrows[...].reshape(every, width), pg[:, :, :, at].reshape(every, wide)).astype(bf)
         pltpu.make_async_copy(guv.at[:, at], gup_ref.at[:, at], gsem.at[n]).start()
         gdv[at, :] = tn(hidden[:, :, :, at].reshape(every, wide), og[...].reshape(every, width)).astype(bf)
         pltpu.make_async_copy(gdv.at[at, :], gdown_ref.at[at, :], gsem.at[ffn // wide + n]).start()
+        return carry
+
+    lax.fori_loop(0, ffn // wide, expert_grads, 0)
+
+    qkv_rows = 3 * cols // experts
+    share = shared_ref.shape[1] // 6
+    parts = [slice(c * share, (c + 1) * share) for c in range(6)]
+
+    def pack_out(total):
+        half_rows = agt_rows // 2
+        return jnp.concatenate([total[..., 0:half_rows, :], total[..., half_rows:, :]], axis=-1).astype(bf)
+
+    @pl.when(s == 0)
+    def _():
+        passed = [agt_own]
+        for copy, k in agt_out:
+            copy.wait_recv()
+            forward = remote(agt_all.at[peer[k], t], agt_all.at[peer[k], t], sem_agtf + k, sib)
+            forward.start()
+            passed.append(forward)
+        for copy in passed:
+            copy.wait()
+        for copy, _ in agt_out:
+            copy.wait_send()
+        total = jnp.zeros((agt_rows, cols), f32)
+        for q in range(experts):
+            for m in range(micro):
+                total = total + nn(agt_all[q, m], mix_all[q, m])
+        shared_ref[d, qkv_rows:, :] = pack_out(total)
+
+        def qkv_slice(q):
+            return nn(qt_all[q], jnp.concatenate([no_all[t, q], no_all[u, q]], axis=0))
+
+        total = qkv_slice(d)
+        for copy, k in zip(qgt_out, reversed(steps)):
+            copy.wait_recv()
+            total = total + qkv_slice(peer[k])
+        for copy in qgt_out:
+            copy.wait_send()
+        shared_ref[d, 0:qkv_rows, :] = total.astype(bf)
 
     @pl.when(s == 1)
     def _():
-        gather_factors()
-
-    passed = [agt_own]
-    for copy, k in agt_out:
-        copy.wait_recv()
-        forward = remote(agt_all.at[peer[k], t], agt_all.at[peer[k], t], sem_agtf + k, sib)
-        forward.start()
-        passed.append(forward)
-    for copy in passed:
-        copy.wait()
-    for copy, _ in agt_out:
-        copy.wait_send()
-    total = jnp.zeros((agt_rows, cols), f32)
-    for q in range(experts):
-        for m in range(micro):
-            total = total + nn(agt_all[q, m], mix_all[q, m])
-    qkv_rows = 3 * cols // experts
-    shared_ref[d, qkv_rows:, 0:cols] = total[0 : agt_rows // 2].astype(bf)
-    shared_ref[d, qkv_rows:, cols:] = total[agt_rows // 2 :].astype(bf)
-    def qkv_slice(q):
-        return nn(qt_all[q], jnp.concatenate([no_all[t, q], no_all[u, q]], axis=0))
-
-    total = qkv_slice(d)
-    for copy, k in zip(qgt_out, reversed(steps)):
-        copy.wait_recv()
-        total = total + qkv_slice(peer[k])
-    for copy in qgt_out:
-        copy.wait_send()
-    shared_ref[d, 0:qkv_rows, :] = total.astype(bf)
+        normed_rows = no1[...].reshape(micro * length, width)
+        own = jnp.concatenate([tn(qkvg[c].reshape(micro * length, cols), normed_rows) for c in range(3)], axis=0)
+        rs_buf[:, 0:qkv_rows, :] = own.astype(bf).reshape(experts, qkv_rows, width)
+        own = tn(ag[...].reshape(micro * length, width), mixed[...].reshape(micro * length, cols))
+        rs_buf[:, qkv_rows:, :] = pack_out(own.reshape(experts, agt_rows, cols))
+
+        relay(dyrows, sem_ddy, 1)
+
+        def hop(number, direction, shift, k):
+            owner = ring_device(ring_at + direction * (hops(number, direction) - k))
+            return remote(
+                rs_buf.at[owner, parts[number]],
+                rs_in.at[shift + k, parts[number]],
+                sem_ring_sum + number * experts + shift + k,
+                (s, ring_device(ring_at + direction), t),
+            )
+
+        lines = [(number, direction, shift) for number in range(len(parts)) for direction, shift in ways]
+        longest = experts // 2
+        for k in range(longest):
+            for number, direction, shift in lines:
+                if k < hops(number, direction):
+                    if k > 0:
+                        rows = parts[number]
+                        owner = ring_device(ring_at + direction * (hops(number, direction) - k))
+                        hop(number, direction, shift, k - 1).wait_recv()
+                        total = rs_buf[owner, rows, :].astype(f32) + rs_in[shift + k - 1, rows, :].astype(f32)
+                        rs_buf[owner, rows, :] = total.astype(bf)
+                    hop(number, direction, shift, k).start()
+        for number, rows in enumerate(parts):
+            total = rs_buf[d, rows, :].astype(f32)
+            for direction, shift in ways:
+                last = hops(number, direction) - 1
+                hop(number, direction, shift, last).wait_recv()
+                total = total + rs_in[shift + last, rows, :].astype(f32)
+            shared_ref[d, rows, :] = total.astype(bf)
+        for number, direction, shift in lines:
+            for k in range(hops(number, direction)):
+                hop(number, direction, shift, k).wait_send()
+
     finish(small_out)
     small_total = small_in[0]
     for k in steps:
@@ -1071,18 +1271,14 @@
         finish(small_back)
         sums_copy.start()
 
-    share = shared_ref.shape[1] // 6
-    ring_gather(
-        [
-            (
-                lambda q, c=c: shared_ref.at[q, c * share : (c + 1) * share],
-                1 if c % 2 == 0 else -1,
-                sem_ring_out + c * experts,
-            )
-            for c in range(6)
-        ],
-        pass_sums,
-    )
+
+    streams = [
+        (lambda q, rows=rows: shared_ref.at[q, rows], sem_ring_out + c * experts) for c, rows in enumerate(parts)
+    ]
+
+    ring_gather(streams, pass_sums)
+    for q in range(experts):
+        pltpu.make_async_copy(shared_ref.at[q], shared_hbm.at[q], osem.at[2 + q]).start()
     sums_copy.wait()
     for g in range(groups):
         lanes = slice(g * 128, (g + 1) * 128)
@@ -1092,12 +1288,19 @@
     @pl.when(s == 1)
     def _():
         dy_copy.wait_send()
+        for k in relayed:
+            passed_on(xrows, sem_dx, 0, k).wait_send()
+            passed_on(dyrows, sem_ddy, 1, k).wait_send()
         wait_back(eob, eoret, sem_re)
         layer_output()
-        hand_out(out_own, secout_ref, sem_so)
+        hand_out(out_own, secout_ref, sem_so, secout_hbm, 0)
 
     for copy in sent:
         copy.wait_send()
+    pltpu.make_async_copy(secout_ref, secout_hbm, osem.at[0]).wait()
+    pltpu.make_async_copy(ingrad_ref, ingrad_hbm, osem.at[1]).wait()
+    for q in range(experts):
+        pltpu.make_async_copy(shared_ref.at[q], shared_hbm.at[q], osem.at[2 + q]).wait()
     for n in range(ffn // wide):
         at = slice(n * wide, (n + 1) * wide)
         pltpu.make_async_copy(guv.at[:, at], gup_ref.at[:, at], gsem.at[n]).wait()
@@ -1212,12 +1415,13 @@
     ffn = expert_up.shape[3]
     slots = experts * cap
     pairs = cols // 128
+    shared_rows = 3 * cols // experts + width // experts // 2
     lay = Layout()
     lay.experts = experts
     lay.cap = cap
     lay.buckets = rel_bias.shape[1]
     lay.wide = min(ffn, 256)
-    lay.sems = 25 * experts + 10
+    lay.sems = 28 * experts + 12 + experts // 2
     bf = jnp.bfloat16
     f32 = jnp.float32
     vm = pltpu.VMEM
@@ -1257,9 +1461,10 @@
         vm((experts, cap, width), bf),
         vm((experts, cap, width), bf),
         vm((length, width), f32),
-        vm((length, width), bf),
         vm((experts, micro, cap, experts), f32),
         vm((experts, micro, cap, width), bf),
+        vm((micro, experts, 8, 128), f32),
+        vm((experts, 8, 128), f32),
         vm((experts, 8, 128), f32),
         vm((experts, 8, 128), f32),
         vm((experts, micro, cap, ffn), bf),
@@ -1287,14 +1492,22 @@
         vm((experts, 2 * experts, 128), f32),
         vm((experts, 2 * experts, 128), f32),
         vm((experts, 2 * experts, 128), f32),
+        vm((micro, length, width // 2), f32),
+        vm((micro, length, width // 2), f32),
+        vm((experts, shared_rows, width), bf),
+        vm((length, width), bf),
+        vm((experts, shared_rows, width), bf),
+        vm((experts, shared_rows, width), bf),
+        vm((shared_rows, width), bf),
+        vm((4, cap, width), bf),
         dma((5,)),
         dma((2 * (ffn // lay.wide),)),
+        dma((experts + 2,)),
         dma((lay.sems,)),
         dma((lay.sems,)),
     ]
     whole = pl.BlockSpec(memory_space=pltpu.VMEM)
     anywhere = pl.BlockSpec(memory_space=pl.ANY)
-    shared_rows = 3 * cols // experts + width // experts // 2
     out_shape = (
         shape((micro, length, width // 2), f32),
         shape((micro, length, width // 2), f32),
@@ -1309,7 +1522,7 @@
         partial(layer_kernel, lay),
         out_shape=out_shape,
         in_specs=[anywhere] * 2 + [whole] * 5 + [anywhere] * 2 + [whole] * 2 + [anywhere] * 2,
-        out_specs=[whole] * 6 + [anywhere] * 2,
+        out_specs=[anywhere] * 2 + [whole, anywhere, whole, whole] + [anywhere] * 2,
         scratch_shapes=scratch,
         name="two_sections",
         compiler_params=pltpu.CompilerParams(

time: 195 us -> 182 us (0.933)
  the two profiles are of different devices: /device:TPU:3 before, /device:TPU:0 now
where the time goes in v4:
time: 182 us; the launch traced here: 181 us
  Pallas kernels  181 us (99%)
    pallas_call x1, Pallas kernels, fused_local(): pl.pallas_call(partial(layer_kernel, lay), out_shape=out_shape, in_specs=...  173 us
    pallas_call x1, Pallas kernels, fused_local(): pl.pallas_call(widen_kernel, out_shape=(out_shape[0], out_shape[1], out_s...  7.43 us

profile of v4, /device:TPU:0, one launch (start us, length us, event | category | flops | bytes accessed | tf_op | source)
XLA Modules:
  0.0 181.4 jit_solution(3920353620238145125)
XLA Ops:
  0.6 173.2 %two_sections.1 = (f32[2,128,384]{2,1,0:T(8,128)}, f32[2,128,384]{2,1,0:T(8,128)}, f32[2,768]{1,0:T(2,128)}, bf16[8,192,768]{2,1,0:T(8,128)(2,1)}, f32[6,128]{1,...) custom-call(bf16[2,128,768]{2,1,0:T(8,128)(2,1)} %bitcast.42, ...), custom_call_target="tpu_custom_call" | custom-call | tf_op jit(solution)/shard_map/two_sections/pallas_call | solution.py:1521
  173.8 7.4 %widen.1 = (f32[2,128,384]{2,1,0:T(8,128)}, f32[2,128,384]{2,1,0:T(8,128)}, f32[2,768]{1,0:T(2,128)}, f32[6,1,32]{2,1,0:T(1,128)}, f32[8,768]{1,0:T(8,128)}, /*i...) custom-call(f32[2,128,384]{2,1,0:T(8,128)} %get-tuple-element.26.sec_ref, ...), custom_call_target="tpu_custom_call" | custom-call | tf_op jit(solution)/shard_map/widen/pallas_call | solution.py:1546

commit v5 on v4

--- a/solution.py
+++ b/solution.py
@@ -395,14 +395,14 @@
     (
         tok_ref, cot_ref, seg_ref, pad_ref, routes_ref, dist_ref, gains_ref, qkvw_hbm, outw_hbm, relb_ref, wr_ref,
         up_ref, down_ref,
-        secout_hbm, ingrad_hbm, ggain_ref, shared_hbm, gbias_ref, grouter_ref, gup_ref, gdown_ref,
+        secout_ref, ingrad_ref, ggain_ref, shared_ref, gbias_ref, grouter_ref, guv, gdv,
         upv, downv, qkvw_ref, outw_ref, xb, dyb, rr, place, bias_buf, probs_buf, no1, qkvb, mixed, att_send, att_recv, mid, ntb,
         gate_t, hit_t, wrp, score_sum, disp_x, xrows, disp_y, dyrows, hidden, dgelu, halves, eo_send, eo_recv, eob, eoret, out_own,
         other, og, gg_part, gg_other, gg_send, gg_recv, pg, cg_send, cg_recv, cgb, cgret, mgrad, ag, mg, qkvg,
-        no_send, no_recv, ig_own, dy_send, guv, gdv,
+        no_send, no_recv, ig_own, dy_send,
         no_all, mix_all, qgt, qt_all, agt, agt_all, small_send, small_in, small_all, small_sib,
-        secout_ref, ingrad_ref, shared_ref, x_send, rs_buf, rs_in, help_buf, relay_buf,
-        wsem, gsem, osem, ss, rs,
+        x_send, rs_buf, rs_in, relay_buf,
+        wsem, ss, rs,
     ) = refs
     bf = jnp.bfloat16
     f32 = jnp.float32
@@ -441,64 +441,64 @@
         return partner(c + (k % 2) * (4 + 2 * (c % 2) + c // 2 - c))
 
 
-    def remote(src, dst, index, device):
+    def remote(src, dst, sem, device, k=0):
         return pltpu.make_async_remote_copy(
             src_ref=src,
             dst_ref=dst,
-            send_sem=ss.at[index],
-            recv_sem=rs.at[index],
+            send_sem=ss.at[sem[0]],
+            recv_sem=rs.at[sem[1] + k],
             device_id=device,
             device_id_type=pl.DeviceIdType.MESH,
         )
 
-    counter = [0]
-
-    def take(amount):
-        counter[0] += amount
-        return counter[0] - amount
-
-    sent = []
-
-    def fire(copy):
-        copy.start()
-        sent.append(copy)
-
-    sem_routes = take(experts)
-    sem_x = take(1)
-    sem_relay = take(2 * len(relayed))
-    sem_pass = take(2 * len(relayed))
-    sem_xf = take(1)
-    sem_dy = take(1)
-    sem_att = take(1)
-    sem_eo = take(experts)
-    sem_cg = take(experts)
-    sem_ag = take(1)
-    sem_no = take(1)
-    sem_so = take(1)
-    sem_ig = take(1)
-    sem_dx = take(experts)
-    sem_dxf = take(experts)
-    sem_ddy = take(experts)
-    sem_ddyf = take(experts)
-    sem_re = take(experts)
-    sem_rc = take(experts)
-    sem_gg = take(experts)
+    counter = [0, 0]
+
+    def take(arrivals=1):
+        pair_of = (counter[0], counter[1])
+        counter[0] += 1
+        counter[1] += arrivals
+        return pair_of
+
+    def all_sent(like, sem):
+        remote(like, like, sem, sib).wait_send()
+
+    def all_here(like, sem, k=0):
+        remote(like, like, sem, sib, k).wait_recv()
+
+    ring_hops = experts - 1
+    sem_routes = take()
+    sem_x = take()
+    sem_relay = [take(len(relayed)) for _ in range(2)]
+    sem_pass = [take(0) for _ in range(2)]
+    sem_xf = take()
+    sem_dy = take()
+    sem_att = take()
+    sem_eo = take(len(chunks))
+    sem_cg = take(len(chunks))
+    sem_ag = take()
+    sem_no = take()
+    sem_so = take()
+    sem_ig = take()
+    sem_dx = take(len(chunks))
+    sem_dxf = take(len(chunks))
+    sem_ddy = take(len(chunks))
+    sem_ddyf = take(len(chunks))
+    sem_re = take()
+    sem_rc = take()
+    sem_gg = take()
     sem_gg_core = take(len(chunks))
-    sem_help = take(2)
-    sem_spread = take(2 * experts)
     sem_qgt = take(experts)
-    sem_small = take(experts)
-    sem_back = take(experts)
-    sem_sums = take(1)
-    sem_noall = take(1)
-    sem_section_zero = take(6 * experts)
-    sem_ring_no = sem_section_zero
-    sem_ring_mix = sem_section_zero + 2 * experts
-    sem_agt = sem_section_zero + 4 * experts
-    sem_agtf = sem_section_zero + 5 * experts
-    sem_ring_out = take(6 * experts)
-    sem_ring_sum = sem_section_zero
-    assert counter[0] == lay.sems
+    sem_agt = take()
+    sem_agtf = take()
+    sem_small = take()
+    sem_back = take()
+    sem_sums = take()
+    sem_noall = take()
+    sem_ring_no = take(2 * ring_hops)
+    sem_ring_mix = take(2 * ring_hops)
+    sem_ring_sum = (take(0)[0], sem_ring_no[1])
+    sem_ring_out = take(4 * ring_hops)
+    assert tuple(counter) == lay.sems
 
     def block(index, rows):
         return pl.ds(pl.multiple_of(index * rows, rows), rows)
@@ -511,18 +511,23 @@
         p = lax.rem(position + 2 * experts, experts)
         return 2 * p + (p // (experts // 2)) * (2 * experts - 1 - 4 * p)
 
-    ways = ((1, 0), (-1, 4))
-
     def hops(number, direction):
         return experts // 2 - (number % 2 == (direction > 0))
 
+    def hop_index(number, direction, k):
+        return number * ring_hops + k + (0 if direction > 0 else hops(number, 1))
+
+    def lines_of(amount):
+        return [(number, direction) for number in range(amount) for direction in (1, -1)]
+
     def ring_gather(parts, at_half=None):
-        def hop(number, direction, shift, k):
-            view, base = parts[number]
+        def hop(number, direction, k):
+            view, sem, first = parts[number]
             held = view(ring_device(ring_at - direction * k))
-            return remote(held, held, base + shift + k, (s, ring_device(ring_at + direction), t))
-
-        lines = [(number, direction, shift) for number in range(len(parts)) for direction, shift in ways]
+            index = hop_index(number, direction, k) - first * ring_hops
+            return remote(held, held, sem, (s, ring_device(ring_at + direction), t), index)
+
+        lines = lines_of(len(parts))
         for line in lines:
             hop(*line, 0).start()
 
@@ -538,21 +543,11 @@
             at_half()
         for line in lines:
             hop(*line, short - 1).wait_recv()
-            if hops(*line[:2]) > short:
+            if hops(*line) > short:
                 hop(*line, short).start()
         for line in lines:
-            if hops(*line[:2]) > short:
+            if hops(*line) > short:
                 hop(*line, short).wait_recv()
-
-        def sent_one(k, carry):
-            for line in lines:
-                hop(*line, k).wait_send()
-            return carry
-
-        lax.fori_loop(0, short, sent_one, 0)
-        for line in lines:
-            if hops(*line[:2]) > short:
-                hop(*line, short).wait_send()
 
     load_up = pltpu.make_async_copy(up_ref, upv, wsem.at[0])
     load_down = pltpu.make_async_copy(down_ref, downv, wsem.at[1])
@@ -583,7 +578,7 @@
     pl.semaphore_wait(barrier, 2 * experts)
 
     for k in steps:
-        fire(remote(routes_ref, rr.at[k], sem_routes + k, (s, peer[k], t)))
+        remote(routes_ref, rr.at[k], sem_routes, (s, peer[k], t)).start()
     rr[0] = routes_ref[...]
 
     lanes8 = lax.broadcasted_iota(jnp.int32, (experts, length), 0)
@@ -606,29 +601,21 @@
         place[e * cap : (e + 1) * cap, :] = (slot_at == spot[e : e + 1, :]).astype(f32).astype(bf)
 
     def to_relay(source, k, leg):
-        slot = leg * len(relayed) + relayed.index(k)
-        return remote(source, relay_buf.at[slot], sem_relay + slot, across)
-
-    def passed_on(landing, base, leg, k):
-        slot = leg * len(relayed) + relayed.index(k)
-        return pltpu.make_async_remote_copy(
-            src_ref=relay_buf.at[slot],
-            dst_ref=landing.at[k, t],
-            send_sem=ss.at[sem_pass + slot],
-            recv_sem=rs.at[base + k],
-            device_id=(0, peer[k], t),
-            device_id_type=pl.DeviceIdType.MESH,
-        )
-
-    def relay(landing, base, leg):
-        for k in relayed:
-            slot = leg * len(relayed) + relayed.index(k)
-            held = relay_buf.at[slot]
-            remote(held, held, sem_relay + slot, across).wait_recv()
-            passed_on(landing, base, leg, k).start()
-
-    def dispatch(rows, send, landing, base, base_fwd, leg=None, both=False):
+        i = relayed.index(k)
+        return remote(source, relay_buf.at[leg * len(relayed) + i], sem_relay[leg], across, i)
+
+    def relay(landing, sem, leg):
+        for i, k in enumerate(relayed):
+            held = relay_buf.at[leg * len(relayed) + i]
+            all_here(held, sem_relay[leg], i)
+            through = (sem_pass[leg][0], sem[1] + k // 2)
+            remote(held, landing.at[k, t], through, (0, peer[k], t)).start()
+
+    def dispatch(rows, send, landing, sem, sem_fwd, leg=None, both=False):
         send[...] = nn(place[...], rows).astype(bf).reshape(send.shape)
+
+        def direct(k):
+            remote(send.at[k], landing.at[k, t], sem, (s, peer[k], t), k // 2).start()
 
         def start_relayed():
             for k in relayed:
@@ -636,75 +623,64 @@
 
         def start_direct():
             for k in relayed:
-                remote(send.at[k], landing.at[k, t], base + k, (s, peer[k], t)).start()
-
+                direct(k)
+
+        direct(1)
         if both:
             pl.when(s == 0)(start_relayed)
         elif leg is not None:
             start_relayed()
-        for k in steps:
+        for k in steps[1:]:
             if k not in relayed:
-                remote(send.at[k], landing.at[k, t], base + k, (s, peer[k], t)).start()
+                direct(k)
         if both:
             pl.when(s == 1)(start_direct)
         elif leg is None:
             start_direct()
-        remote(send.at[0], landing.at[0, t], base_fwd, sib).start()
         landing[0, t] = send[0]
 
-        def arrived(k):
-            own = landing.at[k, t]
-            remote(own, own, base + k, sib).wait_recv()
-            remote(own, own, base_fwd + k, sib).start()
-
-        def joined(k):
-            own = landing.at[k, t]
-            remote(own, own, base_fwd + k, sib).wait_recv()
+        def arrive(c):
+            held = landing.at[pair(c), t]
+            all_here(landing.at[1, t] if isinstance(c, int) and c == 0 else held, sem, c)
+            remote(held, held, sem_fwd, sib, c).start()
+
+        def joined(c):
+            all_here(landing.at[pair(c), t], sem_fwd, c)
 
         def drain(zero):
-            def one(k, carry):
-                remote(send.at[k], landing.at[k, t], base_fwd + k, sib).wait_send()
-                return carry
-
-            lax.fori_loop(0, experts, one, 0)
-            for k in steps:
-                if zero and k in relayed:
-                    to_relay(send.at[k], k, leg).wait_send()
-                else:
-                    remote(send.at[k], landing.at[k, t], base + k, sib).wait_send()
-
-        return arrived, joined, drain
+            all_sent(send, sem_fwd)
+            if zero:
+                all_sent(send.at[0 : experts - 1 - len(relayed)], sem)
+                all_sent(send.at[0 : len(relayed)], sem_relay[leg])
+            else:
+                all_sent(send.at[1:experts], sem)
+
+        return arrive, joined, drain
 
     def stream(dispatched, first, second, finish_chunk, eager, zero):
-        arrived, joined, drain = dispatched
+        arrive, joined, drain = dispatched
         last = len(chunks) - 1
-        arrived(1)
+        arrive(0)
         joined(0)
-        joined(1)
-
-        def arrive_next(c):
-            arrived(2 * c + 2)
-            arrived(2 * c + 3)
 
         def one(c, carry):
             first(c)
             if eager:
                 pl.when(c > 0)(lambda: finish_chunk(c - 1))
-                pl.when(c < last)(lambda: arrive_next(c))
+                pl.when(c < last)(lambda: arrive(c + 1))
                 second(c)
             else:
                 second(c)
 
                 @pl.when(c < last)
                 def _():
-                    arrive_next(c)
+                    arrive(c + 1)
                     finish_chunk(c)
 
 
             @pl.when(c < last)
             def _():
-                joined(2 * c + 2)
-                joined(2 * c + 3)
+                joined(c + 1)
 
             return carry
 
@@ -713,8 +689,7 @@
         drain(zero)
 
     def other_experts():
-        for k in steps:
-            remote(routes_ref, rr.at[k], sem_routes + k, (s, peer[k], t)).wait_recv()
+        all_here(rr.at[1:experts], sem_routes)
 
         def one(i, carry):
             q = i // micro
@@ -741,18 +716,19 @@
         load_cot.wait()
         relay(xrows, sem_dx, 0)
         other_experts()
-        arrived, joined, drain = dispatch(dyb[...], disp_y, dyrows, sem_ddy, sem_ddyf)
-
-        def pass_one(k, carry):
-            arrived(k)
+        arrive, joined, drain = dispatch(dyb[...], disp_y, dyrows, sem_ddy, sem_ddyf)
+
+        def pass_one(c, carry):
+            arrive(c)
             return carry
 
-        def join_one(k, carry):
-            joined(k)
+        def join_one(c, carry):
+            joined(c)
             return carry
 
-        lax.fori_loop(1, experts, pass_one, 0)
-        lax.fori_loop(0, experts, join_one, 0)
+        arrive(0)
+        lax.fori_loop(1, len(chunks), pass_one, 0)
+        lax.fori_loop(0, len(chunks), join_one, 0)
         drain(False)
 
     dist_rows = (
@@ -873,14 +849,14 @@
         for m in range(micro):
             halves[m] = total.reshape(2, micro, cap, width)[:, m]
         send[pair(c)] = halves[u].astype(bf)
-        remote(send.at[pair(c)], recv.at[pair(c)], base + c, sib).start()
+        remote(send.at[pair(c)], recv.at[pair(c)], base, sib, c).start()
 
     def hand_back(c, send, recv, base, total, landing, base_back):
-        remote(send.at[pair(c)], recv.at[pair(c)], base + c, sib).wait()
+        all_here(recv.at[pair(c)], base, c)
         total[pair(c)] = (halves[t] + recv[pair(c)].astype(f32)).astype(bf)
 
         def give(k):
-            remote(total.at[k], landing.at[k], base_back + k, (s, partner_at(k), t)).start()
+            remote(total.at[k], landing.at[k], base_back, (s, partner_at(k), t)).start()
 
         def keep():
             landing[0] = total[0]
@@ -892,12 +868,9 @@
             pl.when(c > 0)(lambda: give(2 * c))
         give(2 * c + 1)
 
-    def wait_back(total, landing, base_back):
-        def one(k, carry):
-            remote(total.at[k], landing.at[k], base_back + k, sib).wait()
-            return carry
-
-        lax.fori_loop(1, experts, one, 0)
+    def wait_back(total, landing, sem):
+        all_here(landing.at[1:experts], sem)
+        all_sent(total.at[1:experts], sem)
 
     def rows_chunk(c):
         split_sum(c, nn(flat(hidden, pair(c)), downv[...]), eo_send, eo_recv, sem_eo)
@@ -926,7 +899,7 @@
                 gg_part[m, 2 * c + i, :, 0:cap] = nt(ones, product[at : at + cap])
 
     def back_chunk(c):
-        remote(gg_part.at[u, pair(c)], gg_other.at[pair(c)], sem_gg_core + c, sib).start()
+        remote(gg_part.at[u, pair(c)], gg_other.at[pair(c)], sem_gg_core, sib, c).start()
         split_sum(c, nt(flat(pg, pair(c)), upv[...]), cg_send, cg_recv, sem_cg)
 
     def both_chunk(c):
@@ -935,11 +908,11 @@
 
     def back_finish(c):
         hand_back(c, cg_send, cg_recv, sem_cg, cgb, cgret, sem_rc)
-        remote(gg_part.at[u, pair(c)], gg_other.at[pair(c)], sem_gg_core + c, sib).wait()
+        all_here(gg_other.at[pair(c)], sem_gg_core, c)
         gg_send[pair(c)] = gg_part[t, pair(c)] + gg_other[pair(c)]
 
         def give(k):
-            remote(gg_send.at[k], gg_recv.at[k], sem_gg + k, (s, partner_at(k), t)).start()
+            remote(gg_send.at[k], gg_recv.at[k], sem_gg, (s, partner_at(k), t)).start()
 
         def keep():
             gg_recv[0] = gg_send[0]
@@ -959,17 +932,13 @@
         eo_copy = remote(eo_send, eo_recv, sem_eo, sib)
         eo_copy.start()
         total = nn(hidden_of(t), downv[...])
-        eo_copy.wait()
+        eo_copy.wait_recv()
         eob[...] = (total + eo_recv[...].astype(f32).reshape(slots, width)).astype(bf).reshape(eob.shape)
 
     def send_back(source, landing, base):
         for k in steps:
-            remote(source.at[k], landing.at[k], base + k, (s, peer[k], t)).start()
+            remote(source.at[k], landing.at[k], base, (s, peer[k], t)).start()
         landing[0] = source[0]
-
-    def finish(copies):
-        for copy in copies:
-            copy.wait()
 
     def layer_output():
         result = mid[...] + tn(spread_gates(gate_t), eoret[...].reshape(slots, width))
@@ -982,24 +951,25 @@
     def other_half():
         return pl.ds(pl.multiple_of(u * half, half), half)
 
-    def hand_out(rows_ref, out_ref, index, hbm_ref, index_out):
+    def hand_out(rows_ref, out_ref, index):
         copy = remote(rows_ref.at[:, other_half()], out_ref.at[t], index, sib)
         copy.start()
         out_ref[t] = rows_ref[:, own_half()]
         copy.wait()
-        pltpu.make_async_copy(out_ref, hbm_ref, osem.at[index_out]).start()
 
     def gather_factors():
         no_all[t, d] = no1[t]
         mix_all[d] = mixed[...]
         ring_gather(
             [
-                (lambda q: no_all.at[t, q, 0 : length // 2], sem_ring_no),
-                (lambda q: no_all.at[t, q, length // 2 : length], sem_ring_no + experts),
-                (lambda q: mix_all.at[q, 0], sem_ring_mix),
-                (lambda q: mix_all.at[q, 1], sem_ring_mix + experts),
+                (lambda q: no_all.at[t, q, 0 : length // 2], sem_ring_no, 0),
+                (lambda q: no_all.at[t, q, length // 2 : length], sem_ring_no, 0),
+                (lambda q: mix_all.at[q, 0], sem_ring_mix, 2),
+                (lambda q: mix_all.at[q, 1], sem_ring_mix, 2),
             ]
         )
+        all_sent(no_all.at[t, 1:experts], sem_ring_no)
+        all_sent(mix_all.at[1:experts], sem_ring_mix)
         copy = remote(no_all.at[t], no_all.at[t], sem_noall, sib)
         copy.start()
         copy.wait()
@@ -1010,7 +980,7 @@
         wait_back(eob, eoret, sem_re)
         x_send[...] = layer_output().astype(bf)
         x_copy.start()
-        hand_out(out_own, secout_ref, sem_so, secout_hbm, 0)
+        hand_out(out_own, secout_ref, sem_so)
         other_experts()
         gather_factors()
         x_copy.wait_send()
@@ -1059,17 +1029,13 @@
     ag_copy.start()
 
     agt_rows = width // experts
-    agt_out = [
-        (remote(agt.at[block(peer[k], agt_rows)], agt_all.at[d, t], sem_agt + k, (s, peer[k], t)), k)
-        for k in reversed(steps)
-    ]
     agt_own = remote(agt.at[block(d, agt_rows)], agt_all.at[d, t], sem_agtf, sib)
 
     @pl.when(s == 0)
     def _():
         agt[...] = jnp.transpose(ag[t])
-        for copy, _ in agt_out:
-            copy.start()
+        for k in reversed(steps):
+            remote(agt.at[block(peer[k], agt_rows)], agt_all.at[d, t], sem_agt, (s, peer[k], t)).start()
         agt_all[d, t] = agt[block(d, agt_rows), :]
         agt_own.start()
 
@@ -1099,7 +1065,11 @@
             query_grad = nn(jnp.concatenate(raws, axis=1), keys2)
             for c, grad in enumerate((query_grad, key_grad, value_grad)):
                 qkvg[c, m, :, at] = grad.astype(bf)
-                qgt[c * cols + p * 128 : c * cols + (p + 1) * 128, lane_of_m] = jnp.transpose(grad).astype(bf)
+
+        @pl.when(s == 0)
+        def _():
+            for c in range(3):
+                qgt[c * cols : (c + 1) * cols, lane_of_m] = jnp.transpose(qkvg[c, m])
 
     score_sum[...] = jnp.zeros_like(score_sum)
 
@@ -1113,14 +1083,10 @@
 
     lax.fori_loop(0, micro, back_one, 0)
     qgt_rows = 3 * cols // experts
-    qgt_out = [
-        remote(qgt.at[block(peer[k], qgt_rows)], qt_all.at[d], sem_qgt + k, (s, peer[k], t)) for k in reversed(steps)
-    ]
-
     @pl.when(s == 0)
     def _():
-        for copy in qgt_out:
-            copy.start()
+        for k in reversed(steps):
+            remote(qgt.at[block(peer[k], qgt_rows)], qt_all.at[d], sem_qgt, (s, peer[k], t), k).start()
         qt_all[d] = qgt[block(d, qgt_rows), :]
 
     def project_back(m):
@@ -1148,7 +1114,7 @@
     def _():
         dy_copy.start()
 
-    hand_out(ig_own, ingrad_ref, sem_ig, ingrad_hbm, 1)
+    hand_out(ig_own, ingrad_ref, sem_ig)
 
     sums = []
     for head in range(2 * pairs):
@@ -1159,9 +1125,8 @@
     small_send[groups, 0 : 2 * pairs, 0 : lay.buckets] = nt(high, dist_rows) + nt(low, dist_rows)
     for g in range(groups):
         small_send[g, experts : experts + 1, :] = gain_one_grad[:, g * 128 : (g + 1) * 128]
-    small_out = [remote(small_send.at[peer[k]], small_in.at[k], sem_small + k, (s, peer[k], t)) for k in steps]
-    for copy in small_out:
-        copy.start()
+    for k in steps:
+        remote(small_send.at[peer[k]], small_in.at[k], sem_small, (s, peer[k], t)).start()
     small_in[0] = small_send[d]
 
     wide = lay.wide
@@ -1170,16 +1135,14 @@
     def expert_grads(n, carry):
         at = pl.ds(pl.multiple_of(n * wide, wide), wide)
         guv[:, at] = tn(xrows[...].reshape(every, width), pg[:, :, :, at].reshape(every, wide)).astype(bf)
-        pltpu.make_async_copy(guv.at[:, at], gup_ref.at[:, at], gsem.at[n]).start()
         gdv[at, :] = tn(hidden[:, :, :, at].reshape(every, wide), og[...].reshape(every, width)).astype(bf)
-        pltpu.make_async_copy(gdv.at[at, :], gdown_ref.at[at, :], gsem.at[ffn // wide + n]).start()
         return carry
 
     lax.fori_loop(0, ffn // wide, expert_grads, 0)
 
     qkv_rows = 3 * cols // experts
-    share = shared_ref.shape[1] // 6
-    parts = [slice(c * share, (c + 1) * share) for c in range(6)]
+    share = shared_ref.shape[1] // 4
+    parts = [slice(c * share, (c + 1) * share) for c in range(4)]
 
     def pack_out(total):
         half_rows = agt_rows // 2
@@ -1187,16 +1150,13 @@
 
     @pl.when(s == 0)
     def _():
-        passed = [agt_own]
-        for copy, k in agt_out:
-            copy.wait_recv()
-            forward = remote(agt_all.at[peer[k], t], agt_all.at[peer[k], t], sem_agtf + k, sib)
-            forward.start()
-            passed.append(forward)
-        for copy in passed:
-            copy.wait()
-        for copy, _ in agt_out:
-            copy.wait_send()
+        all_here(agt_all.at[1:experts, 0], sem_agt)
+        for k in steps:
+            held = agt_all.at[peer[k], t]
+            remote(held, held, sem_agtf, sib).start()
+        all_here(agt_all.at[:, 0], sem_agtf)
+        all_sent(agt_all.at[1:experts, 0], sem_agt)
+        all_sent(agt_all.at[:, 0], sem_agtf)
         total = jnp.zeros((agt_rows, cols), f32)
         for q in range(experts):
             for m in range(micro):
@@ -1207,11 +1167,10 @@
             return nn(qt_all[q], jnp.concatenate([no_all[t, q], no_all[u, q]], axis=0))
 
         total = qkv_slice(d)
-        for copy, k in zip(qgt_out, reversed(steps)):
-            copy.wait_recv()
+        for k in reversed(steps):
+            all_here(qt_all.at[0], sem_qgt, k)
             total = total + qkv_slice(peer[k])
-        for copy in qgt_out:
-            copy.wait_send()
+        all_sent(qt_all.at[1:experts], sem_qgt)
         shared_ref[d, 0:qkv_rows, :] = total.astype(bf)
 
     @pl.when(s == 1)
@@ -1224,62 +1183,59 @@
 
         relay(dyrows, sem_ddy, 1)
 
-        def hop(number, direction, shift, k):
-            owner = ring_device(ring_at + direction * (hops(number, direction) - k))
+        def owner_at(number, direction, k):
+            return ring_device(ring_at + direction * (hops(number, direction) - k))
+
+        def hop(number, direction, k):
+            index = hop_index(number, direction, k)
             return remote(
-                rs_buf.at[owner, parts[number]],
-                rs_in.at[shift + k, parts[number]],
-                sem_ring_sum + number * experts + shift + k,
+                rs_buf.at[owner_at(number, direction, k), parts[number]],
+                rs_in.at[index % ring_hops, parts[number]],
+                sem_ring_sum,
                 (s, ring_device(ring_at + direction), t),
+                index,
             )
 
-        lines = [(number, direction, shift) for number in range(len(parts)) for direction, shift in ways]
-        longest = experts // 2
-        for k in range(longest):
-            for number, direction, shift in lines:
-                if k < hops(number, direction):
+        lines = lines_of(len(parts))
+        for k in range(experts // 2):
+            for line in lines:
+                if k < hops(*line):
                     if k > 0:
-                        rows = parts[number]
-                        owner = ring_device(ring_at + direction * (hops(number, direction) - k))
-                        hop(number, direction, shift, k - 1).wait_recv()
-                        total = rs_buf[owner, rows, :].astype(f32) + rs_in[shift + k - 1, rows, :].astype(f32)
-                        rs_buf[owner, rows, :] = total.astype(bf)
-                    hop(number, direction, shift, k).start()
+                        rows = parts[line[0]]
+                        owner = owner_at(*line, k)
+                        hop(*line, k - 1).wait_recv()
+                        came = rs_in[hop_index(*line, k - 1) % ring_hops, rows, :].astype(f32)
+                        rs_buf[owner, rows, :] = (rs_buf[owner, rows, :].astype(f32) + came).astype(bf)
+                    hop(*line, k).start()
         for number, rows in enumerate(parts):
             total = rs_buf[d, rows, :].astype(f32)
-            for direction, shift in ways:
+            for direction in (1, -1):
                 last = hops(number, direction) - 1
-                hop(number, direction, shift, last).wait_recv()
-                total = total + rs_in[shift + last, rows, :].astype(f32)
+                hop(number, direction, last).wait_recv()
+                total = total + rs_in[hop_index(number, direction, last) % ring_hops, rows, :].astype(f32)
             shared_ref[d, rows, :] = total.astype(bf)
-        for number, direction, shift in lines:
-            for k in range(hops(number, direction)):
-                hop(number, direction, shift, k).wait_send()
-
-    finish(small_out)
+
+    all_here(small_in.at[1:experts], sem_small)
     small_total = small_in[0]
     for k in steps:
         small_total = small_total + small_in[k]
     small_all[d] = small_total
-    small_back = [remote(small_all.at[d], small_all.at[d], sem_back + k, (s, peer[k], t)) for k in steps]
-    for copy in small_back:
-        copy.start()
+    for k in steps:
+        remote(small_all.at[d], small_all.at[d], sem_back, (s, peer[k], t)).start()
 
     sums_copy = remote(small_all, small_sib, sem_sums, sib)
 
     def pass_sums():
-        finish(small_back)
+        all_here(small_all.at[1:experts], sem_back)
         sums_copy.start()
 
 
     streams = [
-        (lambda q, rows=rows: shared_ref.at[q, rows], sem_ring_out + c * experts) for c, rows in enumerate(parts)
+        (lambda q, rows=rows: shared_ref.at[q, rows], sem_ring_out, 0) for rows in parts
     ]
 
     ring_gather(streams, pass_sums)
-    for q in range(experts):
-        pltpu.make_async_copy(shared_ref.at[q], shared_hbm.at[q], osem.at[2 + q]).start()
-    sums_copy.wait()
+    sums_copy.wait_recv()
     for g in range(groups):
         lanes = slice(g * 128, (g + 1) * 128)
         grouter_ref[:, lanes] = small_all[g, 0:experts, :] + small_sib[g, 0:experts, :]
@@ -1288,38 +1244,34 @@
     @pl.when(s == 1)
     def _():
         dy_copy.wait_send()
-        for k in relayed:
-            passed_on(xrows, sem_dx, 0, k).wait_send()
-            passed_on(dyrows, sem_ddy, 1, k).wait_send()
+        for sem in sem_pass:
+            all_sent(relay_buf.at[0 : len(relayed)], sem)
+        all_sent(rs_in, sem_ring_sum)
         wait_back(eob, eoret, sem_re)
         layer_output()
-        hand_out(out_own, secout_ref, sem_so, secout_hbm, 0)
-
-    for copy in sent:
-        copy.wait_send()
-    pltpu.make_async_copy(secout_ref, secout_hbm, osem.at[0]).wait()
-    pltpu.make_async_copy(ingrad_ref, ingrad_hbm, osem.at[1]).wait()
-    for q in range(experts):
-        pltpu.make_async_copy(shared_ref.at[q], shared_hbm.at[q], osem.at[2 + q]).wait()
-    for n in range(ffn // wide):
-        at = slice(n * wide, (n + 1) * wide)
-        pltpu.make_async_copy(guv.at[:, at], gup_ref.at[:, at], gsem.at[n]).wait()
-        pltpu.make_async_copy(gdv.at[at, :], gdown_ref.at[at, :], gsem.at[ffn // wide + n]).wait()
+        hand_out(out_own, secout_ref, sem_so)
+
+    all_sent(rr.at[1:experts], sem_routes)
+    all_sent(eo_send, sem_eo)
+    all_sent(cg_send, sem_cg)
+    all_sent(gg_part.at[0], sem_gg_core)
+    all_sent(small_in.at[1:experts], sem_small)
+    all_sent(small_all.at[1:experts], sem_back)
+    all_sent(small_all, sem_sums)
+    all_sent(shared_ref.at[1:experts], sem_ring_out)
 
 
 def widen_kernel(
     sec_ref, ing_ref, gain_ref, shared_ref, bias_ref, router_ref, up_ref, down_ref,
     sec_out, ing_out, gain_out, bias_out, router_out, qkv_out, out_out, up_out, down_out,
-    up_low, up_wide, down_low, down_wide, shared_low, qkv_wide, out_wide, bias_low, bias_wide,
-    sec_low, ing_low, gain_low, router_low, in_sem, out_sem,
+    up_wide, down_wide, qkv_wide, out_wide, bias_wide, out_sem,
 ):
     f32 = jnp.float32
     parts = 3
     experts, shared_rows, width = shared_ref.shape
     cols = out_wide.shape[0]
     qkv_rows = 3 * cols // experts
-    low = ((up_ref, up_low), (down_ref, down_low))
-    wide = ((up_low, up_wide, up_out), (down_low, down_wide, down_out))
+    wide = ((up_ref, up_wide, up_out), (down_ref, down_wide, down_out))
     stores = []
 
     def store(src, dst):
@@ -1327,52 +1279,36 @@
         copy.start()
         stores.append(copy)
 
-    def rows(ref, n):
-        size = ref.shape[0] // parts
-        return pl.ds(n * size, size)
-
-    load_shared = pltpu.make_async_copy(shared_ref, shared_low, in_sem.at[2 * parts])
-    load_bias = pltpu.make_async_copy(bias_ref, bias_low, in_sem.at[2 * parts + 1])
-    loads = [
-        pltpu.make_async_copy(src.at[rows(src, n)], dst.at[rows(dst, n)], in_sem.at[i * parts + n])
-        for i, (src, dst) in enumerate(low)
-        for n in range(parts)
-    ]
-    loads[0].start()
-    load_shared.start()
-    for copy in loads[1:]:
-        copy.start()
-    load_bias.start()
-    through = ((sec_ref, sec_low, sec_out), (ing_ref, ing_low, ing_out), (gain_ref, gain_low, gain_out), (router_ref, router_low, router_out))
-    passing = [
-        pltpu.make_async_copy(src, mid, in_sem.at[2 * parts + 2 + i]) for i, (src, mid, _) in enumerate(through)
-    ]
-    for copy in passing:
-        copy.start()
-
     def widen(i, n):
-        loads[i * parts + n].wait()
         src, dst, out = wide[i]
-        dst[rows(dst, n), :] = src[rows(src, n), :].astype(f32)
-        store(dst.at[rows(dst, n)], out.at[rows(out, n)])
+        size = src.shape[0] // parts
+        rows = pl.ds(n * size, size)
+        dst[rows, :] = src[rows, :].astype(f32)
+        store(dst.at[rows], out.at[rows])
 
     def turn_qkv(c):
-        block = shared_low[:, 0:qkv_rows, :].reshape(3 * cols, width)[c * cols : (c + 1) * cols]
+        block = shared_ref[:, 0:qkv_rows, :].reshape(3 * cols, width)[c * cols : (c + 1) * cols]
         qkv_wide[c] = jnp.transpose(block.astype(f32))
         store(qkv_wide.at[c], qkv_out.at[c])
 
     widen(0, 0)
-    load_shared.wait()
+    store(sec_ref, sec_out)
+    store(ing_ref, ing_out)
+    store(gain_ref, gain_out)
+    store(router_ref, router_out)
+    for h in range(bias_wide.shape[0]):
+        bias_wide[h] = bias_ref[h : h + 1, 0 : bias_wide.shape[2]]
+    store(bias_wide, bias_out)
+    widen(0, 1)
     turn_qkv(0)
-    widen(0, 1)
     widen(0, 2)
     turn_qkv(1)
     widen(1, 0)
+    turn_qkv(2)
     widen(1, 1)
-    turn_qkv(2)
     out_block = jnp.concatenate(
         [
-            shared_low[e, qkv_rows:, h * cols : (h + 1) * cols].astype(f32)
+            shared_ref[e, qkv_rows:, h * cols : (h + 1) * cols].astype(f32)
             for e in range(experts)
             for h in range(2)
         ],
@@ -1381,13 +1317,6 @@
     out_wide[...] = jnp.transpose(out_block)
     store(out_wide, out_out)
     widen(1, 2)
-    for copy, (_, mid, out) in zip(passing, through):
-        copy.wait()
-        store(mid, out)
-    load_bias.wait()
-    for h in range(bias_wide.shape[0]):
-        bias_wide[h] = bias_low[h : h + 1, 0 : bias_wide.shape[2]]
-    store(bias_wide, bias_out)
     for copy in stores:
         copy.wait()
 
@@ -1421,7 +1350,8 @@
     lay.cap = cap
     lay.buckets = rel_bias.shape[1]
     lay.wide = min(ffn, 256)
-    lay.sems = 28 * experts + 12 + experts // 2
+    chunks = experts // 2
+    lay.sems = (34, 7 * chunks + experts + 8 * (experts - 1) + 22)
     bf = jnp.bfloat16
     f32 = jnp.float32
     vm = pltpu.VMEM
@@ -1480,8 +1410,6 @@
         vm((length, width), bf),
         vm((length, width), f32),
         vm((length, width), bf),
-        vm((width, ffn), bf),
-        vm((ffn, width), bf),
         vm((micro, experts, length, width), bf),
         vm((experts, micro, length, cols), bf),
         vm((3 * cols, micro * length), bf),
@@ -1492,41 +1420,35 @@
         vm((experts, 2 * experts, 128), f32),
         vm((experts, 2 * experts, 128), f32),
         vm((experts, 2 * experts, 128), f32),
-        vm((micro, length, width // 2), f32),
-        vm((micro, length, width // 2), f32),
-        vm((experts, shared_rows, width), bf),
         vm((length, width), bf),
         vm((experts, shared_rows, width), bf),
-        vm((experts, shared_rows, width), bf),
-        vm((shared_rows, width), bf),
+        vm((experts - 1, shared_rows, width), bf),
         vm((4, cap, width), bf),
         dma((5,)),
-        dma((2 * (ffn // lay.wide),)),
-        dma((experts + 2,)),
-        dma((lay.sems,)),
-        dma((lay.sems,)),
+        dma((lay.sems[0],)),
+        dma((lay.sems[1],)),
     ]
     whole = pl.BlockSpec(memory_space=pltpu.VMEM)
     anywhere = pl.BlockSpec(memory_space=pl.ANY)
     out_shape = (
-        shape((micro, length, width // 2), f32),
-        shape((micro, length, width // 2), f32),
-        shape((2, width), f32),
-        shape((experts, shared_rows, width), bf),
-        shape((heads, 128), f32),
-        shape((experts, width), f32),
-        shape((width, ffn), bf),
-        shape((ffn, width), bf),
+        vm((micro, length, width // 2), f32),
+        vm((micro, length, width // 2), f32),
+        vm((2, width), f32),
+        vm((experts, shared_rows, width), bf),
+        vm((heads, 128), f32),
+        vm((experts, width), f32),
+        vm((width, ffn), bf),
+        vm((ffn, width), bf),
     )
     results = pl.pallas_call(
         partial(layer_kernel, lay),
         out_shape=out_shape,
         in_specs=[anywhere] * 2 + [whole] * 5 + [anywhere] * 2 + [whole] * 2 + [anywhere] * 2,
-        out_specs=[anywhere] * 2 + [whole, anywhere, whole, whole] + [anywhere] * 2,
+        out_specs=[whole] * 8,
         scratch_shapes=scratch,
         name="two_sections",
         compiler_params=pltpu.CompilerParams(
-            collective_id=0, has_side_effects=True, vmem_limit_bytes=60 * 1024 * 1024
+            collective_id=0, has_side_effects=True, vmem_limit_bytes=54 * 1024 * 1024
         ),
     )(
         tokens[:, 0],
@@ -1546,38 +1468,29 @@
     section_out, input_grads, gains, bias, router, qkv, out, up, down = pl.pallas_call(
         widen_kernel,
         out_shape=(
-            out_shape[0],
-            out_shape[1],
-            out_shape[2],
+            shape((micro, length, width // 2), f32),
+            shape((micro, length, width // 2), f32),
+            shape((2, width), f32),
             shape((heads, 1, lay.buckets), f32),
-            out_shape[5],
+            shape((experts, width), f32),
             shape((3, width, cols), f32),
             shape((cols, width), f32),
             shape((width, ffn), f32),
             shape((ffn, width), f32),
         ),
-        in_specs=[anywhere] * 8,
+        in_specs=[whole] * 8,
         out_specs=[anywhere] * 9,
         scratch_shapes=[
-            vm((width, ffn), bf),
             vm((width, ffn), f32),
-            vm((ffn, width), bf),
             vm((ffn, width), f32),
-            vm((experts, shared_rows, width), bf),
             vm((3, width, cols), f32),
             vm((cols, width), f32),
-            vm((heads, 128), f32),
             vm((heads, 1, lay.buckets), f32),
-            vm((micro, length, width // 2), f32),
-            vm((micro, length, width // 2), f32),
-            vm((2, width), f32),
-            vm((experts, width), f32),
-            dma((12,)),
             dma((15,)),
         ],
         name="widen",
-        compiler_params=pltpu.CompilerParams(vmem_limit_bytes=60 * 1024 * 1024),
-    )(*results)
+        compiler_params=pltpu.CompilerParams(vmem_limit_bytes=40 * 1024 * 1024),
+    )(*[pltpu.with_memory_space_constraint(result, pltpu.VMEM) for result in results])
     return (
         section_out[None, :, None],
         input_grads[None, :, None],

time: 182 us -> 174 us (0.956)
  Pallas kernels: 181 us -> 173 us
    pallas_call x1, Pallas kernels: 173 us -> 168 us  [fused_local(): pl.pallas_call(partial(layer_kernel, lay), out_shape=out_shape, in_specs=...]
where the time goes in v5:
time: 174 us
  Pallas kernels  173 us (99%)
    pallas_call x1, Pallas kernels, fused_local(): pl.pallas_call(partial(layer_kernel, lay), out_shape=out_shape, in_specs=...  168 us
    pallas_call x1, Pallas kernels, fused_local(): pl.pallas_call(widen_kernel, out_shape=(shape((micro, length, width // 2)...  5.76 us

profile of v5, /device:TPU:0, one launch (start us, length us, event | category | flops | bytes accessed | tf_op | source)
XLA Modules:
  0.0 174.2 jit_solution(1859877204391941663)
XLA Ops:
  0.6 167.6 %two_sections.1 = (f32[2,128,384]{2,1,0:T(8,128)S(1)}, f32[2,128,384]{2,1,0:T(8,128)S(1)}, f32[2,768]{1,0:T(2,128)S(1)}, bf16[8,192,768]{2,1,0:T(8,128)(2,1)S(1)...) custom-call(bf16[2,128,768]{2,1,0:T(8,128)(2,1)} %bitcast.42, ...), custom_call_target="tpu_custom_call" | custom-call | tf_op jit(solution)/shard_map/two_sections/pallas_call | solution.py:1443
  168.2 5.8 %widen.1 = (f32[2,128,384]{2,1,0:T(8,128)}, f32[2,128,384]{2,1,0:T(8,128)}, f32[2,768]{1,0:T(2,128)}, f32[6,1,32]{2,1,0:T(1,128)}, f32[8,768]{1,0:T(8,128)}, /*i...) custom-call(f32[2,128,384]{2,1,0:T(8,128)S(1)} %get-tuple-element.26.sec_ref, ...), custom_call_target="tpu_custom_call" | custom-call | tf_op jit(solution)/shard_map/widen/pallas_call | solution.py:1468

commit v6 on v5

--- a/solution.py
+++ b/solution.py
@@ -393,15 +393,15 @@
 
 def layer_kernel(lay, *refs):
     (
-        tok_ref, cot_ref, seg_ref, pad_ref, routes_ref, dist_ref, gains_ref, qkvw_hbm, outw_hbm, relb_ref, wr_ref,
+        tok_ref, cot_ref, seg_hbm, pad_hbm, routes_hbm, dist_hbm, gains_hbm, qkvw_hbm, outw_hbm, relb_hbm, wr_hbm,
         up_ref, down_ref,
         secout_ref, ingrad_ref, ggain_ref, shared_ref, gbias_ref, grouter_ref, guv, gdv,
-        upv, downv, qkvw_ref, outw_ref, xb, dyb, rr, place, bias_buf, probs_buf, no1, qkvb, mixed, att_send, att_recv, mid, ntb,
+        seg_ref, pad_ref, routes_ref, dist_ref, gains_ref, relb_ref, wr_ref, upv, downv, upt, downt, qkvwt, outwt, qkvw_ref, outw_ref, xb, dyb, rr, place, bias_buf, probs_buf, no1, qkvb, mixed, att_send, att_recv, mid, ntb,
         gate_t, hit_t, wrp, score_sum, disp_x, xrows, disp_y, dyrows, hidden, dgelu, halves, eo_send, eo_recv, eob, eoret, out_own,
         other, og, gg_part, gg_other, gg_send, gg_recv, pg, cg_send, cg_recv, cgb, cgret, mgrad, ag, mg, qkvg,
         no_send, no_recv, ig_own, dy_send,
         no_all, mix_all, qgt, qt_all, agt, agt_all, small_send, small_in, small_all, small_sib,
-        x_send, rs_buf, rs_in, relay_buf,
+        x_send, rs_buf, rs_in, relay_buf, relay_q,
         wsem, ss, rs,
     ) = refs
     bf = jnp.bfloat16
@@ -470,6 +470,8 @@
     sem_x = take()
     sem_relay = [take(len(relayed)) for _ in range(2)]
     sem_pass = [take(0) for _ in range(2)]
+    sem_relay_q = take(len(relayed))
+    sem_pass_q = take(0)
     sem_xf = take()
     sem_dy = take()
     sem_att = take()
@@ -549,6 +551,22 @@
             if hops(*line) > short:
                 hop(*line, short).wait_recv()
 
+    small_loads = [
+        pltpu.make_async_copy(src, dst, wsem.at[5 + i])
+        for i, (src, dst) in enumerate(
+            (
+                (routes_hbm, routes_ref),
+                (wr_hbm, wr_ref),
+                (seg_hbm, seg_ref),
+                (pad_hbm, pad_ref),
+                (dist_hbm, dist_ref),
+                (gains_hbm, gains_ref),
+                (relb_hbm, relb_ref),
+            )
+        )
+    ]
+    for copy in small_loads:
+        copy.start()
     load_up = pltpu.make_async_copy(up_ref, upv, wsem.at[0])
     load_down = pltpu.make_async_copy(down_ref, downv, wsem.at[1])
     load_qkvw = pltpu.make_async_copy(qkvw_hbm, qkvw_ref, wsem.at[2])
@@ -573,9 +591,12 @@
     for k in steps:
         pl.semaphore_signal(barrier, inc=1, device_id=(s, peer[k], t), device_id_type=pl.DeviceIdType.MESH)
     pl.semaphore_signal(barrier, inc=1, device_id=sib, device_id_type=pl.DeviceIdType.MESH)
-    for k in range(experts):
+    for k in (0,) + relayed:
         pl.semaphore_signal(barrier, inc=1, device_id=(1 - s, peer[k], t), device_id_type=pl.DeviceIdType.MESH)
-    pl.semaphore_wait(barrier, 2 * experts)
+    pl.semaphore_wait(barrier, experts + 1 + len(relayed))
+
+    for copy in small_loads:
+        copy.wait()
 
     for k in steps:
         remote(routes_ref, rr.at[k], sem_routes, (s, peer[k], t)).start()
@@ -688,6 +709,13 @@
         finish_chunk(last)
         drain(zero)
 
+    def turn_weights():
+        upt[...] = jnp.transpose(upv[...])
+        downt[...] = jnp.transpose(downv[...])
+        for c in range(3):
+            qkvwt[c] = jnp.transpose(qkvw_ref[c])
+        outwt[...] = jnp.transpose(outw_ref[...])
+
     def other_experts():
         all_here(rr.at[1:experts], sem_routes)
 
@@ -710,11 +738,18 @@
     @pl.when(s == 0)
     def _():
         load_tok.wait()
+        load_qkvw.wait()
+        load_outw.wait()
 
     @pl.when(s == 1)
     def _():
         load_cot.wait()
         relay(xrows, sem_dx, 0)
+        load_up.wait()
+        load_down.wait()
+        load_qkvw.wait()
+        load_outw.wait()
+        turn_weights()
         other_experts()
         arrive, joined, drain = dispatch(dyb[...], disp_y, dyrows, sem_ddy, sem_ddyf)
 
@@ -768,8 +803,6 @@
         x_copy.wait_recv()
         x_forward.start()
 
-    load_qkvw.wait()
-    load_outw.wait()
     gain_one = gains_ref[0:1, :].astype(f32)
     gain_two = gains_ref[1:2, :].astype(f32)
     low_lanes = lax.broadcasted_iota(jnp.int32, (length, 128), 1) < 64
@@ -833,8 +866,6 @@
     gate_t[...] = terms / jnp.sum(terms, axis=0, keepdims=True)
 
     arrivals = dispatch(ntb[...], disp_x, xrows, sem_dx, sem_dxf, 0, True)
-    load_up.wait()
-    load_down.wait()
     rows_of = 2 * micro * cap
 
     def flat(ref, chunk):
@@ -890,7 +921,7 @@
         gate = 1.0 / (1.0 + jnp.exp(other_logit - own_logit))
         dy_flat = flat(dyrows, pair(c))
         og[pair(c)] = (dy_flat.astype(f32) * gate).astype(bf).reshape(2, micro, cap, width)
-        grad = nt(dy_flat, downv[...])
+        grad = nn(dy_flat, downt[...])
         pg[pair(c)] = (grad * gate * flat(dgelu, pair(c)).astype(f32)).astype(bf).reshape(2, micro, cap, ffn)
         product = (grad * flat(hidden, pair(c)).astype(f32)).astype(bf)
         for i in range(2):
@@ -900,7 +931,7 @@
 
     def back_chunk(c):
         remote(gg_part.at[u, pair(c)], gg_other.at[pair(c)], sem_gg_core, sib, c).start()
-        split_sum(c, nt(flat(pg, pair(c)), upv[...]), cg_send, cg_recv, sem_cg)
+        split_sum(c, nn(flat(pg, pair(c)), upt[...]), cg_send, cg_recv, sem_cg)
 
     def both_chunk(c):
         front_chunk(c)
@@ -976,11 +1007,14 @@
 
     @pl.when(s == 0)
     def _():
+        load_up.wait()
+        load_down.wait()
         stream(arrivals, front_chunk, rows_chunk, rows_finish, True, True)
         wait_back(eob, eoret, sem_re)
         x_send[...] = layer_output().astype(bf)
         x_copy.start()
         hand_out(out_own, secout_ref, sem_so)
+        turn_weights()
         other_experts()
         gather_factors()
         x_copy.wait_send()
@@ -1039,8 +1073,10 @@
         agt_all[d, t] = agt[block(d, agt_rows), :]
         agt_own.start()
 
-    def attend_back(m, lane_of_m):
-        mg[m] = nt(ag[m], outw_ref[...]).astype(bf)
+    qgt_rows = 3 * cols // experts
+
+    def attend_back(m, i):
+        mg[m] = nn(ag[m], outwt[...]).astype(bf)
         for p in range(pairs):
             at = slice(p * 128, (p + 1) * 128)
             mg_pair = mg[m, :, at]
@@ -1069,7 +1105,11 @@
         @pl.when(s == 0)
         def _():
             for c in range(3):
-                qgt[c * cols : (c + 1) * cols, lane_of_m] = jnp.transpose(qkvg[c, m])
+                qgt[i, c * cols : (c + 1) * cols, :] = jnp.transpose(qkvg[c, m])
+            for k in reversed([k for k in steps if k not in relayed]):
+                rows = block(peer[k], qgt_rows)
+                remote(qgt.at[i, rows], qt_all.at[d, i], sem_qgt, (s, peer[k], t), k).start()
+            qt_all[d, i] = qgt[i, block(d, qgt_rows), :]
 
     score_sum[...] = jnp.zeros_like(score_sum)
 
@@ -1078,21 +1118,24 @@
         def _():
             ag_copy.wait()
 
-        attend_back(t + i * (u - t), pl.ds(pl.multiple_of(i * length, length), length))
+        attend_back(t + i * (u - t), i)
         return carry
 
     lax.fori_loop(0, micro, back_one, 0)
-    qgt_rows = 3 * cols // experts
+
+    def relay_q_copy(i, k):
+        return remote(qgt.at[:, block(peer[k], qgt_rows)], relay_q.at[i], sem_relay_q, across, i)
+
     @pl.when(s == 0)
     def _():
-        for k in reversed(steps):
-            remote(qgt.at[block(peer[k], qgt_rows)], qt_all.at[d], sem_qgt, (s, peer[k], t), k).start()
-        qt_all[d] = qgt[block(d, qgt_rows), :]
+        for i, k in enumerate(relayed):
+            relay_q_copy(i, k).start()
+
 
     def project_back(m):
-        total = nt(qkvg[0, m], qkvw_ref[0])
+        total = nn(qkvg[0, m], qkvwt[0])
         for c in range(1, 3):
-            total = total + nt(qkvg[c, m], qkvw_ref[c])
+            total = total + nn(qkvg[c, m], qkvwt[c])
         return total
 
     no_send[...] = project_back(u).astype(bf)
@@ -1164,13 +1207,15 @@
         shared_ref[d, qkv_rows:, :] = pack_out(total)
 
         def qkv_slice(q):
-            return nn(qt_all[q], jnp.concatenate([no_all[t, q], no_all[u, q]], axis=0))
+            rows = jnp.concatenate([qt_all[q, 0], qt_all[q, 1]], axis=1)
+            return nn(rows, jnp.concatenate([no_all[t, q], no_all[u, q]], axis=0))
 
         total = qkv_slice(d)
-        for k in reversed(steps):
+        for k in [k for k in reversed(steps) if k not in relayed] + list(relayed):
             all_here(qt_all.at[0], sem_qgt, k)
             total = total + qkv_slice(peer[k])
-        all_sent(qt_all.at[1:experts], sem_qgt)
+        all_sent(qt_all.at[0 : experts - 1 - len(relayed)], sem_qgt)
+        all_sent(relay_q, sem_relay_q)
         shared_ref[d, 0:qkv_rows, :] = total.astype(bf)
 
     @pl.when(s == 1)
@@ -1214,6 +1259,9 @@
                 hop(number, direction, last).wait_recv()
                 total = total + rs_in[hop_index(number, direction, last) % ring_hops, rows, :].astype(f32)
             shared_ref[d, rows, :] = total.astype(bf)
+        for i, k in enumerate(relayed):
+            all_here(relay_q.at[i], sem_relay_q, i)
+            remote(relay_q.at[i], qt_all.at[d], (sem_pass_q[0], sem_qgt[1] + k), (0, peer[k], t)).start()
 
     all_here(small_in.at[1:experts], sem_small)
     small_total = small_in[0]
@@ -1247,6 +1295,7 @@
         for sem in sem_pass:
             all_sent(relay_buf.at[0 : len(relayed)], sem)
         all_sent(rs_in, sem_ring_sum)
+        all_sent(relay_q, sem_pass_q)
         wait_back(eob, eoret, sem_re)
         layer_output()
         hand_out(out_own, secout_ref, sem_so)
@@ -1267,7 +1316,7 @@
     up_wide, down_wide, qkv_wide, out_wide, bias_wide, out_sem,
 ):
     f32 = jnp.float32
-    parts = 3
+    parts = 6
     experts, shared_rows, width = shared_ref.shape
     cols = out_wide.shape[0]
     qkv_rows = 3 * cols // experts
@@ -1291,21 +1340,25 @@
         qkv_wide[c] = jnp.transpose(block.astype(f32))
         store(qkv_wide.at[c], qkv_out.at[c])
 
-    widen(0, 0)
     store(sec_ref, sec_out)
     store(ing_ref, ing_out)
+    widen(0, 0)
     store(gain_ref, gain_out)
     store(router_ref, router_out)
     for h in range(bias_wide.shape[0]):
         bias_wide[h] = bias_ref[h : h + 1, 0 : bias_wide.shape[2]]
     store(bias_wide, bias_out)
     widen(0, 1)
+    widen(0, 2)
     turn_qkv(0)
-    widen(0, 2)
+    widen(0, 3)
+    widen(0, 4)
     turn_qkv(1)
+    widen(0, 5)
     widen(1, 0)
     turn_qkv(2)
     widen(1, 1)
+    widen(1, 2)
     out_block = jnp.concatenate(
         [
             shared_ref[e, qkv_rows:, h * cols : (h + 1) * cols].astype(f32)
@@ -1316,7 +1369,9 @@
     )
     out_wide[...] = jnp.transpose(out_block)
     store(out_wide, out_out)
-    widen(1, 2)
+    widen(1, 3)
+    widen(1, 4)
+    widen(1, 5)
     for copy in stores:
         copy.wait()
 
@@ -1351,15 +1406,26 @@
     lay.buckets = rel_bias.shape[1]
     lay.wide = min(ffn, 256)
     chunks = experts // 2
-    lay.sems = (34, 7 * chunks + experts + 8 * (experts - 1) + 22)
+    lay.sems = (36, 7 * chunks + experts + 8 * (experts - 1) + 24)
     bf = jnp.bfloat16
     f32 = jnp.float32
     vm = pltpu.VMEM
     shape = jax.ShapeDtypeStruct
     dma = pltpu.SemaphoreType.DMA
     scratch = [
+        vm((micro, length), jnp.int32),
+        vm((micro, length), jnp.int32),
+        vm((micro, 2, length), jnp.int32),
+        vm((1, length), jnp.int32),
+        vm((2, width), bf),
+        vm((heads, lay.buckets), bf),
+        vm((experts, width), bf),
         vm((width, ffn), bf),
         vm((ffn, width), bf),
+        vm((ffn, width), bf),
+        vm((width, ffn), bf),
+        vm((3, cols, width), bf),
+        vm((width, cols), bf),
         vm((3, width, cols), bf),
         vm((cols, width), bf),
         vm((micro, length, width), bf),
@@ -1412,8 +1478,8 @@
         vm((length, width), bf),
         vm((micro, experts, length, width), bf),
         vm((experts, micro, length, cols), bf),
-        vm((3 * cols, micro * length), bf),
-        vm((experts, 3 * cols // experts, micro * length), bf),
+        vm((micro, 3 * cols, length), bf),
+        vm((experts, micro, 3 * cols // experts, length), bf),
         vm((width, length), bf),
         vm((experts, micro, width // experts, length), bf),
         vm((experts, 2 * experts, 128), f32),
@@ -1424,7 +1490,8 @@
         vm((experts, shared_rows, width), bf),
         vm((experts - 1, shared_rows, width), bf),
         vm((4, cap, width), bf),
-        dma((5,)),
+        vm((2, micro, 3 * cols // experts, length), bf),
+        dma((12,)),
         dma((lay.sems[0],)),
         dma((lay.sems[1],)),
     ]
@@ -1443,12 +1510,12 @@
     results = pl.pallas_call(
         partial(layer_kernel, lay),
         out_shape=out_shape,
-        in_specs=[anywhere] * 2 + [whole] * 5 + [anywhere] * 2 + [whole] * 2 + [anywhere] * 2,
+        in_specs=[anywhere] * 13,
         out_specs=[whole] * 8,
         scratch_shapes=scratch,
         name="two_sections",
         compiler_params=pltpu.CompilerParams(
-            collective_id=0, has_side_effects=True, vmem_limit_bytes=54 * 1024 * 1024
+            collective_id=0, has_side_effects=True, vmem_limit_bytes=55 * 1024 * 1024
         ),
     )(
         tokens[:, 0],
@@ -1486,7 +1553,7 @@
             vm((3, width, cols), f32),
             vm((cols, width), f32),
             vm((heads, 1, lay.buckets), f32),
-            dma((15,)),
+            dma((21,)),
         ],
         name="widen",
         compiler_params=pltpu.CompilerParams(vmem_limit_bytes=40 * 1024 * 1024),

time: 174 us -> 165 us (0.948)
  Pallas kernels: 173 us -> 164 us
    pallas_call x1, Pallas kernels: 168 us -> 159 us  [fused_local(): pl.pallas_call(partial(layer_kernel, lay), out_shape=out_shape, in_specs=...]
where the time goes in v6:
time: 165 us
  Pallas kernels  164 us (99%)
    pallas_call x1, Pallas kernels, fused_local(): pl.pallas_call(partial(layer_kernel, lay), out_shape=out_shape, in_specs=...  159 us
    pallas_call x1, Pallas kernels, fused_local(): pl.pallas_call(widen_kernel, out_shape=(shape((micro, length, width // 2)...  5.46 us

profile of v6, /device:TPU:0, one launch (start us, length us, event | category | flops | bytes accessed | tf_op | source)
XLA Modules:
  0.0 165.1 jit_solution(9707670572307047922)
XLA Ops:
  0.6 158.8 %two_sections.1 = (f32[2,128,384]{2,1,0:T(8,128)S(1)}, f32[2,128,384]{2,1,0:T(8,128)S(1)}, f32[2,768]{1,0:T(2,128)S(1)}, bf16[8,192,768]{2,1,0:T(8,128)(2,1)S(1)...) custom-call(bf16[2,128,768]{2,1,0:T(8,128)(2,1)} %bitcast.42, ...), custom_call_target="tpu_custom_call" | custom-call | tf_op jit(solution)/shard_map/two_sections/pallas_call | solution.py:1510
  159.5 5.5 %widen.1 = (f32[2,128,384]{2,1,0:T(8,128)}, f32[2,128,384]{2,1,0:T(8,128)}, f32[2,768]{1,0:T(2,128)}, f32[6,1,32]{2,1,0:T(1,128)}, f32[8,768]{1,0:T(8,128)}, /*i...) custom-call(f32[2,128,384]{2,1,0:T(8,128)S(1)} %get-tuple-element.26.sec_ref, ...), custom_call_target="tpu_custom_call" | custom-call | tf_op jit(solution)/shard_map/widen/pallas_call | solution.py:1535

commit v7 on v6

--- a/solution.py
+++ b/solution.py
@@ -398,7 +398,7 @@
         secout_ref, ingrad_ref, ggain_ref, shared_ref, gbias_ref, grouter_ref, guv, gdv,
         seg_ref, pad_ref, routes_ref, dist_ref, gains_ref, relb_ref, wr_ref, upv, downv, upt, downt, qkvwt, outwt, qkvw_ref, outw_ref, xb, dyb, rr, place, bias_buf, probs_buf, no1, qkvb, mixed, att_send, att_recv, mid, ntb,
         gate_t, hit_t, wrp, score_sum, disp_x, xrows, disp_y, dyrows, hidden, dgelu, halves, eo_send, eo_recv, eob, eoret, out_own,
-        other, og, gg_part, gg_other, gg_send, gg_recv, pg, cg_send, cg_recv, cgb, cgret, mgrad, ag, mg, qkvg,
+        other, gate_slots, og, gg_part, gg_other, gg_send, gg_recv, pg, cg_send, cg_recv, cgb, cgret, mgrad, ag, mg, qkvg,
         no_send, no_recv, ig_own, dy_send,
         no_all, mix_all, qgt, qt_all, agt, agt_all, small_send, small_in, small_all, small_sib,
         x_send, rs_buf, rs_in, relay_buf, relay_q,
@@ -832,7 +832,7 @@
     att_copy = remote(att_send, att_recv, sem_att, sib)
 
     def project_other():
-        att_send[...] = nn(mixed[u], outw_ref[...])
+        att_send[...] = nn(mixed[u], outw_ref[...]).astype(bf)
         att_copy.start()
 
     begin = u + s * (t - u)
@@ -858,14 +858,14 @@
 
     part_own = nn(mixed[t], outw_ref[...])
     att_copy.wait()
-    middle = xb[t].astype(f32) + part_own + att_recv[...]
+    middle = xb[t].astype(f32) + part_own + att_recv[...].astype(f32)
     mid[...] = middle
     ntb[...] = (middle * inverse_rms(middle) * gain_two).astype(bf)
+
+    arrivals = dispatch(ntb[...], disp_x, xrows, sem_dx, sem_dxf, 0, True)
     logits_t = jnp.where(hit_t[...] > 0.0, nt(wrp[...], ntb[...]), masked_score)
     terms = jnp.exp(logits_t - jnp.max(logits_t, axis=0, keepdims=True))
     gate_t[...] = terms / jnp.sum(terms, axis=0, keepdims=True)
-
-    arrivals = dispatch(ntb[...], disp_x, xrows, sem_dx, sem_dxf, 0, True)
     rows_of = 2 * micro * cap
 
     def flat(ref, chunk):
@@ -914,13 +914,16 @@
     ones = jnp.ones((8, ffn), bf)
     gg_part[...] = jnp.zeros_like(gg_part)
 
-    def slope_chunk(c):
+    def gate_chunk(c):
         slot_logits = nt(flat(xrows, pair(c)), wr_ref[...])
         own_logit = jnp.sum(slot_logits * mine_hot, axis=-1, keepdims=True)
         other_logit = jnp.sum(slot_logits * flat(other, pair(c)), axis=-1, keepdims=True)
         gate = 1.0 / (1.0 + jnp.exp(other_logit - own_logit))
+        gate_slots[pair(c)] = gate.reshape(2, micro, cap, 1)
+
+    def slope_chunk(c):
         dy_flat = flat(dyrows, pair(c))
-        og[pair(c)] = (dy_flat.astype(f32) * gate).astype(bf).reshape(2, micro, cap, width)
+        gate = flat(gate_slots, pair(c))
         grad = nn(dy_flat, downt[...])
         pg[pair(c)] = (grad * gate * flat(dgelu, pair(c)).astype(f32)).astype(bf).reshape(2, micro, cap, ffn)
         product = (grad * flat(hidden, pair(c)).astype(f32)).astype(bf)
@@ -935,6 +938,7 @@
 
     def both_chunk(c):
         front_chunk(c)
+        gate_chunk(c)
         slope_chunk(c)
 
     def back_finish(c):
@@ -1016,6 +1020,12 @@
         hand_out(out_own, secout_ref, sem_so)
         turn_weights()
         other_experts()
+
+        def gate_one(c, carry):
+            gate_chunk(c)
+            return carry
+
+        lax.fori_loop(0, len(chunks), gate_one, 0)
         gather_factors()
         x_copy.wait_send()
         dy_copy.wait_recv()
@@ -1043,18 +1053,11 @@
     gate_grad = jnp.concatenate(gg_rows, axis=0)
     gates = gate_t[...]
     logit_grad = (gates * (gate_grad - jnp.sum(gates * gate_grad, axis=0, keepdims=True))).astype(bf)
-    router_grad = nn(tn(turn, logit_grad).astype(bf), ntb[...])
     two_grad = tn(logit_grad, wrp[...]) + tn(place[...], cgret[...].reshape(slots, width))
     dy = dyb[...].astype(f32)
     middle = mid[...]
     scale = inverse_rms(middle)
     normed = middle * scale
-    gain_two_grad = jnp.sum(two_grad * normed, axis=0, keepdims=True)
-    groups = width // 128
-    small_send[...] = jnp.zeros_like(small_send)
-    for g in range(groups):
-        small_send[g, 0:experts, :] = router_grad[:, g * 128 : (g + 1) * 128]
-        small_send[g, experts + 1 : experts + 2, :] = gain_two_grad[:, g * 128 : (g + 1) * 128]
     scaled = two_grad * gain_two
     middle_grad = dy + scale * (scaled - normed * jnp.mean(scaled * normed, axis=-1, keepdims=True))
     mgrad[...] = middle_grad
@@ -1073,6 +1076,8 @@
         agt_all[d, t] = agt[block(d, agt_rows), :]
         agt_own.start()
 
+    two_normed = normed
+    groups = width // 128
     qgt_rows = 3 * cols // experts
 
     def attend_back(m, i):
@@ -1147,18 +1152,24 @@
     x_rows = xb[t].astype(f32)
     scale = inverse_rms(x_rows)
     normed = x_rows * scale
-    gain_one_grad = jnp.sum(one_grad * normed, axis=0, keepdims=True)
     scaled = one_grad * gain_one
     input_grad = mgrad[...] + scale * (scaled - normed * jnp.mean(scaled * normed, axis=-1, keepdims=True))
-    ig_own[...] = input_grad
     dy_send[...] = input_grad.astype(bf)
 
     @pl.when(s == 1)
     def _():
         dy_copy.start()
 
+    ig_own[...] = input_grad
+    gain_one_grad = jnp.sum(one_grad * normed, axis=0, keepdims=True)
     hand_out(ig_own, ingrad_ref, sem_ig)
 
+    router_grad = nn(tn(turn, logit_grad).astype(bf), ntb[...])
+    gain_two_grad = jnp.sum(two_grad * two_normed, axis=0, keepdims=True)
+    small_send[...] = jnp.zeros_like(small_send)
+    for g in range(groups):
+        small_send[g, 0:experts, :] = router_grad[:, g * 128 : (g + 1) * 128]
+        small_send[g, experts + 1 : experts + 2, :] = gain_two_grad[:, g * 128 : (g + 1) * 128]
     sums = []
     for head in range(2 * pairs):
         high, low = split_low(score_sum[head])
@@ -1174,6 +1185,9 @@
 
     wide = lay.wide
     every = micro * slots
+
+    for k in range(experts):
+        og[k] = (dyrows[k].astype(f32) * gate_slots[k]).astype(bf)
 
     def expert_grads(n, carry):
         at = pl.ds(pl.multiple_of(n * wide, wide), wide)
@@ -1437,8 +1451,8 @@
         vm((micro, length, width), bf),
         vm((3, micro, length, cols), bf),
         vm((micro, length, cols), bf),
-        vm((length, width), f32),
-        vm((length, width), f32),
+        vm((length, width), bf),
+        vm((length, width), bf),
         vm((length, width), f32),
         vm((length, width), bf),
         vm((experts, length), f32),
@@ -1458,6 +1472,7 @@
         vm((experts, cap, width), bf),
         vm((length, width), f32),
         vm((experts, micro, cap, experts), f32),
+        vm((experts, micro, cap, 1), f32),
         vm((experts, micro, cap, width), bf),
         vm((micro, experts, 8, 128), f32),
         vm((experts, 8, 128), f32),
@@ -1515,7 +1530,7 @@
         scratch_shapes=scratch,
         name="two_sections",
         compiler_params=pltpu.CompilerParams(
-            collective_id=0, has_side_effects=True, vmem_limit_bytes=55 * 1024 * 1024
+            collective_id=0, has_side_effects=True, vmem_limit_bytes=56 * 1024 * 1024
         ),
     )(
         tokens[:, 0],

time: 165 us -> 164 us (level)
  no operation moved by 1% of the time
where the time goes in v7:
time: 164 us
  Pallas kernels  163 us (99%)
    pallas_call x1, Pallas kernels, fused_local(): pl.pallas_call(partial(layer_kernel, lay), out_shape=out_shape, in_specs=...  158 us
    pallas_call x1, Pallas kernels, fused_local(): pl.pallas_call(widen_kernel, out_shape=(shape((micro, length, width // 2)...  5.46 us

profile of v7, /device:TPU:0, one launch (start us, length us, event | category | flops | bytes accessed | tf_op | source)
XLA Modules:
  0.0 163.8 jit_solution(5790191174522165388)
XLA Ops:
  0.6 157.5 %two_sections.1 = (f32[2,128,384]{2,1,0:T(8,128)S(1)}, f32[2,128,384]{2,1,0:T(8,128)S(1)}, f32[2,768]{1,0:T(2,128)S(1)}, bf16[8,192,768]{2,1,0:T(8,128)(2,1)S(1)...) custom-call(bf16[2,128,768]{2,1,0:T(8,128)(2,1)} %bitcast.42, ...), custom_call_target="tpu_custom_call" | custom-call | tf_op jit(solution)/shard_map/two_sections/pallas_call | solution.py:1525
  158.2 5.5 %widen.1 = (f32[2,128,384]{2,1,0:T(8,128)}, f32[2,128,384]{2,1,0:T(8,128)}, f32[2,768]{1,0:T(2,128)}, f32[6,1,32]{2,1,0:T(1,128)}, f32[8,768]{1,0:T(8,128)}, /*i...) custom-call(f32[2,128,384]{2,1,0:T(8,128)S(1)} %get-tuple-element.26.sec_ref, ...), custom_call_target="tpu_custom_call" | custom-call | tf_op jit(solution)/shard_map/widen/pallas_call | solution.py:1550

commit v8 on v7

--- a/solution.py
+++ b/solution.py
@@ -1118,15 +1118,9 @@
 
     score_sum[...] = jnp.zeros_like(score_sum)
 
-    def back_one(i, carry):
-        @pl.when(i == 1)
-        def _():
-            ag_copy.wait()
-
-        attend_back(t + i * (u - t), i)
-        return carry
-
-    lax.fori_loop(0, micro, back_one, 0)
+    attend_back(t, 0)
+    ag_copy.wait()
+    attend_back(u, 1)
 
     def relay_q_copy(i, k):
         return remote(qgt.at[:, block(peer[k], qgt_rows)], relay_q.at[i], sem_relay_q, across, i)

time: 164 us -> 164 us (level)
  no operation moved by 1% of the time
where the time goes in v8:
time: 164 us; the launch traced here: 163 us
  Pallas kernels  163 us (99%)
    pallas_call x1, Pallas kernels, fused_local(): pl.pallas_call(partial(layer_kernel, lay), out_shape=out_shape, in_specs=...  157 us
    pallas_call x1, Pallas kernels, fused_local(): pl.pallas_call(widen_kernel, out_shape=(shape((micro, length, width // 2)...  5.46 us

profile of v8, /device:TPU:0, one launch (start us, length us, event | category | flops | bytes accessed | tf_op | source)
XLA Modules:
  0.0 163.4 jit_solution(66636881513110906)
XLA Ops:
  0.6 157.1 %two_sections.1 = (f32[2,128,384]{2,1,0:T(8,128)S(1)}, f32[2,128,384]{2,1,0:T(8,128)S(1)}, f32[2,768]{1,0:T(2,128)S(1)}, bf16[8,192,768]{2,1,0:T(8,128)(2,1)S(1)...) custom-call(bf16[2,128,768]{2,1,0:T(8,128)(2,1)} %bitcast.42, ...), custom_call_target="tpu_custom_call" | custom-call | tf_op jit(solution)/shard_map/two_sections/pallas_call | solution.py:1519
  157.8 5.5 %widen.1 = (f32[2,128,384]{2,1,0:T(8,128)}, f32[2,128,384]{2,1,0:T(8,128)}, f32[2,768]{1,0:T(2,128)}, f32[6,1,32]{2,1,0:T(1,128)}, f32[8,768]{1,0:T(8,128)}, /*i...) custom-call(f32[2,128,384]{2,1,0:T(8,128)S(1)} %get-tuple-element.26.sec_ref, ...), custom_call_target="tpu_custom_call" | custom-call | tf_op jit(solution)/shard_map/widen/pallas_call | solution.py:1544

commit v9 on v8

--- a/solution.py
+++ b/solution.py
@@ -837,20 +837,14 @@
 
     begin = u + s * (t - u)
 
-    def attend_one(i, carry):
-        @pl.when((s == 1) & (i == 1))
-        def _():
-            x_forward.wait()
-
-        attend(begin + i * (1 - 2 * begin))
-
-        @pl.when((s == 0) & (i == 0))
-        def _():
-            project_other()
-
-        return carry
-
-    lax.fori_loop(0, micro, attend_one, 0)
+    attend(begin)
+    pl.when(s == 0)(project_other)
+
+    @pl.when(s == 1)
+    def _():
+        x_forward.wait()
+
+    attend(1 - begin)
 
     @pl.when(s == 1)
     def _():

time: 164 us -> 164 us (level)
  no operation moved by 1% of the time
where the time goes in v9:
time: 164 us; the launch traced here: 163 us
  Pallas kernels  163 us (99%)
    pallas_call x1, Pallas kernels, fused_local(): pl.pallas_call(partial(layer_kernel, lay), out_shape=out_shape, in_specs=...  157 us
    pallas_call x1, Pallas kernels, fused_local(): pl.pallas_call(widen_kernel, out_shape=(shape((micro, length, width // 2)...  5.46 us

profile of v9, /device:TPU:0, one launch (start us, length us, event | category | flops | bytes accessed | tf_op | source)
XLA Modules:
  0.0 163.4 jit_solution(9907006147994248334)
XLA Ops:
  0.6 157.1 %two_sections.1 = (f32[2,128,384]{2,1,0:T(8,128)S(1)}, f32[2,128,384]{2,1,0:T(8,128)S(1)}, f32[2,768]{1,0:T(2,128)S(1)}, bf16[8,192,768]{2,1,0:T(8,128)(2,1)S(1)...) custom-call(bf16[2,128,768]{2,1,0:T(8,128)(2,1)} %bitcast.42, ...), custom_call_target="tpu_custom_call" | custom-call | tf_op jit(solution)/shard_map/two_sections/pallas_call | solution.py:1513
  157.8 5.5 %widen.1 = (f32[2,128,384]{2,1,0:T(8,128)}, f32[2,128,384]{2,1,0:T(8,128)}, f32[2,768]{1,0:T(2,128)}, f32[6,1,32]{2,1,0:T(1,128)}, f32[8,768]{1,0:T(8,128)}, /*i...) custom-call(f32[2,128,384]{2,1,0:T(8,128)S(1)} %get-tuple-element.26.sec_ref, ...), custom_call_target="tpu_custom_call" | custom-call | tf_op jit(solution)/shard_map/widen/pallas_call | solution.py:1538
